TPU v7x, 32 devices: a whole 2x2x4 slice. The times are simulated.
32 devices in a mesh: dp: 16 (over z, x, core), tensor: 2 (over y).
Axes of the slice: x: 2, y: 2, z: 4, core: 2. Of those that a mesh axis runs over, the one named last changes fastest.
Arguments:
- layer_input: bfloat16 [16, 1024, 1024], P('dp', 'tensor'), may hold values from -6 to 6
- segments: int32 [16, 1024], P('dp'), may hold values from 0 to 3, never falling along the last dimension, each value on 1 to 512 neighbouring positions
- valid_mask: int32 [16, 1024], P('dp', 'tensor'), may hold values from 0 to 1, as said below
- teacher: bfloat16 [16, 1024, 1024], P('dp', 'tensor'), may hold values from -6 to 6
- out_grad: bfloat16 [16, 1024, 1024], P('dp', 'tensor'), may hold values from -6 to 6
- norm_gain: bfloat16 [1024], P('dp'), may hold values from 0.25 to 1.75
- w_query: bfloat16 [1024, 1024], P('dp', 'tensor'), may hold values from -0.1875 to 0.1875
- w_key: bfloat16 [1024, 1024], P('dp', 'tensor'), may hold values from -0.1875 to 0.1875
- w_value: bfloat16 [1024, 1024], P('dp', 'tensor'), may hold values from -0.1875 to 0.1875
- w_beta: bfloat16 [1024, 8], P('dp', 'tensor'), may hold values from -0.1875 to 0.1875
- conv_weight: bfloat16 [3, 4, 8, 128], P(None, None, 'tensor', 'dp'), may hold values from -3 to 3
- head_gain: bfloat16 [128], P('dp'), may hold values from 0.25 to 1.75
- w_out: bfloat16 [1024, 1024], P('tensor', 'dp'), may hold values from -0.1875 to 0.1875
- mlp_gain: bfloat16 [1024], P('dp'), may hold values from 0.25 to 1.75
- w_gate: bfloat16 [1024, 2816], P('dp', 'tensor'), may hold values from -0.1875 to 0.1875
- w_up: bfloat16 [1024, 2816], P('dp', 'tensor'), may hold values from -0.1875 to 0.1875
- w_down: bfloat16 [2816, 1024], P('tensor', 'dp'), may hold values from -0.109375 to 0.109375
Outputs:
- layer_output: bfloat16 [16, 1024, 1024], P('dp', 'tensor')
- teacher_loss: float32 [], replicated
- grad_input: float32 [16, 1024, 1024], P('dp', 'tensor')
- grad_norm_gain: float32 [1024], P('dp')
- grad_query: float32 [1024, 1024], P('dp', 'tensor')
- grad_key: float32 [1024, 1024], P('dp', 'tensor')
- grad_value: float32 [1024, 1024], P('dp', 'tensor')
- grad_beta: float32 [1024, 8], P('dp', 'tensor')
- grad_conv: float32 [3, 4, 8, 128], P(None, None, 'tensor', 'dp')
- grad_head_gain: float32 [128], P('dp')
- grad_out: float32 [1024, 1024], P('tensor', 'dp')
- grad_mlp_gain: float32 [1024], P('dp')
- grad_gate: float32 [1024, 2816], P('dp', 'tensor')
- grad_up: float32 [1024, 2816], P('dp', 'tensor')
- grad_down: float32 [2816, 1024], P('tensor', 'dp')
Inputs may be any that keep to these rules, and one draw needn't show every extreme that they name: `segments`: document numbers start at 0 and never fall along a sequence; each of 0 to 3 is used, no document holds more than 512 tokens, and one holds exactly 512. `valid_mask`: the first token of every sequence is valid.
All inputs are finite; a program needn't handle non-finite values.
Results may differ from a plain program's by a relative error of at most 0.014.
Values may be sent and summed in bfloat16 or wider, within the bound.
A program may use at most 320 MiB of HBM per device.

v0:
```python
import jax
import jax.numpy as jnp
from jax import lax
from jax.sharding import PartitionSpec as P

BLOCK = 64


highest = lax.Precision.HIGHEST


def shifted(values, offset, fill):
    widths = [(0, 0)] * values.ndim
    widths[1] = (offset, 0)
    return jnp.pad(values[:, : values.shape[1] - offset], widths, constant_values=fill)


def conv_keeps(segment, taps_count):
    return [
        (shifted(segment, offset, -1) == segment).astype(jnp.float32)[..., None]
        for offset in range(taps_count)
    ]


def conv_mix(linear, taps, keeps):
    total = linear * taps[0]
    for offset in range(1, len(keeps)):
        total = total + taps[offset] * shifted(linear, offset, 0.0) * keeps[offset]
    return total


def unit_rows(values, factor):
    return values * lax.rsqrt(jnp.sum(values * values, -1, keepdims=True) + 1e-06) * factor


def advance(state, inputs):
    feed, pull, keep = inputs
    updated = (
        keep[:, None, None, None] * state
        + feed
        - jnp.einsum("bhef,bhfg->bheg", pull, state, precision=highest)
    )
    return (updated, state)


def delta_rule(queries, keys_in, values_in, strength, segment, block):
    batch, length, heads, width = queries.shape
    number = length // block
    total = batch * number

    def by_blocks(values):
        return values.reshape((total, block) + values.shape[2:])

    q_b = by_blocks(queries)
    k_b = by_blocks(keys_in)
    v_b = by_blocks(values_in)
    s_b = by_blocks(strength)
    seg = by_blocks(segment)
    ends = segment.reshape(batch, number, block)[:, :, -1]
    previous = jnp.concatenate([jnp.full((batch, 1), -1, jnp.int32), ends[:, :-1]], 1).reshape(
        total
    )
    same = (seg[:, :, None] == seg[:, None, :]).astype(jnp.float32)
    first_mask = (seg == previous[:, None]).astype(jnp.float32)
    last_mask = (seg == seg[:, -1:]).astype(jnp.float32)
    rows = jnp.arange(block)[:, None]
    cols = jnp.arange(block)[None, :]
    strict = (rows > cols).astype(jnp.float32)
    inclusive = (rows >= cols).astype(jnp.float32)
    kk_prod = jnp.einsum("bihe,bjhe->bhij", k_b, k_b, precision=highest)
    strength_t = jnp.transpose(s_b, (0, 2, 1))
    system = jnp.eye(block, dtype=jnp.float32) + strength_t[..., None] * (
        kk_prod * (same * strict)[:, None]
    )
    keys_t = jnp.transpose(k_b, (0, 2, 1, 3))
    values_t = jnp.transpose(v_b, (0, 2, 1, 3))
    right = strength_t[..., None] * jnp.concatenate(
        [values_t, first_mask[:, None, :, None] * keys_t], -1
    )
    solved = lax.linalg.triangular_solve(
        system, right, left_side=True, lower=True, unit_diagonal=True
    )
    plain = solved[..., :width]
    along = solved[..., width:]
    scores = (
        jnp.einsum("bihe,bjhe->bhij", q_b, k_b, precision=highest) * (same * inclusive)[:, None]
    )
    last_keys = keys_t * last_mask[:, None, :, None]
    feed = jnp.einsum("bhie,bhif->bhef", last_keys, plain, precision=highest)
    pull = jnp.einsum("bhie,bhif->bhef", last_keys, along, precision=highest)
    keep = first_mask[:, -1]

    def by_turns(values):
        return jnp.moveaxis(values.reshape((batch, number) + values.shape[1:]), 1, 0)

    start = jnp.zeros((batch, heads, width, width), jnp.float32)
    ending, befores = lax.scan(
        jax.checkpoint(advance), start, (by_turns(feed), by_turns(pull), by_turns(keep))
    )
    befores = jnp.moveaxis(befores, 0, 1).reshape(total, heads, width, width)
    queries_t = jnp.transpose(q_b, (0, 2, 1, 3))
    reach = first_mask[:, None, :, None] * queries_t - jnp.einsum(
        "bhij,bhje->bhie", scores, along, precision=highest
    )
    outputs = jnp.einsum("bhie,bhef->bhif", reach, befores, precision=highest) + jnp.einsum(
        "bhij,bhjf->bhif", scores, plain, precision=highest
    )
    return jnp.transpose(outputs, (0, 2, 1, 3)).reshape(batch, length, heads, width)


def mixer(linears, taps, head_gain, keeps, segment, heads, block):
    q_lin, k_lin, v_lin, b_lin = linears
    batch, length, channels = q_lin.shape
    width = channels // heads

    def prepare(linear, index):
        return jax.nn.silu(conv_mix(linear, taps[index], keeps)).reshape(
            batch, length, heads, width
        )

    queries = unit_rows(prepare(q_lin, 0), width ** (-0.5))
    keys_in = unit_rows(prepare(k_lin, 1), 1.0)
    values_in = prepare(v_lin, 2)
    strength = jax.nn.sigmoid(b_lin)
    mixed = delta_rule(queries, keys_in, values_in, strength, segment, block)
    normed = mixed * lax.rsqrt(jnp.mean(mixed * mixed, -1, keepdims=True) + 1e-05) * head_gain
    return normed.reshape(batch, length, channels)


def product(left, right):
    return jnp.dot(left, right, preferred_element_type=jnp.float32)


def back_product(left, right):
    return lax.dot_general(
        left, right, (((1,), (1,)), ((), ())), preferred_element_type=jnp.float32
    )


def transposed(left, right):
    return lax.dot_general(
        left, right, (((0,), (0,)), ((), ())), preferred_element_type=jnp.float32
    )


def norm_back(d_rows, unit, rho, gain_f):
    d_unit = d_rows * gain_f
    d_input = rho * (d_unit - unit * jnp.mean(d_unit * unit, -1, keepdims=True))
    return (d_input, jnp.sum(d_rows * unit, (0, 1)))


def local(
    layer_input,
    segments,
    valid_mask,
    teacher,
    out_grad,
    norm_gain,
    w_query,
    w_key,
    w_value,
    w_beta,
    conv_weight,
    head_gain,
    w_out,
    mlp_gain,
    w_gate,
    w_up,
    w_down,
):

    def fetch_mixer():
        return (
            lax.all_gather(norm_gain, "dp", axis=0, tiled=True),
            lax.all_gather(w_query, "dp", axis=0, tiled=True),
            lax.all_gather(w_key, "dp", axis=0, tiled=True),
            lax.all_gather(w_value, "dp", axis=0, tiled=True),
            lax.all_gather(w_beta, "dp", axis=0, tiled=True),
            lax.all_gather(conv_weight, "dp", axis=3, tiled=True),
            lax.all_gather(head_gain, "dp", axis=0, tiled=True),
            lax.all_gather(w_out, "dp", axis=1, tiled=True),
        )

    def fetch_mlp():
        return (
            lax.all_gather(mlp_gain, "dp", axis=0, tiled=True),
            lax.all_gather(w_gate, "dp", axis=0, tiled=True),
            lax.all_gather(w_up, "dp", axis=0, tiled=True),
            lax.all_gather(w_down, "dp", axis=1, tiled=True),
        )

    def widen(rows_half):
        return lax.all_gather(rows_half, "tensor", axis=1, tiled=True)

    def narrow(terms):
        return lax.psum_scatter(
            terms.astype(jnp.bfloat16), "tensor", scatter_dimension=1, tiled=True
        ).astype(jnp.float32)

    gain_one, w_q, w_k, w_v, w_b, conv_full, gain_head, w_o = fetch_mixer()
    batch = layer_input.shape[0]
    width_d = layer_input.shape[2]
    tokens_all = batch * layer_input.shape[1] * lax.axis_size("dp") * lax.axis_size("tensor")
    inputs = layer_input.astype(jnp.float32)
    rho_one = lax.rsqrt(jnp.mean(inputs * inputs, -1, keepdims=True) + 1e-05)
    unit_one = inputs * rho_one
    gain_one_f = gain_one.astype(jnp.float32)
    normed_one = widen((unit_one * gain_one_f).astype(jnp.bfloat16))
    length = normed_one.shape[1]
    flat_one = normed_one.reshape(-1, width_d)
    linears = tuple(
        (product(flat_one, weight).reshape(batch, length, -1) for weight in (w_q, w_k, w_v, w_b))
    )
    heads = w_b.shape[1]
    taps_count = conv_full.shape[1]
    taps = conv_full.astype(jnp.float32).reshape(3, taps_count, -1)
    keeps = conv_keeps(segments, taps_count)

    def local_mix(linear_set, tap_set, gain_set):
        return mixer(linear_set, tap_set, gain_set, keeps, segments, heads, BLOCK)

    normed, mix_back = jax.vjp(local_mix, linears, taps, gain_head.astype(jnp.float32))
    mixed_low = normed.astype(jnp.bfloat16).reshape(-1, normed.shape[-1])
    attention = narrow(product(mixed_low, w_o).reshape(batch, length, width_d))
    hidden = inputs + attention
    gain_two, w_g, w_u, w_d = fetch_mlp()
    rho_two = lax.rsqrt(jnp.mean(hidden * hidden, -1, keepdims=True) + 1e-05)
    unit_two = hidden * rho_two
    gain_two_f = gain_two.astype(jnp.float32)
    normed_two = widen((unit_two * gain_two_f).astype(jnp.bfloat16))
    flat_two = normed_two.reshape(-1, width_d)
    gate = product(flat_two, w_g)
    upper = product(flat_two, w_u)
    sigmoid_gate = jax.nn.sigmoid(gate)
    active = gate * sigmoid_gate
    inner = (active * upper).astype(jnp.bfloat16)
    mlp_rows = narrow(product(inner, w_d).reshape(batch, length, width_d))
    outputs = hidden + mlp_rows
    mask = valid_mask.astype(jnp.float32)[..., None]
    differ = outputs - teacher.astype(jnp.float32)
    square_sum, valid_sum = lax.psum(
        (jnp.sum(mask * differ * differ), jnp.sum(mask)), ("dp", "tensor")
    )
    loss_value = square_sum / (width_d * valid_sum)
    d_out = out_grad.astype(jnp.float32) + mask * differ * (tokens_all / 4.0) / valid_sum
    gain_two, w_g, w_u, w_d = fetch_mlp()
    d_mlp = widen(d_out.astype(jnp.bfloat16)).reshape(-1, width_d)
    d_inner = back_product(d_mlp, w_d)
    grad_down = transposed(inner, d_mlp)
    d_gate = (d_inner * upper * sigmoid_gate * (1.0 + gate * (1.0 - sigmoid_gate))).astype(
        jnp.bfloat16
    )
    d_upper = (d_inner * active).astype(jnp.bfloat16)
    d_two = back_product(d_gate, w_g) + back_product(d_upper, w_u)
    grad_gate = transposed(flat_two, d_gate)
    grad_up = transposed(flat_two, d_upper)
    grad_gate, grad_up, grad_down = (
        lax.psum_scatter(grad_gate, "dp", scatter_dimension=0, tiled=True),
        lax.psum_scatter(grad_up, "dp", scatter_dimension=0, tiled=True),
        lax.psum_scatter(grad_down, "dp", scatter_dimension=1, tiled=True),
    )
    d_two_rows = narrow(d_two.reshape(batch, length, width_d))
    d_norm_two, grad_gain_two = norm_back(d_two_rows, unit_two, rho_two, gain_two_f)
    d_hidden = d_out + d_norm_two
    gain_one, w_q, w_k, w_v, w_b, conv_full, gain_head, w_o = fetch_mixer()
    d_attention = widen(d_hidden.astype(jnp.bfloat16)).reshape(-1, width_d)
    d_mixed = back_product(d_attention, w_o)
    grad_out_w = transposed(mixed_low, d_attention)
    d_linears, grad_taps, grad_head = mix_back(d_mixed.reshape(normed.shape))
    rounded = tuple(
        (piece.astype(jnp.bfloat16).reshape(-1, piece.shape[-1]) for piece in d_linears)
    )
    d_one = (
        back_product(rounded[0], w_q)
        + back_product(rounded[1], w_k)
        + back_product(rounded[2], w_v)
        + back_product(rounded[3], w_b)
    )
    grad_q = transposed(flat_one, rounded[0])
    grad_k = transposed(flat_one, rounded[1])
    grad_v = transposed(flat_one, rounded[2])
    grad_b = transposed(flat_one, rounded[3])
    d_one_rows = narrow(d_one.reshape(batch, length, width_d))
    d_norm_one, grad_gain_one = norm_back(d_one_rows, unit_one, rho_one, gain_one_f)
    d_input = d_hidden + d_norm_one
    grad_gain_one, grad_head, grad_gain_two = lax.psum(
        (grad_gain_one, grad_head, grad_gain_two), "tensor"
    )
    grad_conv_full = grad_taps.reshape(conv_full.shape)
    (
        grad_gain_one,
        grad_q,
        grad_k,
        grad_v,
        grad_b,
        grad_conv_full,
        grad_head,
        grad_out_w,
        grad_gain_two,
    ) = (
        lax.psum_scatter(grad_gain_one, "dp", scatter_dimension=0, tiled=True),
        lax.psum_scatter(grad_q, "dp", scatter_dimension=0, tiled=True),
        lax.psum_scatter(grad_k, "dp", scatter_dimension=0, tiled=True),
        lax.psum_scatter(grad_v, "dp", scatter_dimension=0, tiled=True),
        lax.psum_scatter(grad_b, "dp", scatter_dimension=0, tiled=True),
        lax.psum_scatter(grad_conv_full, "dp", scatter_dimension=3, tiled=True),
        lax.psum_scatter(grad_head, "dp", scatter_dimension=0, tiled=True),
        lax.psum_scatter(grad_out_w, "dp", scatter_dimension=1, tiled=True),
        lax.psum_scatter(grad_gain_two, "dp", scatter_dimension=0, tiled=True),
    )
    return (
        outputs.astype(jnp.bfloat16),
        loss_value,
        d_input,
        grad_gain_one,
        grad_q,
        grad_k,
        grad_v,
        grad_b,
        grad_conv_full,
        grad_head,
        grad_out_w,
        grad_gain_two,
        grad_gate,
        grad_up,
        grad_down,
    )


def solution(mesh):
    in_specs = (
        P("dp", "tensor", None),
        P("dp", None),
        P("dp", "tensor"),
        P("dp", "tensor", None),
        P("dp", "tensor", None),
        P("dp"),
        P("dp", "tensor"),
        P("dp", "tensor"),
        P("dp", "tensor"),
        P("dp", "tensor"),
        P(None, None, "tensor", "dp"),
        P("dp"),
        P("tensor", "dp"),
        P("dp"),
        P("dp", "tensor"),
        P("dp", "tensor"),
        P("tensor", "dp"),
    )
    out_specs = (
        P("dp", "tensor", None),
        P(),
        P("dp", "tensor", None),
        P("dp"),
        P("dp", "tensor"),
        P("dp", "tensor"),
        P("dp", "tensor"),
        P("dp", "tensor"),
        P(None, None, "tensor", "dp"),
        P("dp"),
        P("tensor", "dp"),
        P("dp"),
        P("dp", "tensor"),
        P("dp", "tensor"),
        P("tensor", "dp"),
    )
    return jax.shard_map(local, mesh=mesh, in_specs=in_specs, out_specs=out_specs, check_vma=False)
```

profile of v0, /device:TPU:0, one launch (start us, length us, event | category | flops | bytes accessed | tf_op | source)
XLA Modules:
  0.0 1888.0 jit_solution(1381325187297772062)
XLA Ops:
  13.1 36.2 %all-reduce.47 = (bf16[128]{0:T(256)(128)(2,1)S(1)}, bf16[1024]{0:T(1024)(128)(2,1)S(1)}, bf16[1024]{0:T(1024)(128)(2,1)}) all-reduce(bf16[128]{0:T(256)(128)(2,1)S(1)} %dynamic-update-slice.1, bf16[1024]{0:T(1024)(128)(2,1)S(1)} %dynamic-update-slice, bf16[1024]{0:T(1024)(128)(2,1)S(1)} %dynamic-update-slice.2), channel_id=1, replica_groups=mesh['dp'=16,'tensor'=2] {'dp'}, use_global_device_ids=true, to_apply=%add.39 | all-reduce | flops 2176 | bytes 8704
  56.8 18.2 all_gather.59
  82.8 19.3 %all-gather = bf16[16,64,4]{1,2,0:T(4,128)(2,1)S(1)} all-gather(bf16[1,64,4]{1,2,0:T(4,128)(2,1)S(1)} %bitcast.522), channel_id=1, replica_groups=mesh['dp'=16,'tensor'=2] {'dp'}, dimensions={0}, use_global_device_ids=true | all-gather | bytes 8704 | tf_op jit(solution)/shard_map/all_gather | solution.py:178
  110.3 15.0 all-gather.17.cloned.1.call-done
  156.7 316.0 %custom-call.7 = f32[16,4,1,64,64]{3,4,2,1,0:T(8,128)} custom-call(f32[16,4,1,64,64]{4,3,2,1,0:T(8,128)} %add_bitcast_fusion.2), custom_call_target="InvertDiagBlocksLowerTriangular" | custom-call | tf_op jit(solution)/shard_map/jvp()/triangular_solve | solution.py:80
  516.6 54.8 %while.32 = (s32[]{:T(128)}, f32[1,4,128,128]{3,2,1,0:T(8,128)S(1)}, f32[16,1,4,128,128]{4,3,2,1,0:T(8,128)}, f32[16,1]{0,1:T(1,128)S(1)}, f32[16,1,4,128,128]{4...) while((s32[]{:T(128)}, f32[1,4,128,128]{3,2,1,0:T(8,128)S(1)}, ...), condition=%wide.region_4.5_spmd.clone, body=%wide.region_3.4_spmd.clone.sunk | while | flops 101056512 | bytes 2362475 | solution.py:97
  608.6 30.1 %reduce-scatter.16.cloned.1.call-done = bf16[1,512,1024]{2,1,0:T(8,128)(2,1)} async-done(((bf16[1,1024,1024]{2,1,0:T(8,128)(2,1)}), bf16[1,512,1024]{2,1,0:T(8,128)(2,1)}) %reduce-scatter.16.cloned.1.call-update) | async-done | bytes 1048592 | tf_op jit(solution)/shard_map/reduce_scatter | solution.py:196
  643.2 42.4 %all-gather.25.cloned.1.call-done = bf16[1024,1408]{1,0:T(8,128)(2,1)} async-done(((bf16[64,1408]{1,0:T(8,128)(2,1)}), bf16[1024,1408]{1,0:T(8,128)(2,1)}) %all-gather.25.cloned.1.call-update) | async-done | bytes 2883600 | tf_op jit(solution)/shard_map/all_gather | solution.py:187
  685.6 33.7 %all-gather.23.cloned.1.call-done = bf16[1,1024,1024]{2,1,0:T(8,128)(2,1)} async-done(((bf16[1,512,1024]{2,1,0:T(8,128)(2,1)}), bf16[1,1024,1024]{2,1,0:T(8,128)(2,1)}) %all-gather.23.cloned.1.call-update) | async-done | bytes 2097168 | tf_op jit(solution)/shard_map/all_gather | solution.py:193
  727.6 38.6 %all-gather.27.cloned.1.call-done = bf16[1024,1408]{1,0:T(8,128)(2,1)} async-done(((bf16[64,1408]{1,0:T(8,128)(2,1)}), bf16[1024,1408]{1,0:T(8,128)(2,1)}) %all-gather.27.cloned.1.call-update) | async-done | bytes 2883600 | tf_op jit(solution)/shard_map/all_gather | solution.py:188
  777.5 33.9 %all-gather.29.cloned.1.call-done = bf16[1408,1024]{0,1:T(8,128)(2,1)} async-done(((bf16[1408,64]{0,1:T(8,128)(2,1)}), bf16[1408,1024]{0,1:T(8,128)(2,1)}) %all-gather.29.cloned.1.call-update) | async-done | bytes 2883600 | tf_op jit(solution)/shard_map/all_gather | solution.py:189
  820.1 39.6 %psum.36 = f32[]{:T(128)} all-reduce(f32[]{:T(128)} %convert_reduce_fusion), channel_id=1, replica_groups=mesh['dp'=16,'tensor'=2] {'dp','tensor'}, use_global_device_ids=true, to_apply=%region_12.13 | all-reduce | flops 1 | bytes 8 | tf_op jit(solution)/shard_map/psum | solution.py:241
  865.2 33.0 %all-gather.31.cloned.1.call-done = bf16[1,1024,1024]{2,1,0:T(8,128)(2,1)} async-done(((bf16[1,512,1024]{2,1,0:T(8,128)(2,1)}), bf16[1,1024,1024]{2,1,0:T(8,128)(2,1)}) %all-gather.31.cloned.1.call-update) | async-done | bytes 2097168 | tf_op jit(solution)/shard_map/all_gather | solution.py:193
  917.6 32.0 %reduce-scatter.20.cloned.1.call-done = bf16[1,512,1024]{2,1,0:T(8,128)(2,1)} async-done(((bf16[1,1024,1024]{2,1,0:T(8,128)(2,1)}), bf16[1,512,1024]{2,1,0:T(8,128)(2,1)}) %reduce-scatter.20.cloned.1.call-update) | async-done | bytes 1048592 | tf_op jit(solution)/shard_map/reduce_scatter | solution.py:196
  963.1 27.2 %all-gather.33.cloned.1.call-done = bf16[1,1024,1024]{2,1,0:T(8,128)(2,1)} async-done(((bf16[1,512,1024]{2,1,0:T(8,128)(2,1)}), bf16[1,1024,1024]{2,1,0:T(8,128)(2,1)}) %all-gather.33.cloned.1.call-update) | async-done | bytes 2097168 | tf_op jit(solution)/shard_map/all_gather | solution.py:193
  1043.4 94.4 %while.33 = (s32[]{:T(128)}, f32[1,4,128,128]{2,3,1,0:T(8,128)S(1)}, f32[16,1,4,128,128]{3,4,2,1,0:T(8,128)}, f32[16,1,4,128,128]{4,3,2,1,0:T(8,128)}, f32[16,1,...) while((s32[]{:T(128)}, ...), condition=%wide.region_18.19_spmd.clone, body=%wide.region_17.18_spmd.clone.sunk | while | flops 201719808 | bytes 4980899 | solution.py:97
  1333.5 39.9 %psum.35 = f32[]{:T(128)} all-reduce(f32[]{:T(128)} %get-tuple-element.357), channel_id=1, replica_groups=mesh['dp'=16,'tensor'=2] {'dp','tensor'}, use_global_device_ids=true, to_apply=%region_10.11 | all-reduce | flops 1 | bytes 8 | tf_op jit(solution)/shard_map/psum | solution.py:241
  1377.7 62.1 %all-reduce.45 = (f32[1024]{0:T(1024)S(1)}, f32[3,4,4,128]{3,2,1,0:T(4,128)S(1)}, f32[128]{0:T(128)S(1)}, f32[1024]{0:T(1024)S(1)}) all-reduce(f32[1024]{0:T(1024)S(1)} %get-tuple-element.355, f32[3,4,4,128]{3,2,1,0:T(4,128)S(1)} %reshape.852, f32[128]{0:T(128)S(1)} %bitcast_reduce_fusion, ...), channel_id=6, replica_groups=mesh['dp'=16,'tensor'=2] {'dp'}, use_global_device_ids=true, to_apply=%region_26.27.clone | all-reduce | flops 8320 | bytes 66560
  1451.5 82.4 %reduce-scatter.32.cloned.1.call-done = f32[64,1408]{1,0:T(8,128)} async-done(((f32[1024,1408]{1,0:T(8,128)}), f32[64,1408]{1,0:T(8,128)}) %reduce-scatter.32.cloned.1.call-update) | async-done | bytes 360464 | tf_op jit(solution)/shard_map/reduce_scatter | solution.py:258
  1533.9 85.8 %reduce-scatter.34.cloned.1.call-done = f32[64,1408]{1,0:T(8,128)} async-done(((f32[1024,1408]{1,0:T(8,128)}), f32[64,1408]{1,0:T(8,128)}) %reduce-scatter.34.cloned.1.call-update) | async-done | bytes 360464 | tf_op jit(solution)/shard_map/reduce_scatter | solution.py:259
  1619.7 65.4 %reduce-scatter.26.cloned.1.call-done = f32[64,512]{1,0:T(8,128)} async-done(((f32[1024,512]{1,0:T(8,128)}), f32[64,512]{1,0:T(8,128)}) %reduce-scatter.26.cloned.1.call-update) | async-done | bytes 131088 | tf_op jit(solution)/shard_map/reduce_scatter | solution.py:303
  1685.0 64.9 %reduce-scatter.30.cloned.1.call-done = f32[512,64]{0,1:T(8,128)} async-done(((f32[512,1024]{0,1:T(8,128)}), f32[512,64]{0,1:T(8,128)}) %reduce-scatter.30.cloned.1.call-update) | async-done | bytes 131088 | tf_op jit(solution)/shard_map/reduce_scatter | solution.py:308
  1749.9 65.3 %reduce-scatter.24.cloned.1.call-done = f32[64,512]{1,0:T(8,128)} async-done(((f32[1024,512]{1,0:T(8,128)}), f32[64,512]{1,0:T(8,128)}) %reduce-scatter.24.cloned.1.call-update) | async-done | bytes 131088 | tf_op jit(solution)/shard_map/reduce_scatter | solution.py:302
  1815.2 64.9 %reduce-scatter.28.cloned.1.call-done = f32[64,512]{1,0:T(8,128)} async-done(((f32[1024,512]{1,0:T(8,128)}), f32[64,512]{1,0:T(8,128)}) %reduce-scatter.28.cloned.1.call-update) | async-done | bytes 131088 | tf_op jit(solution)/shard_map/reduce_scatter | solution.py:304
  (751 shorter events, 619.5 us)
Async XLA Ops:
  7.2 99.7 %all-gather.19.cloned.1.call-start = ((), (), s32[]{:S(2)}) async-start(), calls=%async_computation.15 | async-start | bytes 1114112 | tf_op jit(solution)/shard_map/all_gather | solution.py:177
  7.9 99.0 %all-gather.13.cloned.1.call-start = ((), (), s32[]{:S(2)}) async-start(), calls=%async_computation.12 | async-start | bytes 3145728 | tf_op jit(solution)/shard_map/all_gather | solution.py:193
  54.0 71.4 %all-gather.17.cloned.1.call-start = ((), (), s32[]{:S(2)}) async-start(), calls=%async_computation.14 | async-start | bytes 1114112 | tf_op jit(solution)/shard_map/all_gather | solution.py:176
  54.7 452.6 %all-gather.15.cloned.1.call-start = ((), (), s32[]{:S(2)}) async-start(), calls=%async_computation.13 | async-start | bytes 1114112 | tf_op jit(solution)/shard_map/all_gather | solution.py:175
  55.3 545.8 %all-gather.21.cloned.1.call-start = ((), (), s32[]{:S(2)}) async-start(), calls=%async_computation.16 | async-start | bytes 1114112 | tf_op jit(solution)/shard_map/all_gather | solution.py:181
  55.9 582.8 %reduce-scatter.16.cloned.1.call-start = ((), (), s32[]{:S(2)}) async-start(), calls=%async_computation.17 | async-start | bytes 3145728 | tf_op jit(solution)/shard_map/reduce_scatter | solution.py:196
  106.7 486.1 %copy-start.35 = (f32[16,64,64]{2,1,0:T(8,128)}, f32[16,64,64]{2,1,0:T(8,128)S(1)}, u32[]{:S(2)}) copy-start(f32[16,64,64]{2,1,0:T(8,128)S(1)} %get-tuple-element.471) | copy-start | bytes 786436
  607.8 77.8 %all-gather.25.cloned.1.call-start = ((), (), s32[]{:S(2)}) async-start(), calls=%async_computation.19 | async-start | bytes 3063808 | tf_op jit(solution)/shard_map/all_gather | solution.py:187
  608.5 110.8 %all-gather.23.cloned.1.call-start = ((), (), s32[]{:S(2)}) async-start(), calls=%async_computation.18 | async-start | bytes 3145728 | tf_op jit(solution)/shard_map/all_gather | solution.py:193
  641.8 124.4 %all-gather.27.cloned.1.call-start = ((), (), s32[]{:S(2)}) async-start(), calls=%async_computation.20 | async-start | bytes 3063808 | tf_op jit(solution)/shard_map/all_gather | solution.py:188
  642.6 168.8 %all-gather.29.cloned.1.call-start = ((), (), s32[]{:S(2)}) async-start(), calls=%async_computation.21 | async-start | bytes 3063808 | tf_op jit(solution)/shard_map/all_gather | solution.py:189
  643.2 216.5 %reduce-scatter.18.cloned.1.call-start = ((), (), s32[]{:S(2)}) async-start(), calls=%async_computation.22 | async-start | bytes 3145728 | tf_op jit(solution)/shard_map/reduce_scatter | solution.py:196
  818.8 79.4 %all-gather.31.cloned.1.call-start = ((), (), s32[]{:S(2)}) async-start(), calls=%async_computation.23 | async-start | bytes 3145728 | tf_op jit(solution)/shard_map/all_gather | solution.py:193
  864.8 84.8 %reduce-scatter.20.cloned.1.call-start = ((), (), s32[]{:S(2)}) async-start(), calls=%async_computation.24 | async-start | bytes 3145728 | tf_op jit(solution)/shard_map/reduce_scatter | solution.py:196
  917.6 72.7 %all-gather.33.cloned.1.call-start = ((), (), s32[]{:S(2)}) async-start(), calls=%async_computation.25 | async-start | bytes 3145728 | tf_op jit(solution)/shard_map/all_gather | solution.py:193
  957.0 417.2 %reduce-scatter.38.cloned.1.call-start = ((), (), s32[]{:S(2)}) async-start(), calls=%async_computation.34 | async-start | bytes 557056
  1271.0 104.6 %reduce-scatter.22.cloned.1.call-start = ((), (), s32[]{:S(2)}) async-start(), calls=%async_computation.26 | async-start | bytes 3145728 | tf_op jit(solution)/shard_map/reduce_scatter | solution.py:196
  1290.0 161.5 %reduce-scatter.36.cloned.1.call-start = ((), (), s32[]{:S(2)}) async-start(), calls=%async_computation.33 | async-start | bytes 6127616 | tf_op jit(solution)/shard_map/reduce_scatter | solution.py:260
  1298.7 235.2 %reduce-scatter.32.cloned.1.call-start = ((), (), s32[]{:S(2)}) async-start(), calls=%async_computation.31 | async-start | bytes 6127616 | tf_op jit(solution)/shard_map/reduce_scatter | solution.py:258
  1307.4 312.2 %reduce-scatter.34.cloned.1.call-start = ((), (), s32[]{:S(2)}) async-start(), calls=%async_computation.32 | async-start | bytes 6127616 | tf_op jit(solution)/shard_map/reduce_scatter | solution.py:259
  1314.6 370.4 %reduce-scatter.26.cloned.1.call-start = ((), (), s32[]{:S(2)}) async-start(), calls=%async_computation.28 | async-start | bytes 2228224 | tf_op jit(solution)/shard_map/reduce_scatter | solution.py:303
  1318.8 431.1 %reduce-scatter.30.cloned.1.call-start = ((), (), s32[]{:S(2)}) async-start(), calls=%async_computation.30 | async-start | bytes 2228224 | tf_op jit(solution)/shard_map/reduce_scatter | solution.py:308
  1323.6 491.7 %reduce-scatter.24.cloned.1.call-start = ((), (), s32[]{:S(2)}) async-start(), calls=%async_computation.27 | async-start | bytes 2228224 | tf_op jit(solution)/shard_map/reduce_scatter | solution.py:302
  1327.4 552.7 %reduce-scatter.28.cloned.1.call-start = ((), (), s32[]{:S(2)}) async-start(), calls=%async_computation.29 | async-start | bytes 2228224 | tf_op jit(solution)/shard_map/reduce_scatter | solution.py:304
  (157 other events, 4268.7 us)
Sparse Core Ops, SparseCore 0:
  10.2 40.7 all-gather.18
  54.1 31.0 all-gather.12
  87.3 37.9 all-gather.16
  127.4 36.9 all-gather.14
  166.4 37.8 all-gather.20
  607.9 30.7 reduce-scatter.15
  641.2 44.3 all-gather.24
  687.8 31.4 all-gather.22
  721.8 44.3 all-gather.26
  768.6 42.6 all-gather.28
  818.9 30.9 reduce-scatter.17
  864.9 33.3 all-gather.30
  917.7 31.8 reduce-scatter.19
  957.1 33.0 all-gather.32
  1271.1 55.7 reduce-scatter.37
  1329.6 31.5 reduce-scatter.21
  1366.0 82.2 reduce-scatter.35
  1453.1 80.7 reduce-scatter.31
  1538.9 80.7 reduce-scatter.33
  1624.3 60.6 reduce-scatter.25
  1689.3 60.5 reduce-scatter.29
  1754.7 60.5 reduce-scatter.23
  1819.6 60.5 reduce-scatter.27
where the time goes:
time: 1900 us; the launch traced here: 1890 us
  waiting for transfers between devices  719 us (38%)
  other arithmetic  425 us (22%)
  matrix products  317 us (17%)
  blocking collectives  221 us (12%)
  local copies, waits for them, and re-layouts  181 us (10%)
  between operations  21.4 us (1%)
    another operation x5, other arithmetic, delta_rule(): lax.linalg.triangular_solve(system, right, left_side=True, lower=True, un...  320 us
    unnamed x2, blocking collectives  98.3 us
    all_gather x4, waiting for transfers between devices, widen(): return lax.all_gather(rows_half, 'tensor', axis=1, tiled=True)  93.9 us
    reduce_scatter x1, waiting for transfers between devices, local(): lax.psum_scatter(grad_up, 'dp', scatter_dimension=0, tiled=True)  85.8 us
    reduce_scatter x1, waiting for transfers between devices, local(): lax.psum_scatter(grad_gate, 'dp', scatter_dimension=0, tiled=True)  82.4 us
    psum x2, blocking collectives, local(): lax.psum((jnp.sum(mask * differ * differ), jnp.sum(mask)), ('dp', 'tensor'))  79.5 us
    dot_general x48, matrix products, advance(): jnp.einsum('bhef,bhfg->bheg', pull, state, precision=highest)  70.7 us
    reduce_scatter x1, waiting for transfers between devices, local(): lax.psum_scatter(grad_k, 'dp', scatter_dimension=0, tiled=True)  65.4 us
  transfers between devices with their start and end apart: 23, of which 15 were waited for; matrix products, arithmetic and copies ran while one was open for 31% of the time, Pallas kernels for 0%

commit v1 on v0

v1 whole, which is shorter than its diff:
```python
import functools

import jax
import jax.numpy as jnp
from jax import lax
from jax.experimental import pallas as pl
from jax.experimental.pallas import tpu as pltpu
from jax.sharding import PartitionSpec as P

F32, BF16 = jnp.float32, jnp.bfloat16
MESH = pl.DeviceIdType.MESH
CHUNK = 128
HALO = 16
WIDTH = 128
PAIR = 2
TAPS = 4
VMEM_LIMIT = 60 * 1024 * 1024


def contract(left, right, dim_left, dim_right):
    return lax.dot_general(
        left.astype(BF16),
        right.astype(BF16),
        (((dim_left,), (dim_right,)), ((), ())),
        preferred_element_type=F32,
    )


def mm(left, right):
    return contract(left, right, 1, 0)


def mm_t(left, right):
    return contract(left, right, 1, 1)


def t_mm(left, right):
    return contract(left, right, 0, 0)


def tri_inverse(system, rows, cols):
    eye = (rows == cols).astype(F32)
    inverse = eye
    size = 1
    while size < CHUNK:
        link = (
            (rows // (2 * size) == cols // (2 * size))
            & ((rows // size) % 2 == 1)
            & ((cols // size) % 2 == 0)
        )
        part = jnp.where(link, system, 0.0)
        if size == 1:
            inverse = eye - part
        else:
            inverse = inverse - mm(inverse, mm(part, inverse))
        size *= 2
    return inverse


def conv_of(lin_ref, base, lanes, taps, row, keeps, tokens):
    total = lin_ref[0, base : base + tokens, lanes] * taps[row : row + 1]
    for off in range(1, TAPS):
        total = total + taps[row + off : row + off + 1] * (
            lin_ref[0, base - off : base - off + tokens, lanes] * keeps[off]
        )
    return total


def head_column(aux, lane):
    lanes = lax.broadcasted_iota(jnp.int32, aux.shape, 1)
    return jnp.sum(jnp.where(lanes == lane, aux, 0.0), axis=1, keepdims=True)


def greet(partner):
    barrier = pltpu.get_barrier_semaphore()
    pl.semaphore_signal(
        barrier, inc=1, device_id={"tensor": partner}, device_id_type=MESH
    )
    pl.semaphore_wait(barrier, 1)


def chunk_masks(aux, seg_row, at):
    rows = lax.broadcasted_iota(jnp.int32, (CHUNK, CHUNK), 0)
    cols = lax.broadcasted_iota(jnp.int32, (CHUNK, CHUNK), 1)
    same = aux[at : at + CHUNK, 0:1] == seg_row[0:1, at : at + CHUNK]
    return same & (rows > cols), same & (rows >= cols), rows, cols


def mixer_fwd_kernel(
    tokens, q_ref, k_ref, v_ref, aux_ref, seg_ref, taps_ref, gain_ref,
    onb_ref, o_ref, n_ref, t_ref, s_ref,
    state, outbox, inbox, send_sem, recv_sem,
):
    step = pl.program_id(0)
    mine = lax.axis_index("tensor")
    chunks = tokens // CHUNK

    @pl.when(step == 0)
    def _():
        greet(1 - mine)

    def hand_over(head):
        return pltpu.make_async_remote_copy(
            src_ref=outbox.at[head],
            dst_ref=inbox.at[head],
            send_sem=send_sem.at[head],
            recv_sem=recv_sem.at[head],
            device_id={"tensor": 1 - mine},
            device_id_type=MESH,
        )

    aux = aux_ref[...]
    seg_row = seg_ref[...]
    keeps = [None] + [aux[:, 2 + off : 3 + off] for off in range(1, TAPS)]
    heads = []
    for sub in range(PAIR):
        lanes = slice(sub * WIDTH, (sub + 1) * WIDTH)
        taps = taps_ref[:, lanes]
        beta = head_column(aux, 16 + step * PAIR + sub)
        acts = []
        for index, ref in enumerate((q_ref, k_ref, v_ref)):
            mixed = conv_of(ref, HALO, lanes, taps, index * TAPS, keeps, tokens)
            acts.append(mixed * jax.nn.sigmoid(mixed))
        q = acts[0] * (
            lax.rsqrt(jnp.sum(acts[0] * acts[0], -1, keepdims=True) + 1e-06) * WIDTH ** (-0.5)
        )
        k = acts[1] * lax.rsqrt(jnp.sum(acts[1] * acts[1], -1, keepdims=True) + 1e-06)
        heads.append((q, k, acts[2], beta))
    inner = []
    for sub in range(PAIR):
        q, k, v, beta = heads[sub]
        for c in range(chunks):
            at = c * CHUNK
            strict, inclusive, rows, cols = chunk_masks(aux, seg_row, at)
            kc, qc = k[at : at + CHUNK], q[at : at + CHUNK]
            system = jnp.where(strict, beta[at : at + CHUNK] * mm_t(kc, kc), 0.0)
            inverse = tri_inverse(system, rows, cols).astype(BF16)
            t_ref[sub, c] = inverse
            inner.append((inverse, jnp.where(inclusive, mm_t(qc, kc), 0.0).astype(BF16)))

    @pl.when(mine == 0)
    def _():
        state[...] = jnp.zeros_like(state)

    @pl.when(mine == 1)
    def _():
        for sub in range(PAIR):
            head = step * PAIR + sub
            hand_over(head).wait_recv()
            state[sub] = inbox[head]

    carried = [state[sub] for sub in range(PAIR)]
    for c in range(chunks):
        at = c * CHUNK
        first = aux[at : at + CHUNK, 1:2]
        last = aux[at : at + CHUNK, 2:3]
        keep = aux[at + CHUNK - 1 : at + CHUNK, 1:2]
        for sub in range(PAIR):
            q, k, v, beta = heads[sub]
            inverse, scores = inner[sub * chunks + c]
            kc, qc = k[at : at + CHUNK], q[at : at + CHUNK]
            before = carried[sub].astype(BF16)
            s_ref[sub, c] = before
            rhs = beta[at : at + CHUNK] * (v[at : at + CHUNK] - first * mm(kc, before))
            new = mm(inverse, rhs).astype(BF16)
            n_ref[sub, c] = new
            out = first * mm(qc, before) + mm(scores, new)
            lanes = slice(sub * WIDTH, (sub + 1) * WIDTH)
            o_ref[0, at : at + CHUNK, lanes] = out
            scale = lax.rsqrt(jnp.mean(out * out, -1, keepdims=True) + 1e-05)
            onb_ref[0, at : at + CHUNK, lanes] = (out * scale * gain_ref[0:1]).astype(BF16)
            carried[sub] = keep * carried[sub] + t_mm(last * kc, new)

    @pl.when(mine == 0)
    def _():
        for sub in range(PAIR):
            head = step * PAIR + sub
            outbox[head] = carried[sub]
            hand_over(head).start()

    @pl.when((step == pl.num_programs(0) - 1) & (mine == 0))
    def _():
        for head in range(outbox.shape[0]):
            hand_over(head).wait_send()


def mixer_bwd_kernel(
    tokens, q_ref, k_ref, v_ref, aux_ref, seg_ref, taps_ref, gain_ref,
    o_ref, n_ref, t_ref, s_ref, donb_ref,
    dlin_ref, dbl_ref, dtaps_ref, dgain_ref,
    state, extended, outbox, inbox, tailbox, headbox, send_sem, recv_sem, tail_send, tail_recv,
):
    step = pl.program_id(0)
    mine = lax.axis_index("tensor")
    chunks = tokens // CHUNK

    @pl.when(step == 0)
    def _():
        greet(1 - mine)
        dbl_ref[...] = jnp.zeros_like(dbl_ref)
        dgain_ref[...] = jnp.zeros_like(dgain_ref)

    def hand_over(head):
        return pltpu.make_async_remote_copy(
            src_ref=outbox.at[head],
            dst_ref=inbox.at[head],
            send_sem=send_sem.at[head],
            recv_sem=recv_sem.at[head],
            device_id={"tensor": 1 - mine},
            device_id_type=MESH,
        )

    def hand_tail(head):
        return pltpu.make_async_remote_copy(
            src_ref=tailbox.at[head],
            dst_ref=headbox.at[head],
            send_sem=tail_send.at[head],
            recv_sem=tail_recv.at[head],
            device_id={"tensor": 1 - mine},
            device_id_type=MESH,
        )

    aux = aux_ref[...]
    seg_row = seg_ref[...]
    keeps = [None] + [aux[:tokens, 2 + off : 3 + off] for off in range(1, TAPS)]
    heads, inner = [], []
    for sub in range(PAIR):
        lanes = slice(sub * WIDTH, (sub + 1) * WIDTH)
        taps = taps_ref[:, lanes]
        beta = head_column(aux[:tokens], 16 + step * PAIR + sub)
        mixes, sigs, acts = [], [], []
        for index, ref in enumerate((q_ref, k_ref, v_ref)):
            mixed = conv_of(ref, HALO, lanes, taps, index * TAPS, keeps, tokens)
            mixes.append(mixed)
            sigs.append(jax.nn.sigmoid(mixed))
            acts.append(mixed * sigs[-1])
        rho_q = lax.rsqrt(jnp.sum(acts[0] * acts[0], -1, keepdims=True) + 1e-06)
        rho_k = lax.rsqrt(jnp.sum(acts[1] * acts[1], -1, keepdims=True) + 1e-06)
        q = acts[0] * (rho_q * WIDTH ** (-0.5))
        k = acts[1] * rho_k
        out = o_ref[0, :, lanes]
        don = donb_ref[0, :, lanes]
        scale = lax.rsqrt(jnp.mean(out * out, -1, keepdims=True) + 1e-05)
        dgain_ref[0:1] += jnp.sum(don * out * scale, 0, keepdims=True)
        du = don * gain_ref[0:1]
        dout = scale * du - out * (scale * scale * scale) * jnp.mean(
            out * du, -1, keepdims=True
        )
        heads.append((q, k, acts, beta, mixes, sigs, rho_q, rho_k, dout))
        for c in range(chunks):
            at = c * CHUNK
            strict, inclusive, _, _ = chunk_masks(aux, seg_row, at)
            first = aux[at : at + CHUNK, 1:2]
            kc, qc = k[at : at + CHUNK], q[at : at + CHUNK]
            do = dout[at : at + CHUNK]
            before, new = s_ref[sub, c], n_ref[sub, c]
            kk = mm_t(kc, kc)
            scores = jnp.where(inclusive, mm_t(qc, kc), 0.0)
            dscores = jnp.where(inclusive, mm_t(do, new), 0.0)
            dq = first * mm_t(do, before) + mm(dscores, kc)
            dk = t_mm(dscores, qc)
            gap = acts[2][at : at + CHUNK] - first * mm(kc, before)
            inner.append(
                (kk, strict, t_mm(scores, do), t_mm(first * qc, do), dq, dk, gap)
            )

    @pl.when(mine == 1)
    def _():
        state[...] = jnp.zeros_like(state)

    @pl.when(mine == 0)
    def _():
        for sub in range(PAIR):
            head = step * PAIR + sub
            hand_over(head).wait_recv()
            state[sub] = inbox[head]

    carried = [state[sub] for sub in range(PAIR)]
    pieces = [[None] * chunks for _ in range(PAIR)]
    for c in reversed(range(chunks)):
        at = c * CHUNK
        first = aux[at : at + CHUNK, 1:2]
        last = aux[at : at + CHUNK, 2:3]
        keep = aux[at + CHUNK - 1 : at + CHUNK, 1:2]
        for sub in range(PAIR):
            q, k, acts, beta = heads[sub][:4]
            kk, strict, pulled, reached, dq, dk, gap = inner[sub * chunks + c]
            kc = k[at : at + CHUNK]
            bc = beta[at : at + CHUNK]
            before, new = s_ref[sub, c], n_ref[sub, c]
            after = carried[sub].astype(BF16)
            dnew = pulled + mm(last * kc, after)
            back = t_mm(t_ref[sub, c], dnew)
            dv = bc * back
            dks = -(first * dv)
            carried[sub] = keep * carried[sub] + reached + t_mm(kc, dks)
            dsystem = jnp.where(strict, -mm_t(back, new), 0.0)
            dbeta = jnp.sum(back * gap, -1, keepdims=True) + jnp.sum(
                dsystem * kk, -1, keepdims=True
            )
            grow = bc * dsystem
            dk = (
                dk
                + last * mm_t(new, after)
                + mm_t(dks, before)
                + mm(grow, kc)
                + t_mm(grow, kc)
            )
            pieces[sub][c] = (dq, dk, dv, dbeta)

    @pl.when(mine == 1)
    def _():
        for sub in range(PAIR):
            head = step * PAIR + sub
            outbox[head] = carried[sub]
            hand_over(head).start()

    lane_ids = lax.broadcasted_iota(jnp.int32, (tokens, WIDTH), 1)
    for sub in range(PAIR):
        head = step * PAIR + sub
        q, k, acts, beta, mixes, sigs, rho_q, rho_k, dout = heads[sub]
        dq, dk, dv, dbeta = (
            jnp.concatenate([pieces[sub][c][item] for c in range(chunks)], 0)
            for item in range(4)
        )
        dbl_ref[...] += jnp.where(lane_ids == head, dbeta * beta * (1.0 - beta), 0.0)
        dq = dq * WIDTH ** (-0.5)
        dacts = (
            rho_q * dq
            - acts[0] * (rho_q * rho_q * rho_q) * jnp.sum(acts[0] * dq, -1, keepdims=True),
            rho_k * dk
            - acts[1] * (rho_k * rho_k * rho_k) * jnp.sum(acts[1] * dk, -1, keepdims=True),
            dv,
        )
        for index in range(3):
            sig = sigs[index]
            dmix = dacts[index] * sig * (1.0 + mixes[index] * (1.0 - sig))
            extended[sub, index, 0:tokens] = dmix
            tailbox[head, index] = dmix[0:8]

    @pl.when(mine == 1)
    def _():
        extended[:, :, tokens : tokens + 8] = jnp.zeros((PAIR, 3, 8, WIDTH), F32)
        for sub in range(PAIR):
            hand_tail(step * PAIR + sub).start()

    @pl.when(mine == 0)
    def _():
        for sub in range(PAIR):
            head = step * PAIR + sub
            hand_tail(head).wait_recv()
            extended[sub, :, tokens : tokens + 8] = headbox[head]

    later = [None] + [aux[:, 5 + off : 6 + off] for off in range(1, TAPS)]
    refs = (q_ref, k_ref, v_ref)
    for sub in range(PAIR):
        lanes = slice(sub * WIDTH, (sub + 1) * WIDTH)
        taps = taps_ref[:, lanes]
        for index in range(3):
            row = index * TAPS
            dmix = extended[sub, index, 0:tokens]
            dlin = dmix * taps[row : row + 1]
            dtaps_ref[row : row + 1, lanes] = jnp.sum(
                dmix * refs[index][0, HALO : HALO + tokens, lanes], 0, keepdims=True
            )
            for off in range(1, TAPS):
                dlin = dlin + taps[row + off : row + off + 1] * (
                    extended[sub, index, off : off + tokens] * later[off]
                )
                dtaps_ref[row + off : row + off + 1, lanes] = jnp.sum(
                    dmix * keeps[off] * refs[index][0, HALO - off : HALO - off + tokens, lanes],
                    0,
                    keepdims=True,
                )
            dlin_ref[0, index, :, lanes] = dlin.astype(BF16)
        dtaps_ref[12:16, lanes] = jnp.zeros((4, WIDTH), F32)

    @pl.when((step == pl.num_programs(0) - 1) & (mine == 1))
    def _():
        for head in range(outbox.shape[0]):
            hand_over(head).wait_send()
            hand_tail(head).wait_send()


def mixer_specs(rows, half_heads):
    per_half = half_heads // PAIR
    lanes = PAIR * WIDTH

    def at(offset):
        return pl.BlockSpec(
            (1, rows, lanes), lambda i: (i // per_half, 0, offset * per_half + i % per_half)
        )

    return [at(0), at(1), at(2)]


def mixer_fwd(linear, aux, seg_row, taps, gain):
    halves, rows, cols = linear.shape
    tokens = rows - HALO
    half_heads = cols // 3 // WIDTH
    heads = halves * half_heads
    per_half = half_heads // PAIR
    chunks = tokens // CHUNK
    lanes = PAIR * WIDTH

    def whole(shape):
        return pl.BlockSpec(shape, lambda i: (0,) * len(shape))

    token_spec = pl.BlockSpec((1, tokens, lanes), lambda i: (i // per_half, 0, i % per_half))
    square = pl.BlockSpec((PAIR, chunks, CHUNK, WIDTH), lambda i: (i, 0, 0, 0))
    square_shape = jax.ShapeDtypeStruct((heads, chunks, CHUNK, WIDTH), BF16)
    return pl.pallas_call(
        functools.partial(mixer_fwd_kernel, tokens),
        grid=(heads // PAIR,),
        in_specs=mixer_specs(rows, half_heads)
        + [
            whole(aux.shape),
            whole(seg_row.shape),
            pl.BlockSpec((16, lanes), lambda i: (0, i)),
            whole(gain.shape),
        ],
        out_specs=[token_spec, token_spec, square, square, square],
        out_shape=[
            jax.ShapeDtypeStruct((halves, tokens, half_heads * WIDTH), BF16),
            jax.ShapeDtypeStruct((halves, tokens, half_heads * WIDTH), F32),
            square_shape,
            square_shape,
            square_shape,
        ],
        scratch_shapes=[
            pltpu.VMEM((PAIR, WIDTH, WIDTH), F32),
            pltpu.VMEM((heads, WIDTH, WIDTH), F32),
            pltpu.VMEM((heads, WIDTH, WIDTH), F32),
            pltpu.SemaphoreType.DMA((heads,)),
            pltpu.SemaphoreType.DMA((heads,)),
        ],
        compiler_params=pltpu.CompilerParams(
            collective_id=0, has_side_effects=True, vmem_limit_bytes=VMEM_LIMIT
        ),
        name="mixer_fwd",
    )(linear, linear, linear, aux, seg_row, taps, gain)


def mixer_bwd(linear, aux, seg_row, taps, gain, out, new, inverse, before, donb):
    halves, rows, cols = linear.shape
    tokens = rows - HALO
    half_heads = cols // 3 // WIDTH
    heads = halves * half_heads
    per_half = half_heads // PAIR
    chunks = tokens // CHUNK
    lanes = PAIR * WIDTH

    def whole(shape):
        return pl.BlockSpec(shape, lambda i: (0,) * len(shape))

    token_spec = pl.BlockSpec((1, tokens, lanes), lambda i: (i // per_half, 0, i % per_half))
    square = pl.BlockSpec((PAIR, chunks, CHUNK, WIDTH), lambda i: (i, 0, 0, 0))
    taps_spec = pl.BlockSpec((16, lanes), lambda i: (0, i))
    return pl.pallas_call(
        functools.partial(mixer_bwd_kernel, tokens),
        grid=(heads // PAIR,),
        in_specs=mixer_specs(rows, half_heads)
        + [
            whole(aux.shape),
            whole(seg_row.shape),
            taps_spec,
            whole(gain.shape),
            token_spec,
            square,
            square,
            square,
            token_spec,
        ],
        out_specs=[
            pl.BlockSpec(
                (1, 3, tokens, lanes), lambda i: (i // per_half, 0, 0, i % per_half)
            ),
            whole((tokens, WIDTH)),
            taps_spec,
            whole((8, WIDTH)),
        ],
        out_shape=[
            jax.ShapeDtypeStruct((halves, 3, tokens, half_heads * WIDTH), BF16),
            jax.ShapeDtypeStruct((tokens, WIDTH), F32),
            jax.ShapeDtypeStruct((16, heads * WIDTH), F32),
            jax.ShapeDtypeStruct((8, WIDTH), F32),
        ],
        scratch_shapes=[
            pltpu.VMEM((PAIR, WIDTH, WIDTH), F32),
            pltpu.VMEM((PAIR, 3, tokens + 8, WIDTH), F32),
            pltpu.VMEM((heads, WIDTH, WIDTH), F32),
            pltpu.VMEM((heads, WIDTH, WIDTH), F32),
            pltpu.VMEM((heads, 3, 8, WIDTH), F32),
            pltpu.VMEM((heads, 3, 8, WIDTH), F32),
            pltpu.SemaphoreType.DMA((heads,)),
            pltpu.SemaphoreType.DMA((heads,)),
            pltpu.SemaphoreType.DMA((heads,)),
            pltpu.SemaphoreType.DMA((heads,)),
        ],
        compiler_params=pltpu.CompilerParams(
            collective_id=1, has_side_effects=True, vmem_limit_bytes=VMEM_LIMIT
        ),
        name="mixer_bwd",
    )(linear, linear, linear, aux, seg_row, taps, gain, out, new, inverse, before, donb)


def product(left, right):
    return jnp.dot(left, right, preferred_element_type=F32)


def back_product(left, right):
    return lax.dot_general(left, right, (((1,), (1,)), ((), ())), preferred_element_type=F32)


def transposed(left, right):
    return lax.dot_general(left, right, (((0,), (0,)), ((), ())), preferred_element_type=F32)


def norm_back(d_rows, unit, rho, gain_f):
    d_unit = d_rows * gain_f
    d_input = rho * (d_unit - unit * jnp.mean(d_unit * unit, -1, keepdims=True))
    return (d_input, jnp.sum(d_rows * unit, 0))


def mixer_tables(segments, length, beta, tokens):
    mine = lax.axis_index("tensor")
    seg = segments[0]
    position = jnp.arange(length)

    def behind(off):
        return jnp.where(position >= off, jnp.roll(seg, off), -1)

    ends = jnp.repeat(seg[CHUNK - 1 :: CHUNK], CHUNK)
    previous = jnp.where(position >= CHUNK, jnp.roll(ends, CHUNK), -1)
    columns = [seg, seg == previous, seg == ends]
    keeps = [behind(off) == seg for off in range(1, TAPS)]
    columns += keeps
    for off in range(1, TAPS):
        columns.append(jnp.where(position < length - off, jnp.roll(keeps[off - 1], -off), False))
    table = jnp.stack([c.astype(F32) for c in columns], 1)
    table = lax.dynamic_slice_in_dim(table, mine * tokens, tokens, 0)
    aux = jnp.concatenate(
        [
            table,
            jnp.zeros((tokens, 16 - table.shape[1]), F32),
            beta,
            jnp.zeros((tokens, WIDTH - 16 - beta.shape[1]), F32),
        ],
        1,
    )
    row = lax.dynamic_slice_in_dim(seg.astype(F32), mine * tokens, tokens, 0)
    return aux, jnp.broadcast_to(row[None], (8, tokens))


def local(
    layer_input, segments, valid_mask, teacher, out_grad, norm_gain, w_query, w_key, w_value,
    w_beta, conv_weight, head_gain, w_out, mlp_gain, w_gate, w_up, w_down,
):
    both = ("tensor", "dp")
    parts, halves = lax.axis_size("dp"), lax.axis_size("tensor")
    tokens, width_d = layer_input.shape[1:]
    length = segments.shape[1]
    tokens_all = tokens * parts * halves
    half_heads = w_beta.shape[1]
    heads = half_heads * halves
    half_cols = w_query.shape[1]
    half_units = w_gate.shape[1]

    small = jnp.concatenate(
        [w_beta.reshape(-1), conv_weight.reshape(-1), norm_gain, mlp_gain, head_gain]
    )
    small = lax.all_gather(small, both, axis=0, tiled=False)
    first_w = lax.all_gather(
        jnp.concatenate([w_query, w_key, w_value], 1), both, axis=0, tiled=True
    ).reshape(halves, width_d, 3 * half_cols)
    second_w = lax.all_gather(
        jnp.concatenate([w_out.T, w_gate, w_up, w_down.T], 1), both, axis=0, tiled=True
    ).reshape(halves, width_d, half_cols + 3 * half_units)
    w_o = second_w[:, :, :half_cols]
    w_gu = second_w[:, :, half_cols : half_cols + 2 * half_units]
    w_d = second_w[:, :, half_cols + 2 * half_units :]

    small = small.reshape(halves, parts, -1)
    sizes = [w_beta.size, conv_weight.size, norm_gain.size, mlp_gain.size, head_gain.size]
    marks = [sum(sizes[:i]) for i in range(6)]
    beta_w, conv_w, gain_one, gain_two, gain_head = (
        small[:, :, marks[i] : marks[i + 1]] for i in range(5)
    )
    beta_w = beta_w.reshape(halves, width_d, half_heads).transpose(1, 0, 2).reshape(width_d, heads)
    taps = conv_w.reshape((halves, parts) + conv_weight.shape).transpose(2, 3, 0, 4, 1, 5)
    taps = taps.reshape(12, heads * WIDTH).astype(F32)
    taps = jnp.concatenate([taps, jnp.zeros((4, heads * WIDTH), F32)], 0)
    gain_one = gain_one[0].reshape(1, width_d).astype(F32)
    gain_two = gain_two[0].reshape(1, width_d).astype(F32)
    gain_head = jnp.broadcast_to(gain_head[0].reshape(1, WIDTH).astype(F32), (8, WIDTH))

    inputs = layer_input[0].astype(F32)
    rho_one = lax.rsqrt(jnp.mean(inputs * inputs, -1, keepdims=True) + 1e-05)
    unit_one = inputs * rho_one
    normed_one = (unit_one * gain_one).astype(BF16)
    halo = lax.ppermute(normed_one[-HALO:], "tensor", [(0, 1), (1, 0)])
    spread = jnp.concatenate([halo, normed_one], 0)
    linear = jnp.einsum("td,jdc->jtc", spread, first_w, preferred_element_type=F32)
    strength = jax.nn.sigmoid(product(normed_one, beta_w))
    aux, seg_row = mixer_tables(segments, length, strength, tokens)
    onb, out, new, inverse, before = mixer_fwd(linear, aux, seg_row, taps, gain_head)
    attention = sum(back_product(onb[j], w_o[j]) for j in range(halves))
    hidden = inputs + attention
    rho_two = lax.rsqrt(jnp.mean(hidden * hidden, -1, keepdims=True) + 1e-05)
    unit_two = hidden * rho_two
    normed_two = (unit_two * gain_two).astype(BF16)
    mlp_rows = 0.0
    kept = []
    for j in range(halves):
        gate = product(normed_two, w_gu[j, :, :half_units])
        upper = product(normed_two, w_gu[j, :, half_units:])
        sig = jax.nn.sigmoid(gate)
        active = gate * sig
        inner = (active * upper).astype(BF16)
        mlp_rows = mlp_rows + back_product(inner, w_d[j])
        kept.append((gate, upper, sig, active, inner))
    outputs = hidden + mlp_rows
    mask = valid_mask[0].astype(F32)[:, None]
    differ = outputs - teacher[0].astype(F32)
    valid_sum = lax.psum(jnp.sum(mask), ("dp", "tensor"))
    square_sum = lax.psum(jnp.sum(mask * differ * differ), ("dp", "tensor"))
    loss_value = square_sum / (width_d * valid_sum)
    d_out = out_grad[0].astype(F32) + mask * differ * (tokens_all / 4.0) / valid_sum
    d_mlp = d_out.astype(BF16)
    d_two = 0.0
    grads = []
    for j in range(halves):
        gate, upper, sig, active, inner = kept[j]
        d_inner = product(d_mlp, w_d[j])
        d_gate = (d_inner * upper * sig * (1.0 + gate * (1.0 - sig))).astype(BF16)
        d_upper = (d_inner * active).astype(BF16)
        d_two = (
            d_two
            + back_product(d_gate, w_gu[j, :, :half_units])
            + back_product(d_upper, w_gu[j, :, half_units:])
        )
        grads.append(
            [
                transposed(normed_two, d_gate),
                transposed(normed_two, d_upper),
                transposed(d_mlp, inner),
            ]
        )
    d_norm_two, grad_gain_two = norm_back(d_two, unit_two, rho_two, gain_two)
    d_hidden = d_out + d_norm_two
    d_attention = d_hidden.astype(BF16)
    donb = jnp.stack([product(d_attention, w_o[j]) for j in range(halves)])
    for j in range(halves):
        grads[j].insert(0, transposed(d_attention, onb[j]))
    second_g = jnp.stack([jnp.concatenate([g.astype(BF16) for g in grads[j]], 1) for j in range(halves)])
    second_g = lax.psum_scatter(
        second_g.reshape(halves * width_d, -1), both, scatter_dimension=0, tiled=True
    ).astype(F32)
    dlin, dbl, dtaps, dgain = mixer_bwd(
        linear, aux, seg_row, taps, gain_head, out, new, inverse, before, donb
    )
    d_beta = dbl[:, :heads].astype(BF16)
    d_one = back_product(d_beta, beta_w)
    first_g = []
    for j in range(halves):
        row = []
        for c in range(3):
            d_one = d_one + back_product(
                dlin[j, c], first_w[j, :, c * half_cols : (c + 1) * half_cols]
            )
            row.append(transposed(normed_one, dlin[j, c]).astype(BF16))
        first_g.append(jnp.concatenate(row, 1))
    first_g = lax.psum_scatter(
        jnp.concatenate(first_g, 0), both, scatter_dimension=0, tiled=True
    ).astype(F32)
    grad_beta = transposed(normed_one, d_beta)
    d_norm_one, grad_gain_one = norm_back(d_one, unit_one, rho_one, gain_one)
    d_input = d_hidden + d_norm_one

    tail = jnp.concatenate(
        [
            grad_beta.reshape(-1),
            dtaps[:12].reshape(-1),
            grad_gain_one,
            grad_gain_two,
            dgain[0],
        ]
    )
    tail = lax.psum(tail, ("dp", "tensor"))
    tail_sizes = [width_d * heads, 12 * heads * WIDTH, width_d, width_d, WIDTH]
    cuts = [sum(tail_sizes[:i]) for i in range(6)]
    g_beta, g_conv, g_one, g_two, g_head = (tail[cuts[i] : cuts[i + 1]] for i in range(5))
    d_at, t_at = lax.axis_index("dp"), lax.axis_index("tensor")

    def own(values, dim, at, size):
        return lax.dynamic_slice_in_dim(values, at * size, size, dim)

    g_beta = own(g_beta.reshape(width_d, heads), 0, d_at, w_beta.shape[0])
    g_beta = own(g_beta, 1, t_at, half_heads)
    g_conv = own(g_conv.reshape(3, TAPS, heads, WIDTH), 2, t_at, half_heads)
    g_conv = own(g_conv, 3, d_at, conv_weight.shape[3])
    g_one = own(g_one, 0, d_at, norm_gain.shape[0])
    g_two = own(g_two, 0, d_at, mlp_gain.shape[0])
    g_head = own(g_head, 0, d_at, head_gain.shape[0])
    return (
        outputs.astype(BF16)[None],
        loss_value,
        d_input[None],
        g_one,
        first_g[:, :half_cols],
        first_g[:, half_cols : 2 * half_cols],
        first_g[:, 2 * half_cols :],
        g_beta,
        g_conv,
        g_head,
        second_g[:, :half_cols].T,
        g_two,
        second_g[:, half_cols : half_cols + half_units],
        second_g[:, half_cols + half_units : half_cols + 2 * half_units],
        second_g[:, half_cols + 2 * half_units :].T,
    )


def solution(mesh):
    in_specs = (
        P("dp", "tensor", None),
        P("dp", None),
        P("dp", "tensor"),
        P("dp", "tensor", None),
        P("dp", "tensor", None),
        P("dp"),
        P("dp", "tensor"),
        P("dp", "tensor"),
        P("dp", "tensor"),
        P("dp", "tensor"),
        P(None, None, "tensor", "dp"),
        P("dp"),
        P("tensor", "dp"),
        P("dp"),
        P("dp", "tensor"),
        P("dp", "tensor"),
        P("tensor", "dp"),
    )
    out_specs = (
        P("dp", "tensor", None),
        P(),
        P("dp", "tensor", None),
        P("dp"),
        P("dp", "tensor"),
        P("dp", "tensor"),
        P("dp", "tensor"),
        P("dp", "tensor"),
        P(None, None, "tensor", "dp"),
        P("dp"),
        P("tensor", "dp"),
        P("dp"),
        P("dp", "tensor"),
        P("dp", "tensor"),
        P("tensor", "dp"),
    )
    return jax.shard_map(local, mesh=mesh, in_specs=in_specs, out_specs=out_specs, check_vma=False)
```

time: 1900 us -> 881 us (0.46)
  other arithmetic: 425 us -> 43.9 us
  waiting for transfers between devices: 719 us -> 441 us
  matrix products: 317 us -> 116 us
  local copies, waits for them, and re-layouts: 181 us -> 35.8 us
  blocking collectives: 221 us -> 84.5 us
  Pallas kernels: 0 us -> 123 us
    another operation x21 -> x4, other arithmetic: 321 us -> 14.2 us  [the longest x3 12.8 us: local(): jnp.stack([jnp.concatenate([g.astype(BF16) for g in grads[j]], 1) for j i...]
    reduce_scatter x11 -> x1, waiting for transfers between devices: 491 us -> 204 us  [local(): lax.psum_scatter(second_g.reshape(halves * width_d, -1), both, scatter_di...]
    dot_general x78 -> x10, matrix products: 235 us -> 36.4 us  [the longest x9 28.2 us: product(): return jnp.dot(left, right, preferred_element_type=F32)]
    all_gather x11 -> x2, waiting for transfers between devices: 224 us -> 56.5 us  [the longest x1 42.4 us: local(): lax.all_gather(jnp.concatenate([w_out.T, w_gate, w_up, w_down.T], 1), bot...]
    pallas_call x0 -> x2, Pallas kernels: none -> 123 us  [the longest x1 77.5 us: mixer_fwd(): pl.pallas_call(functools.partial(mixer_fwd_kernel, tokens), grid=(heads /...]
    unnamed x24 -> x6, waiting for transfers between devices: 4.61 us -> 115 us
    psum x0 -> x1, waiting for transfers between devices: none -> 66.3 us  [local(): tail = lax.psum(tail, ('dp', 'tensor'))]
    unnamed x2 -> x1, blocking collectives: 98.3 us -> 42.8 us
  transfers between devices with their start and end apart: 23 -> 6, of which waited for: 15 -> 5; matrix products, arithmetic and copies ran while one was open for 31% -> 10% of each run, Pallas kernels for 0% -> 9%
where the time goes in v1:
time: 881 us; the launch traced here: 866 us
  waiting for transfers between devices  441 us (50%)
  Pallas kernels  123 us (14%)
  matrix products  116 us (13%)
  blocking collectives  84.5 us (10%)
  other arithmetic  43.9 us (5%)
  local copies, waits for them, and re-layouts  35.8 us (4%)
  between operations  18.4 us (2%)
    reduce_scatter x1, waiting for transfers between devices, local(): lax.psum_scatter(second_g.reshape(halves * width_d, -1), both, scatter_di...  204 us
    unnamed x6, waiting for transfers between devices  115 us
    pallas_call x1, Pallas kernels, mixer_fwd(): pl.pallas_call(functools.partial(mixer_fwd_kernel, tokens), grid=(heads /...  77.5 us
    psum x1, waiting for transfers between devices, local(): tail = lax.psum(tail, ('dp', 'tensor'))  66.3 us
    dot_general x15, matrix products, back_product(): lax.dot_general(left, right, (((1,), (1,)), ((), ())), preferred_element_...  51.8 us
    pallas_call x1, Pallas kernels, mixer_bwd(): pl.pallas_call(functools.partial(mixer_bwd_kernel, tokens), grid=(heads /...  45.9 us
    unnamed x1, blocking collectives  42.8 us
    all_gather x1, waiting for transfers between devices, local(): lax.all_gather(jnp.concatenate([w_out.T, w_gate, w_up, w_down.T], 1), bot...  42.4 us
  transfers between devices with their start and end apart: 6, of which 5 were waited for; matrix products, arithmetic and copies ran while one was open for 10% of the time, Pallas kernels for 9%

profile of v1, /device:TPU:0, one launch (start us, length us, event | category | flops | bytes accessed | tf_op | source)
XLA Modules:
  0.0 865.6 jit_solution(17428501881899778216)
XLA Ops:
  13.1 42.8 %all-reduce.2 = bf16[24832]{0:T(1024)(128)(2,1)S(1)} all-reduce(bf16[24832]{0:T(1024)(128)(2,1)S(1)} %dynamic-update-slice), channel_id=2, replica_groups=mesh['dp'=16,'tensor'=2] {'tensor','dp'}, use_global_device_ids=true, to_apply=%add.2 | all-reduce | flops 24832 | bytes 99328
  69.9 14.1 %all-gather.4.cloned.1.call-done = bf16[2048,1536]{1,0:T(8,128)(2,1)} async-done(((bf16[64,1536]{1,0:T(8,128)(2,1)}), bf16[2048,1536]{1,0:T(8,128)(2,1)}) %all-gather.4.cloned.1.call-update) | async-done | bytes 6291472 | tf_op jit(solution)/shard_map/all_gather | solution.py:573
  83.9 8.3 convolution_bitcast_fusion.q_ref.k_ref.v_ref
  93.4 77.5 %mixer_fwd.1 = (bf16[2,512,512]{2,1,0:T(8,128)(2,1)}, f32[2,512,512]{2,1,0:T(8,128)}, bf16[8,4,128,128]{3,2,1,0:T(8,128)(2,1)}, bf16[8,4,128,128]{3,2,1,0:T(8,128)(2,1)}, bf16[8,4,128,128]{3,2,1,0:T(8,128)(2,1)}) custom-call(f32[2,528,1536]{2,1,0:T(8,128)} %convolution_bitcast_fusion.q_ref.k_ref.v_ref, ...), custom_call_target="tpu_custom_call" | custom-call | tf_op jit(solution)/shard_map/mixer_fwd/pallas_call | solution.py:412
  171.0 42.4 %all-gather.6.cloned.1.call-done = bf16[2048,4736]{1,0:T(8,128)(2,1)} async-done(((bf16[64,4736]{1,0:T(8,128)(2,1)}), bf16[2048,4736]{1,0:T(8,128)(2,1)}) %all-gather.6.cloned.1.call-update) | async-done | bytes 19398672 | tf_op jit(solution)/shard_map/all_gather | solution.py:576
  218.2 4.7 fusion.16
  229.0 3.5 multiply_convert_fusion.5
  234.4 3.8 fusion.31
  238.2 41.7 %all-reduce.3 = (f32[]{:T(128)}, f32[]{:T(128)}) all-reduce(f32[]{:T(128)} %convert_reduce_fusion, f32[]{:T(128)} %get-tuple-element.154), channel_id=1, replica_groups=mesh['dp'=16,'tensor'=2] {'dp','tensor'}, use_global_device_ids=true, to_apply=%region_5.6 | all-reduce | flops 2 | bytes 16 | tf_op jit(solution)/shard_map/psum | solution.py:625
  279.9 3.6 fusion.87
  283.5 5.6 multiply_convert_fusion
  289.2 4.7 fusion.15
  293.9 4.3 multiply_convert_fusion.2
  298.3 4.7 fusion.9
  303.0 3.6 fusion.11
  306.6 4.3 multiply_reduce_fusion
  319.9 45.9 %mixer_bwd.1 = (bf16[2,3,512,512]{3,2,1,0:T(8,128)(2,1)}, f32[512,128]{1,0:T(8,128)}, f32[16,1024]{1,0:T(8,128)}, f32[8,128]{1,0:T(8,128)}) custom-call(f32[2,528,1536]{2,1,0:T(8,128)} %convolution_bitcast_fusion.q_ref.k_ref.v_ref, f32[2,528,1536]{2,1,0:T(8,128)} %convolution_bitcast_fusion.q_ref.k_ref.v_ref, ...), custom_call_target="tpu_custom_call" | custom-call | tf_op jit(solution)/shard_map/mixer_bwd/pallas_call | solution.py:459
  397.0 7.1 fusion.27
  405.5 8.8 %maximum_maximum_fusion = bf16[2048,1536]{0,1:T(8,128)(2,1)} fusion(bf16[1024,512]{0,1:T(8,128)(2,1)} %convolution_convert_fusion.8, bf16[1024,512]{0,1:T(8,128)(2,1)} %convolution_convert_fusion.9, bf16[1024,512]{0,1:T(8,128)(2,1)} %convolution_convert_fusion.10, bf16[1024,512]{0,1:T(8,128)(2,1)} %convolution_convert_fusion.11, ...), kind=kLoop, calls=%fused_computation.3 | loop fusion | flops 37748736 | bytes 12582912 | tf_op jit(solution)/shard_map/concatenate | solution.py:674
  414.3 8.7 %copy.137 = bf16[2048,1536]{1,0:T(8,128)(2,1)} copy(bf16[2048,1536]{0,1:T(8,128)(2,1)} %maximum_maximum_fusion) | data formatting | bytes 12582912
  445.9 8.3 pad_maximum_fusion
  459.2 66.3 %all-reduce.6.cloned.1.call-done = f32[22656]{0:T(1024)} async-done(((f32[22656]{0:T(1024)}), f32[22656]{0:T(1024)}) %all-reduce.6.cloned.1.call-update) | async-done | bytes 90640 | tf_op jit(solution)/shard_map/psum | solution.py:689
  531.9 114.5 %reduce-scatter.7.cloned.1.call-done = bf16[64,1536]{1,0:T(8,128)(2,1)} async-done(((bf16[2048,1536]{1,0:T(8,128)(2,1)}), bf16[64,1536]{1,0:T(8,128)(2,1)}) %reduce-scatter.7.cloned.1.call-update) | async-done | bytes 196624
  649.9 204.0 %reduce-scatter.5.cloned.1.call-done = bf16[64,4736]{1,0:T(8,128)(2,1)} async-done(((bf16[2048,4736]{1,0:T(8,128)(2,1)}), bf16[64,4736]{1,0:T(8,128)(2,1)}) %reduce-scatter.5.cloned.1.call-update) | async-done | bytes 606224 | tf_op jit(solution)/shard_map/reduce_scatter | solution.py:656
  (238 shorter events, 113.9 us)
Async XLA Ops:
  7.2 5.5 copy-start.28
  7.2 5.5 copy-start.29
  7.2 5.5 copy-start.30
  7.2 48.9 %copy-start = (bf16[1,512,1024]{2,1,0:T(8,128)(2,1)S(1)}, bf16[1,512,1024]{2,1,0:T(8,128)(2,1)}, u32[]{:S(2)}) copy-start(bf16[1,512,1024]{2,1,0:T(8,128)(2,1)} %param.17) | copy-start | bytes 3145732
  7.3 76.7 %all-gather.4.cloned.1.call-start = ((), (), s32[]{:S(2)}) async-start(), calls=%async_computation.2 | async-start | bytes 6488064 | tf_op jit(solution)/shard_map/all_gather | solution.py:573
  9.0 204.4 %all-gather.6.cloned.1.call-start = ((), (), s32[]{:S(2)}) async-start(), calls=%async_computation.3 | async-start | bytes 20004864 | tf_op jit(solution)/shard_map/all_gather | solution.py:576
  11.1 48.0 %copy-start.22 = (s32[1,1024]{1,0:T(1,128)S(1)}, s32[1,1024]{1,0:T(1,128)}, u32[]{:S(2)}) copy-start(s32[1,1024]{1,0:T(1,128)} %param.18) | copy-start | bytes 12292
  11.1 514.4 %all-reduce.6.cloned.1.call-start = ((), (), s32[]{:S(2)}) async-start(), calls=%async_computation.4 | async-start | bytes 188416 | tf_op jit(solution)/shard_map/psum | solution.py:689
  56.7 27.2 %copy-start.3 = (bf16[512,1024]{1,0:T(8,128)(2,1)}, bf16[512,1024]{1,0:T(8,128)(2,1)S(1)}, u32[]{:S(2)}) copy-start(bf16[512,1024]{1,0:T(8,128)(2,1)S(1)} %fusion.21) | copy-start | bytes 3145732
  56.8 13.1 %collective-permute-start = (bf16[16,1024]{1,0:T(8,128)(2,1)S(1)}, bf16[16,1024]{1,0:T(8,128)(2,1)S(1)}, u32[]{:S(2)}, u32[]{:S(2)}) collective-permute-start(bf16[16,1024]{1,0:T(8,128)(2,1)S(1)} %slice.320), channel_id=1, source_target_pairs={{0,1},{1,0},{2,3},{3,2},{4,5},{5,4},{6,7},{7,6},{8,9},{9,8},{10,11... | collective-permute-start | bytes 98312 | tf_op jit(solution)/shard_map/ppermute | solution.py:601
  215.6 8.1 copy-start.12
  218.2 10.8 %copy-start.20 = (bf16[512,1024]{1,0:T(8,128)(2,1)}, bf16[512,1024]{1,0:T(8,128)(2,1)S(1)}, u32[]{:S(2)}) copy-start(bf16[512,1024]{1,0:T(8,128)(2,1)S(1)} %multiply_convert_fusion.6) | copy-start | bytes 3145732
  229.0 5.4 copy-start.32
  283.5 10.4 %copy-start.15 = (bf16[512,1024]{1,0:T(8,128)(2,1)}, bf16[512,1024]{1,0:T(8,128)(2,1)S(1)}, u32[]{:S(2)}) copy-start(bf16[512,1024]{1,0:T(8,128)(2,1)S(1)} %fusion.87) | copy-start | bytes 3145732
  289.1 4.7 copy-start.42
  289.1 17.5 %copy-start.10 = (bf16[512,1408]{1,0:T(8,128)(2,1)}, bf16[512,1408]{1,0:T(8,128)(2,1)S(1)}, u32[]{:S(2)}) copy-start(bf16[512,1408]{1,0:T(8,128)(2,1)S(1)} %get-tuple-element.116) | copy-start | bytes 4325380
  289.1 4.7 copy-start.35
  289.1 4.7 copy-start.46
  298.2 4.7 copy-start.40
  298.2 4.7 copy-start.44
  306.6 4.4 copy-start.2
  306.6 4.4 copy-start.6
  405.5 240.9 %reduce-scatter.7.cloned.1.call-start = ((), (), s32[]{:S(2)}) async-start(), calls=%async_computation.6 | async-start | bytes 6488064
  423.1 430.8 %reduce-scatter.5.cloned.1.call-start = ((), (), s32[]{:S(2)}) async-start(), calls=%async_computation.5 | async-start | bytes 20004864 | tf_op jit(solution)/shard_map/reduce_scatter | solution.py:656
  (29 other events, 71.6 us)
Sparse Core Ops, SparseCore 0:
  11.5 72.3 all-gather.3
  87.4 125.9 all-gather.5
  405.6 119.8 all-reduce.5
  531.0 115.3 reduce-scatter.6
  648.6 205.2 reduce-scatter.4

commit v2 on v1

v2 whole, which is shorter than its diff:
```python
import collections
import functools
import itertools

import jax
import jax.numpy as jnp
from jax import lax
from jax.experimental import pallas as pl
from jax.experimental.pallas import tpu as pltpu
from jax.sharding import PartitionSpec as P

F32, BF16 = jnp.float32, jnp.bfloat16
MESH = pl.DeviceIdType.MESH
CHUNK = 128
HALO = 16
WIDTH = 128
PAIR = 2
EARLY = 4
TAPS = 4
VMEM_LIMIT = 60 * 1024 * 1024

GRID = (4, 2, 2)
DEPTH = GRID[0] - 1 + 2
LAGS = DEPTH + 2
LINKS = [("z", 1), ("z", -1), ("x", 0), ("y", 0)]
Tiles = collections.namedtuple(
    "Tiles", ["array", "order", "row", "rows", "col", "stride", "cols", "count", "start"]
)


def on_grid():
    return lax.axis_size("dp") == GRID[0] * GRID[1] * GRID[2] and lax.axis_size("tensor") == 2


def position():
    mine = lax.axis_index("dp")
    _, size_x, size_c = GRID
    return {
        "y": lax.axis_index("tensor"),
        "z": mine // (size_x * size_c),
        "x": (mine // size_c) % size_x,
        "c": mine % size_c,
    }


def device_of(at):
    _, size_x, size_c = GRID
    return {"dp": (at["z"] * size_x + at["x"]) * size_c + at["c"], "tensor": at["y"]}


def inside(z):
    return (z >= 0) & (z < GRID[0])


def across(at, link):
    axis, way = link
    return dict(at, z=at["z"] + way) if axis == "z" else dict(at, **{axis: 1 - at[axis]})


def greet_all(at):
    barrier = pltpu.get_barrier_semaphore()
    for link in (("x", 0), ("y", 0), ("c", 0)):
        pl.semaphore_signal(
            barrier, inc=1, device_id=device_of(across(at, link)), device_id_type=MESH
        )
    for way in (-1, 1):

        @pl.when(inside(at["z"] + way))
        def _():
            pl.semaphore_signal(
                barrier,
                inc=1,
                device_id=device_of(across(at, ("z", way))),
                device_id_type=MESH,
            )

    peers = 3 + inside(at["z"] - 1).astype(jnp.int32) + inside(at["z"] + 1).astype(jnp.int32)
    pl.semaphore_wait(barrier, peers)


def remote(src, dst, send_sem, recv_sem, to):
    return pltpu.make_async_remote_copy(
        src_ref=src, dst_ref=dst, send_sem=send_sem, recv_sem=recv_sem,
        device_id=device_of(to), device_id_type=MESH,
    )


def offsets(lag):
    every = itertools.product(range(1 - GRID[0], GRID[0]), (0, 1), (0, 1))
    return [off for off in every if abs(off[0]) + off[1] + off[2] == lag]


def moved(at, off):
    return dict(
        at,
        z=at["z"] + off[0],
        x=1 - at["x"] if off[1] else at["x"],
        y=1 - at["y"] if off[2] else at["y"],
    )


def last_axis(order, off):
    shifts = {"z": off[0], "x": off[1], "y": off[2]}
    return max([order.index(axis) for axis in order if shifts[axis]], default=-1)


def onward(order, off):
    last = last_axis(order, off)
    out = []
    if last >= 0 and order[last] == "z":
        out.append(("z", 1 if off[0] < 0 else -1))
    for axis in order[last + 1 :]:
        out += [("z", 1), ("z", -1)] if axis == "z" else [(axis, 0)]
    return out


def backward_link(order, off):
    axis = order[last_axis(order, off)]
    return (axis, (1 if off[0] > 0 else -1) if axis == "z" else 0)


def block_id(at):
    return (at["z"] * GRID[1] + at["x"]) * 2 + at["y"]


def inbox_id(order, link, at):
    if link[0] == "y" or (link[0] == "z" and order[0] != "y"):
        return at["z"] * 2 + at["x"]
    return at["z"] * 2 + at["y"]


def when(test, action):
    if test is None:
        action()
    else:
        pl.when(test)(action)


def both(first, second):
    if first is None or second is None:
        return second if first is None else first
    return first & second


def split_tiles(cols, rows, unit=WIDTH, array=0, start=0):
    half = rows // 2
    count = cols // (3 * unit)
    out = [
        Tiles(array, "zxy", 0, half, 0, 3 * unit, unit, count, start),
        Tiles(array, "zyx", half, half, 0, 3 * unit, unit, count, start),
        Tiles(array, "xzy", 0, half, unit, 3 * unit, 2 * unit, count, start),
        Tiles(array, "yzx", half, half, unit, 3 * unit, 2 * unit, count, start),
    ]
    rest = cols - 3 * unit * count
    if rest:
        out.append(Tiles(array, "xzy", 0, half, cols - rest, rest, rest, 1, start))
        out.append(Tiles(array, "yzx", half, half, cols - rest, rest, rest, 1, start))
    return out


def window(tile, group):
    start = tile.col + group * tile.stride
    if not isinstance(start, int):
        start = pl.multiple_of(start, 128)
    return pl.ds(tile.row, tile.rows), pl.ds(start, tile.cols)


def steps_of(tiles):
    return max(tile.start + tile.count for tile in tiles) + LAGS - 1


def first_slots(tiles):
    return [sum(tile.count for tile in tiles[:i]) for i in range(len(tiles))]


class Gather:
    def __init__(self, tiles, shards, fulls, sems):
        self.tiles, self.shards, self.fulls = tiles, shards, fulls
        self.send_sem, self.recv_sem, self.core_send, self.core_recv, self.own_sem = sems
        self.at = position()
        self.steps = steps_of(tiles)

    @staticmethod
    def sems(tiles, arrays):
        slots = sum(tile.count for tile in tiles)
        return [
            pltpu.SemaphoreType.DMA((len(tiles), 2, len(LINKS), 16)),
            pltpu.SemaphoreType.DMA((slots, 16)),
            pltpu.SemaphoreType.DMA((slots,)),
            pltpu.SemaphoreType.DMA((slots,)),
            pltpu.SemaphoreType.DMA((arrays,)),
        ]

    def begin(self):
        at = self.at
        copies = [
            pltpu.make_async_copy(
                shard, full.at[at["y"], at["z"], at["x"], at["c"]], self.own_sem.at[i]
            )
            for i, (shard, full) in enumerate(zip(self.shards, self.fulls))
        ]
        for copy in copies:
            copy.start()
        greet_all(at)
        for copy in copies:
            copy.wait()

    def copy(self, index, group, slot, src, link, own):
        tile = self.tiles[index]
        rows, cols = window(tile, group)
        full = self.fulls[tile.array].at[src["y"], src["z"], src["x"], src["c"], rows, cols]
        return remote(
            self.shards[tile.array].at[rows, cols] if own else full,
            full,
            self.send_sem.at[index, group % 2, LINKS.index(link), block_id(src)],
            self.recv_sem.at[slot, block_id(src)],
            across(self.at, link),
        )

    def visit(self, index, group, slot, lag):
        at, tile = self.at, self.tiles[index]
        for off in offsets(lag) if lag <= DEPTH else ():
            src = moved(at, off)

            def handle():
                if lag:
                    self.copy(index, group, slot, src, LINKS[-1], False).wait_recv()
                for link in onward(tile.order, off):

                    def send():
                        one = self.copy(index, group, slot, src, link, lag == 0)
                        pl.when(group >= 2)(one.wait_send)
                        one.start()

                    when(inside(at["z"] + link[1]) if link[0] == "z" else None, send)

            when(inside(src["z"]) if off[0] else None, handle)
        if lag >= DEPTH:
            rows, cols = window(tile, group)
            part = self.fulls[tile.array].at[:, :, :, at["c"], rows, cols]
            pair = remote(
                part, part, self.core_send.at[slot], self.core_recv.at[slot], across(at, ("c", 0))
            )
            pair.start() if lag == DEPTH else pair.wait()

    def step(self, step):
        for lag in range(LAGS):
            for index, (tile, first) in enumerate(zip(self.tiles, first_slots(self.tiles))):
                group = step - lag - tile.start
                pl.when((group >= 0) & (group < tile.count))(
                    functools.partial(self.visit, index, group, first + group, lag)
                )

    def finish(self):
        for index, tile in enumerate(self.tiles):
            for group in range(max(0, tile.count - 2), tile.count):
                for off in [off for lag in range(DEPTH + 1) for off in offsets(lag)]:
                    src = moved(self.at, off)
                    here = inside(src["z"]) if off[0] else None
                    for link in onward(tile.order, off):
                        there = inside(self.at["z"] + link[1]) if link[0] == "z" else None
                        one = self.copy(index, group, 0, src, link, False)
                        when(both(here, there), one.wait_send)


class Scatter:
    def __init__(self, tiles, grads, put, boxes, sems):
        self.tiles, self.grads, self.put = tiles, grads, put
        count = len(tiles)
        self.sums, self.pairs, self.inbox = boxes[:count], boxes[count : 2 * count], boxes[2 * count :]
        self.send_sem, self.recv_sem, self.core_send, self.core_recv, self.own_sem = sems
        self.at = position()
        self.steps = steps_of(tiles)

    @staticmethod
    def boxes(tiles, dtypes):
        whole, part = [], []
        for tile in tiles:
            dtype = dtypes[tile.array]
            whole.append(
                pltpu.VMEM((tile.count, 2) + GRID[:2] + (tile.rows, tile.cols), dtype)
            )
            part.append(pltpu.VMEM((tile.count, len(LINKS), 8, tile.rows, tile.cols), dtype))
        return whole + whole + part

    @staticmethod
    def sems(tiles):
        slots = sum(tile.count for tile in tiles)
        return [
            pltpu.SemaphoreType.DMA((len(tiles), 2, 16)),
            pltpu.SemaphoreType.DMA((slots, len(LINKS), 8)),
            pltpu.SemaphoreType.DMA((slots,)),
            pltpu.SemaphoreType.DMA((slots,)),
            pltpu.SemaphoreType.DMA((slots,)),
        ]

    def begin(self):
        greet_all(self.at)

    def copy(self, index, group, slot, dest, link, label):
        tile = self.tiles[index]
        box = inbox_id(tile.order, label, dest)
        return remote(
            self.sums[index].at[group, dest["y"], dest["z"], dest["x"]],
            self.inbox[index].at[group, LINKS.index(label), box],
            self.send_sem.at[index, group % 2, block_id(dest)],
            self.recv_sem.at[slot, LINKS.index(label), box],
            across(self.at, link),
        )

    def visit(self, index, group, slot, stage):
        at, tile = self.at, self.tiles[index]
        rows, cols = window(tile, group)
        grad, sums = self.grads[tile.array], self.sums[index]
        if stage <= 1:
            pair = remote(
                grad.at[:, :, :, 1 - at["c"], rows, cols],
                self.pairs[index].at[group],
                self.core_send.at[slot],
                self.core_recv.at[slot],
                across(at, ("c", 0)),
            )
            own = pltpu.make_async_copy(
                grad.at[:, :, :, at["c"], rows, cols], sums.at[group], self.own_sem.at[slot]
            )
        if stage == 0:
            pair.start()
            own.start()
            return
        if stage == 1:
            own.wait()
            pair.wait()
            sums[group] = (
                sums[group].astype(F32) + self.pairs[index][group].astype(F32)
            ).astype(sums.dtype)
        lag = DEPTH + 1 - stage
        for off in offsets(lag):
            dest = moved(at, off)

            def handle():
                spot = (group, dest["y"], dest["z"], dest["x"])

                def add(links):
                    total = sums[spot].astype(F32)
                    for link in links:
                        self.copy(index, group, slot, dest, link, link).wait_recv()
                        box = inbox_id(tile.order, link, dest)
                        total = total + self.inbox[index][group, LINKS.index(link), box].astype(F32)
                    return total

                fixed = [link for link in onward(tile.order, off) if link[0] != "z"]
                for link in onward(tile.order, off):
                    if link[0] == "z":

                        @pl.when(inside(at["z"] + link[1]))
                        def _():
                            sums[spot] = add([link]).astype(sums.dtype)

                if lag == 0:
                    self.put(tile, group, add(fixed))
                    return
                if fixed:
                    sums[spot] = add(fixed).astype(sums.dtype)
                link = backward_link(tile.order, off)
                one = self.copy(index, group, slot, dest, link, (link[0], -link[1]))
                pl.when(group >= 2)(one.wait_send)
                one.start()

            when(inside(dest["z"]) if off[0] else None, handle)

    def step(self, step):
        for stage in range(LAGS):
            for index, (tile, first) in enumerate(zip(self.tiles, first_slots(self.tiles))):
                group = step - stage - tile.start
                pl.when((group >= 0) & (group < tile.count))(
                    functools.partial(self.visit, index, group, first + group, stage)
                )

    def finish(self):
        for index, tile in enumerate(self.tiles):
            for group in range(max(0, tile.count - 2), tile.count):
                for off in [off for lag in range(1, DEPTH + 1) for off in offsets(lag)]:
                    dest = moved(self.at, off)
                    link = backward_link(tile.order, off)
                    one = self.copy(index, group, 0, dest, link, (link[0], -link[1]))
                    when(inside(dest["z"]) if off[0] else None, one.wait_send)


def run_all(moves):
    moves.begin()
    lax.fori_loop(0, moves.steps, lambda step, _: (moves.step(step), 0)[1], 0)
    moves.finish()


def gather_kernel(tiles, arrays, *refs):
    run_all(Gather(tiles, refs[:arrays], refs[arrays : 2 * arrays], refs[2 * arrays :]))


def gather(shards, tiles, ident):
    halves = lax.axis_size("tensor")
    if not on_grid():
        return [
            lax.all_gather(shard, ("tensor", "dp"), axis=0, tiled=False).reshape(
                (halves, -1) + shard.shape[1:]
            )
            for shard in shards
        ]
    hbm = pl.BlockSpec(memory_space=pl.ANY)
    arrays = len(shards)
    fulls = pl.pallas_call(
        functools.partial(gather_kernel, tiles, arrays),
        in_specs=[hbm] * arrays,
        out_specs=[hbm] * arrays,
        out_shape=[
            jax.ShapeDtypeStruct((halves,) + GRID + shard.shape, shard.dtype) for shard in shards
        ],
        scratch_shapes=Gather.sems(tiles, arrays),
        compiler_params=pltpu.CompilerParams(collective_id=ident, has_side_effects=True),
        name="gather",
    )(*shards)
    return [full.reshape(halves, -1, full.shape[-1]) for full in fulls]


def scatter_kernel(tiles, groups, *refs):
    boxes = 3 * len(tiles)
    grads, outs, rest = refs[:3], refs[3:11], refs[11:]
    gate, upper, down, out, query, key, value, small = outs

    def put(tile, group, total):
        rows = pl.ds(tile.row, tile.rows)
        if tile.array == 2:
            small[...] = total
            return
        if tile.count == 1 and tile.array == 0:
            out[rows, 3 * WIDTH :] = total
            return
        thirds = (gate, upper, down) if tile.array == 0 else (query, key, value)
        offset = tile.col // WIDTH
        width = tile.cols // WIDTH

        def inner():
            lanes = pl.ds(pl.multiple_of(group * WIDTH, WIDTH), WIDTH)
            for i in range(width):
                thirds[offset + i][rows, lanes] = total[:, i * WIDTH : (i + 1) * WIDTH]

        if tile.array == 1:
            inner()
            return
        pl.when(group < groups)(inner)

        @pl.when(group == groups)
        def _():
            out[rows, tile.col : tile.col + tile.cols] = total

    run_all(Scatter(tiles, grads, put, rest[:boxes], rest[boxes:]))


def scatter(second, first, small, ident):
    halves = lax.axis_size("tensor")
    parts = lax.axis_size("dp")
    rows = second.shape[1] // parts
    groups = second.shape[2] // (3 * WIDTH) - 1
    half_cols = second.shape[2] - groups * 3 * WIDTH
    if not on_grid():
        second, first, small = (
            lax.psum_scatter(
                grad.reshape(-1, grad.shape[-1]), ("tensor", "dp"), scatter_dimension=0, tiled=True
            ).astype(F32)
            for grad in (second, first, small)
        )
        return (
            thirds_of(second[:, : groups * 3 * WIDTH])
            + (second[:, groups * 3 * WIDTH :],)
            + thirds_of(first)
            + (small,)
        )
    grads = [grad.reshape((2,) + GRID + (-1, grad.shape[-1])) for grad in (second, first, small)]
    tiles = split_tiles(second.shape[2], rows)
    tiles += split_tiles(first.shape[2], rows, array=1, start=tiles[0].count)
    small_rows = grads[2].shape[-2]
    tiles.append(Tiles(2, "zxy", 0, small_rows, 0, WIDTH, WIDTH, 1, 0))
    hbm = pl.BlockSpec(memory_space=pl.ANY)
    shapes = [(rows, groups * WIDTH)] * 3 + [(rows, half_cols)]
    shapes += [(rows, first.shape[2] // 3)] * 3 + [(small_rows, WIDTH)]
    return pl.pallas_call(
        functools.partial(scatter_kernel, tiles, groups),
        in_specs=[hbm] * 3,
        out_specs=[pl.BlockSpec(memory_space=pltpu.VMEM)] * len(shapes),
        out_shape=[jax.ShapeDtypeStruct(shape, F32) for shape in shapes],
        scratch_shapes=Scatter.boxes(tiles, [grad.dtype for grad in grads]) + Scatter.sems(tiles),
        compiler_params=pltpu.CompilerParams(
            collective_id=ident, has_side_effects=True, vmem_limit_bytes=VMEM_LIMIT
        ),
        name="scatter",
    )(*grads)


def contract(left, right, dim_left, dim_right):
    return lax.dot_general(
        left.astype(BF16),
        right.astype(BF16),
        (((dim_left,), (dim_right,)), ((), ())),
        preferred_element_type=F32,
    )


def mm(left, right):
    return contract(left, right, 1, 0)


def mm_t(left, right):
    return contract(left, right, 1, 1)


def t_mm(left, right):
    return contract(left, right, 0, 0)


def tri_inverses(systems):
    rows = lax.broadcasted_iota(jnp.int32, (CHUNK, CHUNK), 0)
    cols = lax.broadcasted_iota(jnp.int32, (CHUNK, CHUNK), 1)
    inverses = None
    size = 1
    while size < CHUNK:
        link = (
            (rows // (2 * size) == cols // (2 * size))
            & ((rows // size) % 2 == 1)
            & ((cols // size) % 2 == 0)
        )
        parts = [jnp.where(link, system, 0.0) for system in systems]
        if size == 1:
            eye = (rows == cols).astype(F32)
            inverses = [eye - part for part in parts]
        else:
            lows = [inverse.astype(BF16) for inverse in inverses]
            middles = [mm(part, low) for part, low in zip(parts, lows)]
            inverses = [
                inverse - mm(low, middle)
                for inverse, low, middle in zip(inverses, lows, middles)
            ]
        size *= 2
    return inverses


def conv_of(lin_ref, base, lanes, taps, row, keeps, tokens):
    total = lin_ref[0, base : base + tokens, lanes] * taps[row : row + 1]
    for off in range(1, TAPS):
        total = total + taps[row + off : row + off + 1] * (
            lin_ref[0, base - off : base - off + tokens, lanes] * keeps[off]
        )
    return total


def third(sub, index):
    first = (sub * 3 + index) * WIDTH
    return slice(first, first + WIDTH)


def head_column(aux, lane):
    lanes = lax.broadcasted_iota(jnp.int32, aux.shape, 1)
    return jnp.sum(jnp.where(lanes == lane, aux, 0.0), axis=1, keepdims=True)


def greet(partner):
    barrier = pltpu.get_barrier_semaphore()
    pl.semaphore_signal(
        barrier, inc=1, device_id={"tensor": partner}, device_id_type=MESH
    )
    pl.semaphore_wait(barrier, 1)


def chunk_masks(aux, seg_row, at):
    rows = lax.broadcasted_iota(jnp.int32, (CHUNK, CHUNK), 0)
    cols = lax.broadcasted_iota(jnp.int32, (CHUNK, CHUNK), 1)
    same = aux[at : at + CHUNK, 0:1] == seg_row[0:1, at : at + CHUNK]
    return same & (rows > cols), same & (rows >= cols)


def mixer_fwd_kernel(
    tokens, lin_ref, aux_ref, seg_ref, taps_ref, gain_ref,
    onb_ref, o_ref, n_ref, t_ref, s_ref,
    state, outbox, inbox, send_sem, recv_sem,
):
    step = pl.program_id(0)
    mine = lax.axis_index("tensor")
    chunks = tokens // CHUNK

    @pl.when(step == 0)
    def _():
        greet(1 - mine)

    def hand_over(head):
        return pltpu.make_async_remote_copy(
            src_ref=outbox.at[head],
            dst_ref=inbox.at[head],
            send_sem=send_sem.at[head],
            recv_sem=recv_sem.at[head],
            device_id={"tensor": 1 - mine},
            device_id_type=MESH,
        )

    aux = aux_ref[...]
    seg_row = seg_ref[...]
    keeps = [None] + [aux[:, 2 + off : 3 + off] for off in range(1, TAPS)]
    heads = []
    for sub in range(PAIR):
        lanes = slice(sub * WIDTH, (sub + 1) * WIDTH)
        taps = taps_ref[:, lanes]
        beta = head_column(aux, 16 + step * PAIR + sub)
        acts = []
        for index in range(3):
            mixed = conv_of(lin_ref, HALO, third(sub, index), taps, index * TAPS, keeps, tokens)
            acts.append(mixed * jax.nn.sigmoid(mixed))
        q = acts[0] * (
            lax.rsqrt(jnp.sum(acts[0] * acts[0], -1, keepdims=True) + 1e-06) * WIDTH ** (-0.5)
        )
        k = acts[1] * lax.rsqrt(jnp.sum(acts[1] * acts[1], -1, keepdims=True) + 1e-06)
        heads.append((q, k, acts[2], beta))
    spots = [(sub, c) for sub in range(PAIR) for c in range(chunks)]
    masks = [chunk_masks(aux, seg_row, c * CHUNK) for c in range(chunks)]

    def cut(values, c):
        return values[c * CHUNK : (c + 1) * CHUNK]

    lows = [(q.astype(BF16), k.astype(BF16)) for q, k, _, _ in heads]
    systems = [
        jnp.where(
            masks[c][0],
            cut(heads[sub][3], c) * mm_t(cut(lows[sub][1], c), cut(lows[sub][1], c)),
            0.0,
        )
        for sub, c in spots
    ]
    scores_of = [
        jnp.where(masks[c][1], mm_t(cut(lows[sub][0], c), cut(lows[sub][1], c)), 0.0).astype(BF16)
        for sub, c in spots
    ]
    inner = []
    for (sub, c), inverse, scores in zip(spots, tri_inverses(systems), scores_of):
        inverse = inverse.astype(BF16)
        t_ref[sub, c] = inverse
        inner.append((inverse, scores))

    @pl.when(mine == 0)
    def _():
        state[...] = jnp.zeros_like(state)

    @pl.when(mine == 1)
    def _():
        for sub in range(PAIR):
            head = step * PAIR + sub
            hand_over(head).wait_recv()
            state[sub] = inbox[head]

    carried = [state[sub] for sub in range(PAIR)]
    for c in range(chunks):
        at = c * CHUNK
        first = aux[at : at + CHUNK, 1:2]
        last = aux[at : at + CHUNK, 2:3]
        keep = aux[at + CHUNK - 1 : at + CHUNK, 1:2]
        subs = range(PAIR)
        befores = [carried[sub].astype(BF16) for sub in subs]
        reads = [
            mm(jnp.concatenate([cut(lows[sub][1], c), cut(lows[sub][0], c)], 0), befores[sub])
            for sub in subs
        ]
        news = [
            mm(
                inner[sub * chunks + c][0],
                cut(heads[sub][3], c) * (cut(heads[sub][2], c) - first * reads[sub][:CHUNK]),
            ).astype(BF16)
            for sub in subs
        ]
        carried = [
            keep * carried[sub] + t_mm(last * cut(heads[sub][1], c), news[sub]) for sub in subs
        ]
        outs = [
            first * reads[sub][CHUNK:] + mm(inner[sub * chunks + c][1], news[sub]) for sub in subs
        ]
        for sub in subs:
            s_ref[sub, c] = befores[sub]
            n_ref[sub, c] = news[sub]
            lanes = slice(sub * WIDTH, (sub + 1) * WIDTH)
            out = outs[sub]
            o_ref[0, at : at + CHUNK, lanes] = out
            scale = lax.rsqrt(jnp.mean(out * out, -1, keepdims=True) + 1e-05)
            onb_ref[0, at : at + CHUNK, lanes] = (out * scale * gain_ref[0:1]).astype(BF16)

    @pl.when(mine == 0)
    def _():
        for sub in range(PAIR):
            head = step * PAIR + sub
            outbox[head] = carried[sub]
            hand_over(head).start()

    @pl.when((step == pl.num_programs(0) - 1) & (mine == 0))
    def _():
        for head in range(outbox.shape[0]):
            hand_over(head).wait_send()


def mixer_bwd_kernel(
    tokens, lin_ref, aux_ref, seg_ref, taps_ref, gain_ref,
    o_ref, n_ref, t_ref, s_ref, donb_ref,
    dlin_ref, dbl_ref, dtaps_ref, dgain_ref,
    state, extended, outbox, inbox, tailbox, headbox, send_sem, recv_sem, tail_send, tail_recv,
):
    step = pl.program_id(0)
    mine = lax.axis_index("tensor")
    chunks = tokens // CHUNK

    @pl.when(step == 0)
    def _():
        greet(1 - mine)
        dbl_ref[...] = jnp.zeros_like(dbl_ref)
        dgain_ref[...] = jnp.zeros_like(dgain_ref)

    def hand_over(head):
        return pltpu.make_async_remote_copy(
            src_ref=outbox.at[head],
            dst_ref=inbox.at[head],
            send_sem=send_sem.at[head],
            recv_sem=recv_sem.at[head],
            device_id={"tensor": 1 - mine},
            device_id_type=MESH,
        )

    def hand_tail(head):
        return pltpu.make_async_remote_copy(
            src_ref=tailbox.at[head],
            dst_ref=headbox.at[head],
            send_sem=tail_send.at[head],
            recv_sem=tail_recv.at[head],
            device_id={"tensor": 1 - mine},
            device_id_type=MESH,
        )

    aux = aux_ref[...]
    seg_row = seg_ref[...]
    keeps = [None] + [aux[:tokens, 2 + off : 3 + off] for off in range(1, TAPS)]
    heads, inner = [], []
    for sub in range(PAIR):
        lanes = slice(sub * WIDTH, (sub + 1) * WIDTH)
        taps = taps_ref[:, lanes]
        beta = head_column(aux[:tokens], 16 + step * PAIR + sub)
        mixes, sigs, acts = [], [], []
        for index in range(3):
            mixed = conv_of(lin_ref, HALO, third(sub, index), taps, index * TAPS, keeps, tokens)
            mixes.append(mixed)
            sigs.append(jax.nn.sigmoid(mixed))
            acts.append(mixed * sigs[-1])
        rho_q = lax.rsqrt(jnp.sum(acts[0] * acts[0], -1, keepdims=True) + 1e-06)
        rho_k = lax.rsqrt(jnp.sum(acts[1] * acts[1], -1, keepdims=True) + 1e-06)
        q = acts[0] * (rho_q * WIDTH ** (-0.5))
        k = acts[1] * rho_k
        out = o_ref[0, :, lanes]
        don = donb_ref[0, :, lanes]
        scale = lax.rsqrt(jnp.mean(out * out, -1, keepdims=True) + 1e-05)
        dgain_ref[0:1] += jnp.sum(don * out * scale, 0, keepdims=True)
        du = don * gain_ref[0:1]
        dout = scale * du - out * (scale * scale * scale) * jnp.mean(
            out * du, -1, keepdims=True
        )
        heads.append((q, k, acts, beta, mixes, sigs, rho_q, rho_k, dout))
    spots = [(sub, c) for sub in range(PAIR) for c in range(chunks)]
    masks = [chunk_masks(aux, seg_row, c * CHUNK) for c in range(chunks)]
    firsts = [aux[c * CHUNK : (c + 1) * CHUNK, 1:2] for c in range(chunks)]

    def cut(values, c):
        return values[c * CHUNK : (c + 1) * CHUNK]

    lows = [
        (q.astype(BF16), k.astype(BF16), dout.astype(BF16))
        for q, k, _, _, _, _, _, _, dout in heads
    ]
    grams = [
        mm_t(jnp.concatenate([cut(lows[s][1], c), cut(lows[s][0], c)], 0), cut(lows[s][1], c))
        for s, c in spots
    ]
    turned = [
        mm_t(cut(lows[s][2], c), jnp.concatenate([n_ref[s, c], s_ref[s, c]], 0)) for s, c in spots
    ]
    scores_of = [
        jnp.where(masks[c][1], gram[CHUNK:], 0.0).astype(BF16)
        for (s, c), gram in zip(spots, grams)
    ]
    dscores_of = [
        jnp.where(masks[c][1], turn[:, :CHUNK], 0.0).astype(BF16)
        for (s, c), turn in zip(spots, turned)
    ]
    reads = [mm(cut(lows[s][1], c), s_ref[s, c]) for s, c in spots]
    pulls = [t_mm(scores, cut(lows[s][2], c)) for (s, c), scores in zip(spots, scores_of)]
    reaches = [
        t_mm(firsts[c] * cut(heads[s][0], c), cut(lows[s][2], c)) for s, c in spots
    ]
    dqs = [
        firsts[c] * turn[:, CHUNK:] + mm(dscores, cut(lows[s][1], c))
        for (s, c), turn, dscores in zip(spots, turned, dscores_of)
    ]
    dks = [t_mm(dscores, cut(lows[s][0], c)) for (s, c), dscores in zip(spots, dscores_of)]
    gaps = [
        cut(heads[s][2][2], c) - firsts[c] * read for (s, c), read in zip(spots, reads)
    ]
    inner = [
        (gram[:CHUNK], masks[c][0], pull, reach, dq, dk, gap)
        for (s, c), gram, pull, reach, dq, dk, gap in zip(
            spots, grams, pulls, reaches, dqs, dks, gaps
        )
    ]

    @pl.when(mine == 1)
    def _():
        state[...] = jnp.zeros_like(state)

    @pl.when(mine == 0)
    def _():
        for sub in range(PAIR):
            head = step * PAIR + sub
            hand_over(head).wait_recv()
            state[sub] = inbox[head]

    carried = [state[sub] for sub in range(PAIR)]
    pieces = [[None] * chunks for _ in range(PAIR)]
    for c in reversed(range(chunks)):
        at = c * CHUNK
        first = aux[at : at + CHUNK, 1:2]
        last = aux[at : at + CHUNK, 2:3]
        keep = aux[at + CHUNK - 1 : at + CHUNK, 1:2]
        subs = range(PAIR)
        parts = [inner[sub * chunks + c] for sub in subs]
        betas = [cut(heads[sub][3], c) for sub in subs]
        afters = [carried[sub].astype(BF16) for sub in subs]
        dnews = [
            parts[sub][2] + mm(last * cut(heads[sub][1], c), afters[sub]) for sub in subs
        ]
        backs = [t_mm(t_ref[sub, c], dnews[sub]) for sub in subs]
        dvs = [betas[sub] * backs[sub] for sub in subs]
        dreads = [(-(first * dvs[sub])).astype(BF16) for sub in subs]
        carried = [
            keep * carried[sub] + parts[sub][3] + t_mm(cut(lows[sub][1], c), dreads[sub])
            for sub in subs
        ]
        for sub in subs:
            kk, strict, _, _, dq, dk, gap = parts[sub]
            before, new = s_ref[sub, c], n_ref[sub, c]
            kc = cut(lows[sub][1], c)
            back = backs[sub]
            dsystem = jnp.where(strict, -mm_t(back, new), 0.0)
            dbeta = jnp.sum(back * gap + dsystem * kk, -1, keepdims=True)
            grow = (betas[sub] * dsystem).astype(BF16)
            dk = (
                dk
                + last * mm_t(new, afters[sub])
                + mm_t(dreads[sub], before)
                + mm(grow, kc)
                + t_mm(grow, kc)
            )
            pieces[sub][c] = (dq, dk, dvs[sub], dbeta)

    @pl.when(mine == 1)
    def _():
        for sub in range(PAIR):
            head = step * PAIR + sub
            outbox[head] = carried[sub]
            hand_over(head).start()

    lane_ids = lax.broadcasted_iota(jnp.int32, (tokens, WIDTH), 1)
    for sub in range(PAIR):
        head = step * PAIR + sub
        q, k, acts, beta, mixes, sigs, rho_q, rho_k, dout = heads[sub]
        dq, dk, dv, dbeta = (
            jnp.concatenate([pieces[sub][c][item] for c in range(chunks)], 0)
            for item in range(4)
        )
        dbl_ref[...] += jnp.where(lane_ids == head, dbeta * beta * (1.0 - beta), 0.0)
        dq = dq * WIDTH ** (-0.5)
        dacts = (
            rho_q * dq
            - acts[0] * (rho_q * rho_q * rho_q) * jnp.sum(acts[0] * dq, -1, keepdims=True),
            rho_k * dk
            - acts[1] * (rho_k * rho_k * rho_k) * jnp.sum(acts[1] * dk, -1, keepdims=True),
            dv,
        )
        for index in range(3):
            sig = sigs[index]
            dmix = dacts[index] * sig * (1.0 + mixes[index] * (1.0 - sig))
            extended[sub, index, 0:tokens] = dmix
            tailbox[head, index] = dmix[0:8]

    @pl.when(mine == 1)
    def _():
        extended[:, :, tokens : tokens + 8] = jnp.zeros((PAIR, 3, 8, WIDTH), F32)
        for sub in range(PAIR):
            hand_tail(step * PAIR + sub).start()

    @pl.when(mine == 0)
    def _():
        for sub in range(PAIR):
            head = step * PAIR + sub
            hand_tail(head).wait_recv()
            extended[sub, :, tokens : tokens + 8] = headbox[head]

    later = [None] + [aux[:, 5 + off : 6 + off] for off in range(1, TAPS)]
    for sub in range(PAIR):
        lanes = slice(sub * WIDTH, (sub + 1) * WIDTH)
        taps = taps_ref[:, lanes]
        for index in range(3):
            row = index * TAPS
            dmix = extended[sub, index, 0:tokens]
            dlin = dmix * taps[row : row + 1]
            dtaps_ref[row : row + 1, lanes] = jnp.sum(
                dmix * lin_ref[0, HALO : HALO + tokens, third(sub, index)], 0, keepdims=True
            )
            for off in range(1, TAPS):
                dlin = dlin + taps[row + off : row + off + 1] * (
                    extended[sub, index, off : off + tokens] * later[off]
                )
                dtaps_ref[row + off : row + off + 1, lanes] = jnp.sum(
                    dmix
                    * keeps[off]
                    * lin_ref[0, HALO - off : HALO - off + tokens, third(sub, index)],
                    0,
                    keepdims=True,
                )
            dlin_ref[0, :, third(sub, index)] = dlin.astype(BF16)
        dtaps_ref[12:16, lanes] = jnp.zeros((4, WIDTH), F32)

    @pl.when((step == pl.num_programs(0) - 1) & (mine == 1))
    def _():
        for head in range(outbox.shape[0]):
            hand_over(head).wait_send()
            hand_tail(head).wait_send()


def mixer_fwd(linear, aux, seg_row, taps, gain):
    halves, rows, cols = linear.shape
    tokens = rows - HALO
    half_heads = cols // 3 // WIDTH
    heads = halves * half_heads
    per_half = half_heads // PAIR
    chunks = tokens // CHUNK
    lanes = PAIR * WIDTH

    def whole(shape):
        return pl.BlockSpec(shape, lambda i: (0,) * len(shape))

    token_spec = pl.BlockSpec((1, tokens, lanes), lambda i: (i // per_half, 0, i % per_half))
    square = pl.BlockSpec((PAIR, chunks, CHUNK, WIDTH), lambda i: (i, 0, 0, 0))
    square_shape = jax.ShapeDtypeStruct((heads, chunks, CHUNK, WIDTH), BF16)
    return pl.pallas_call(
        functools.partial(mixer_fwd_kernel, tokens),
        grid=(heads // PAIR,),
        in_specs=[
            pl.BlockSpec((1, rows, 3 * lanes), lambda i: (i // per_half, 0, i % per_half)),
            whole(aux.shape),
            whole(seg_row.shape),
            pl.BlockSpec((16, lanes), lambda i: (0, i)),
            whole(gain.shape),
        ],
        out_specs=[token_spec, token_spec, square, square, square],
        out_shape=[
            jax.ShapeDtypeStruct((halves, tokens, half_heads * WIDTH), BF16),
            jax.ShapeDtypeStruct((halves, tokens, half_heads * WIDTH), F32),
            square_shape,
            square_shape,
            square_shape,
        ],
        scratch_shapes=[
            pltpu.VMEM((PAIR, WIDTH, WIDTH), F32),
            pltpu.VMEM((heads, WIDTH, WIDTH), F32),
            pltpu.VMEM((heads, WIDTH, WIDTH), F32),
            pltpu.SemaphoreType.DMA((heads,)),
            pltpu.SemaphoreType.DMA((heads,)),
        ],
        compiler_params=pltpu.CompilerParams(
            collective_id=0, has_side_effects=True, vmem_limit_bytes=VMEM_LIMIT
        ),
        name="mixer_fwd",
    )(linear, aux, seg_row, taps, gain)


def mixer_bwd(linear, aux, seg_row, taps, gain, out, new, inverse, before, donb):
    halves, rows, cols = linear.shape
    tokens = rows - HALO
    half_heads = cols // 3 // WIDTH
    heads = halves * half_heads
    per_half = half_heads // PAIR
    chunks = tokens // CHUNK
    lanes = PAIR * WIDTH

    def whole(shape):
        return pl.BlockSpec(shape, lambda i: (0,) * len(shape))

    token_spec = pl.BlockSpec((1, tokens, lanes), lambda i: (i // per_half, 0, i % per_half))
    square = pl.BlockSpec((PAIR, chunks, CHUNK, WIDTH), lambda i: (i, 0, 0, 0))
    taps_spec = pl.BlockSpec((16, lanes), lambda i: (0, i))
    return pl.pallas_call(
        functools.partial(mixer_bwd_kernel, tokens),
        grid=(heads // PAIR,),
        in_specs=[
            pl.BlockSpec((1, rows, 3 * lanes), lambda i: (i // per_half, 0, i % per_half)),
            whole(aux.shape),
            whole(seg_row.shape),
            taps_spec,
            whole(gain.shape),
            token_spec,
            square,
            square,
            square,
            token_spec,
        ],
        out_specs=[
            pl.BlockSpec((1, tokens, 3 * lanes), lambda i: (i // per_half, 0, i % per_half)),
            whole((tokens, WIDTH)),
            taps_spec,
            whole((8, WIDTH)),
        ],
        out_shape=[
            jax.ShapeDtypeStruct((halves, tokens, cols), BF16),
            jax.ShapeDtypeStruct((tokens, WIDTH), F32),
            jax.ShapeDtypeStruct((16, heads * WIDTH), F32),
            jax.ShapeDtypeStruct((8, WIDTH), F32),
        ],
        scratch_shapes=[
            pltpu.VMEM((PAIR, WIDTH, WIDTH), F32),
            pltpu.VMEM((PAIR, 3, tokens + 8, WIDTH), F32),
            pltpu.VMEM((heads, WIDTH, WIDTH), F32),
            pltpu.VMEM((heads, WIDTH, WIDTH), F32),
            pltpu.VMEM((heads, 3, 8, WIDTH), F32),
            pltpu.VMEM((heads, 3, 8, WIDTH), F32),
            pltpu.SemaphoreType.DMA((heads,)),
            pltpu.SemaphoreType.DMA((heads,)),
            pltpu.SemaphoreType.DMA((heads,)),
            pltpu.SemaphoreType.DMA((heads,)),
        ],
        compiler_params=pltpu.CompilerParams(
            collective_id=1, has_side_effects=True, vmem_limit_bytes=VMEM_LIMIT
        ),
        name="mixer_bwd",
    )(linear, aux, seg_row, taps, gain, out, new, inverse, before, donb)


def mlp_kernel(
    count, inputs_ref, onb_ref, weight_ref, *refs,
):
    wo_refs, refs = refs[:4], refs[4:]
    gain_ref, mask_ref, teacher_ref, cot_ref, coef_ref = refs[:5]
    out_ref, square_ref, early_ref, grad_ref, donb_ref, dhidden_ref, dgain_ref = refs[5:12]
    hidden, normed, normed_t, total, dtotal, dmlp, dmlp_t, gates, uppers, inners = refs[12:]
    step = pl.program_id(0)
    unit = WIDTH

    def out_weight(half):
        return jnp.concatenate([ref[half] for ref in wo_refs], 1)

    def rho_of(values):
        return lax.rsqrt(jnp.mean(values * values, -1, keepdims=True) + 1e-05)

    def spans(first, parts):
        return [weight_ref[half, :, (first + part) * unit : (first + part + 1) * unit]
                for half in range(2) for part in range(parts)]

    @pl.when(step == 0)
    def _():
        rows = inputs_ref[...].astype(F32)
        for half in range(2):
            rows = rows + mm_t(onb_ref[half], out_weight(half))
        hidden[...] = rows
        xn = rows * rho_of(rows) * gain_ref[0:1]
        normed[...] = xn.astype(BF16)
        normed_t[...] = xn.T.astype(BF16)
        total[...] = jnp.zeros_like(total)

    @pl.when(step < count)
    def _():
        both_w = jnp.concatenate(spans(0, 2), 1)
        gu = mm(normed[...], both_w)
        gate = jnp.concatenate([gu[:, 0:unit], gu[:, 2 * unit : 3 * unit]], 1)
        upper = jnp.concatenate([gu[:, unit : 2 * unit], gu[:, 3 * unit :]], 1)
        gates[step] = gate
        uppers[step] = upper
        inner = (gate * jax.nn.sigmoid(gate) * upper).astype(BF16)
        inners[step] = inner
        total[...] += mm_t(inner, jnp.concatenate(spans(2, 1), 1))

    @pl.when(step == count - 1)
    def _():
        rows = hidden[...] + total[...]
        out_ref[...] = rows.astype(BF16)
        differ = rows - teacher_ref[...].astype(F32)
        masked = mask_ref[...] * differ
        square_ref[...] = jnp.sum(
            (masked * differ).reshape(-1, 8, rows.shape[1]), 0
        )
        dout = cot_ref[...].astype(F32) + masked * coef_ref[0:1, 0:1]
        dhidden_ref[...] = dout
        dmlp[...] = dout.astype(BF16)
        dmlp_t[...] = dout.T.astype(BF16)
        dtotal[...] = jnp.zeros_like(dtotal)

    @pl.when((step >= count) & (step < 2 * count))
    def _():
        tile = step - count
        dinner = mm(dmlp[...], jnp.concatenate(spans(2, 1), 1))
        gate, upper = gates[tile], uppers[tile]
        sig = jax.nn.sigmoid(gate)
        dgate = (dinner * upper * sig * (1.0 + gate * (1.0 - sig))).astype(BF16)
        dupper = (dinner * (gate * sig)).astype(BF16)
        dgu = jnp.concatenate(
            [dgate[:, :unit], dupper[:, :unit], dgate[:, unit:], dupper[:, unit:]], 1
        )
        dtotal[...] += mm_t(dgu, jnp.concatenate(spans(0, 2), 1))
        grown = mm(normed_t[...], dgu).astype(BF16)
        down = mm(dmlp_t[...], inners[tile]).astype(BF16)

        def put(ref):
            for half in range(2):
                ref[half, :, 0 : 2 * unit] = grown[:, half * 2 * unit : (half + 1) * 2 * unit]
                ref[half, :, 2 * unit :] = down[:, half * unit : (half + 1) * unit]

        pl.when(tile < EARLY)(functools.partial(put, early_ref))
        pl.when(tile >= EARLY)(functools.partial(put, grad_ref))

    @pl.when(step == 2 * count)
    def _():
        rows = hidden[...]
        rho = rho_of(rows)
        unit_rows = rows * rho
        drows = dtotal[...]
        du = drows * gain_ref[0:1]
        dgain_ref[...] = jnp.sum((drows * unit_rows).reshape(-1, 8, rows.shape[1]), 0)
        dh = dhidden_ref[...] + rho * (du - unit_rows * jnp.mean(du * unit_rows, -1, keepdims=True))
        dhidden_ref[...] = dh
        dattn = dh.astype(BF16)
        dmlp_t[...] = dh.T.astype(BF16)
        for half in range(2):
            donb_ref[half] = mm(dattn, out_weight(half))
            grad_ref[half] = mm(dmlp_t[...], onb_ref[half, :, 0 : 3 * unit]).astype(BF16)

    @pl.when(step == 2 * count + 1)
    def _():
        for half in range(2):
            grad_ref[half, :, 0:unit] = mm(dmlp_t[...], onb_ref[half, :, 3 * unit :]).astype(BF16)


def mlp(inputs, onb, weights, gain, mask, teacher, cotangent, coef):
    tokens, width_d = inputs.shape
    halves, _, cols = weights.shape
    half_cols = onb.shape[2]
    count = (cols - half_cols) // (3 * WIDTH)
    first_out = count * 3

    def whole(shape):
        return pl.BlockSpec(shape, lambda i: (0,) * len(shape))

    def tile(i):
        return (0, 0, jnp.where(i < count, i, jnp.minimum(i - count, count - 1)))

    wide = (halves, width_d, 3 * WIDTH)
    return pl.pallas_call(
        functools.partial(mlp_kernel, count),
        grid=(2 * count + 2,),
        in_specs=[whole(inputs.shape), whole(onb.shape), pl.BlockSpec(wide, tile)]
        + [
            pl.BlockSpec((halves, width_d, WIDTH), functools.partial(lambda n, i: (0, 0, n), first_out + n))
            for n in range(4)
        ]
        + [whole(gain.shape), whole(mask.shape), whole(teacher.shape), whole(cotangent.shape), whole(coef.shape)],
        out_specs=[
            whole((tokens, width_d)),
            whole((8, width_d)),
            pl.BlockSpec(wide, lambda i: (0, 0, jnp.clip(i - count, 0, EARLY - 1))),
            pl.BlockSpec(wide, lambda i: (0, 0, jnp.maximum(i - count - EARLY, 0))),
            whole((halves, tokens, half_cols)),
            whole((tokens, width_d)),
            whole((8, width_d)),
        ],
        out_shape=[
            jax.ShapeDtypeStruct((tokens, width_d), BF16),
            jax.ShapeDtypeStruct((8, width_d), F32),
            jax.ShapeDtypeStruct((halves, width_d, EARLY * 3 * WIDTH), BF16),
            jax.ShapeDtypeStruct((halves, width_d, cols - EARLY * 3 * WIDTH), BF16),
            jax.ShapeDtypeStruct((halves, tokens, half_cols), F32),
            jax.ShapeDtypeStruct((tokens, width_d), F32),
            jax.ShapeDtypeStruct((8, width_d), F32),
        ],
        scratch_shapes=[
            pltpu.VMEM((tokens, width_d), F32),
            pltpu.VMEM((tokens, width_d), BF16),
            pltpu.VMEM((width_d, tokens), BF16),
            pltpu.VMEM((tokens, width_d), F32),
            pltpu.VMEM((tokens, width_d), F32),
            pltpu.VMEM((tokens, width_d), BF16),
            pltpu.VMEM((width_d, tokens), BF16),
            pltpu.VMEM((count, tokens, 2 * WIDTH), F32),
            pltpu.VMEM((count, tokens, 2 * WIDTH), F32),
            pltpu.VMEM((count, tokens, 2 * WIDTH), BF16),
        ],
        compiler_params=pltpu.CompilerParams(vmem_limit_bytes=VMEM_LIMIT),
        name="mlp",
    )(inputs, onb, weights, weights, weights, weights, weights, gain, mask, teacher, cotangent, coef)


def project_back_kernel(
    dlin_ref, weight_ref, inputs_ref, gain_ref, dbl_ref, beta_ref, dhidden_ref,
    grad_ref, dinput_ref, dgain_ref, dbeta_ref,
    normed_t, total,
):
    step = pl.program_id(0)

    def unit():
        rows = inputs_ref[...].astype(F32)
        rho = lax.rsqrt(jnp.mean(rows * rows, -1, keepdims=True) + 1e-05)
        return rows * rho, rho

    @pl.when(step == 0)
    def _():
        normed_t[...] = (unit()[0] * gain_ref[0:1]).T.astype(BF16)
        dbl = dbl_ref[...].astype(BF16)
        total[...] = mm_t(dbl, beta_ref[...])
        dbeta_ref[...] = mm(normed_t[...], dbl)

    total[...] += mm_t(dlin_ref[0], weight_ref[0])
    grad_ref[0] = mm(normed_t[...], dlin_ref[0]).astype(BF16)

    @pl.when(step == pl.num_programs(0) - 1)
    def _():
        rows, rho = unit()
        drows = total[...]
        du = drows * gain_ref[0:1]
        dgain_ref[...] = jnp.sum((drows * rows).reshape(-1, 8, rows.shape[1]), 0)
        dinput_ref[...] = dhidden_ref[...] + rho * (
            du - rows * jnp.mean(du * rows, -1, keepdims=True)
        )


def project_back(dlin, weights, inputs, gain, dbl, beta_w, dhidden):
    halves, tokens, cols = dlin.shape
    width_d = inputs.shape[1]
    kinds = 2
    part = cols // kinds

    def whole(shape):
        return pl.BlockSpec(shape, lambda i: (0,) * len(shape))

    columns = pl.BlockSpec((1, width_d, part), lambda i: (i // kinds, 0, i % kinds))
    return pl.pallas_call(
        project_back_kernel,
        grid=(halves * kinds,),
        in_specs=[
            pl.BlockSpec((1, tokens, part), lambda i: (i // kinds, 0, i % kinds)),
            columns,
            whole(inputs.shape),
            whole(gain.shape),
            whole(dbl.shape),
            whole(beta_w.shape),
            whole(dhidden.shape),
        ],
        out_specs=[columns, whole(dhidden.shape), whole((8, width_d)), whole((width_d, WIDTH))],
        out_shape=[
            jax.ShapeDtypeStruct((halves, width_d, cols), BF16),
            jax.ShapeDtypeStruct((tokens, width_d), F32),
            jax.ShapeDtypeStruct((8, width_d), F32),
            jax.ShapeDtypeStruct((width_d, WIDTH), F32),
        ],
        scratch_shapes=[
            pltpu.VMEM((width_d, tokens), BF16),
            pltpu.VMEM((tokens, width_d), F32),
        ],
        compiler_params=pltpu.CompilerParams(vmem_limit_bytes=VMEM_LIMIT),
        name="project_back",
    )(dlin, weights, inputs, gain, dbl, beta_w, dhidden)


def mixer_tables(segments, length, beta, tokens):
    mine = lax.axis_index("tensor")
    seg = segments[0]
    position = jnp.arange(length)

    def behind(off):
        return jnp.where(position >= off, jnp.roll(seg, off), -1)

    ends = jnp.repeat(seg[CHUNK - 1 :: CHUNK], CHUNK)
    previous = jnp.where(position >= CHUNK, jnp.roll(ends, CHUNK), -1)
    columns = [seg, seg == previous, seg == ends]
    keeps = [behind(off) == seg for off in range(1, TAPS)]
    columns += keeps
    for off in range(1, TAPS):
        columns.append(jnp.where(position < length - off, jnp.roll(keeps[off - 1], -off), False))
    table = jnp.stack([c.astype(F32) for c in columns], 1)
    table = lax.dynamic_slice_in_dim(table, mine * tokens, tokens, 0)
    aux = jnp.concatenate(
        [
            table,
            jnp.zeros((tokens, 16 - table.shape[1]), F32),
            beta,
            jnp.zeros((tokens, WIDTH - 16 - beta.shape[1]), F32),
        ],
        1,
    )
    row = lax.dynamic_slice_in_dim(seg.astype(F32), mine * tokens, tokens, 0)
    return aux, jnp.broadcast_to(row[None], (8, tokens))


def by_thirds(first, second, third_one):
    rows = first.shape[0]
    tiles = jnp.stack([a.reshape(rows, -1, WIDTH) for a in (first, second, third_one)], 2)
    return tiles.reshape(rows, -1)


def thirds_of(values):
    rows = values.shape[0]
    tiles = values.reshape(rows, -1, 3, WIDTH)
    return tuple(tiles[:, :, i].reshape(rows, -1) for i in range(3))


def padded_rows(parts, multiple):
    flat = jnp.concatenate([p.reshape(-1) for p in parts])
    size = -(-flat.shape[0] // (multiple * WIDTH)) * multiple * WIDTH
    return jnp.pad(flat, (0, size - flat.shape[0])).reshape(-1, WIDTH)


def local(
    layer_input, segments, valid_mask, teacher, out_grad, norm_gain, w_query, w_key, w_value,
    w_beta, conv_weight, head_gain, w_out, mlp_gain, w_gate, w_up, w_down,
):
    parts, halves = lax.axis_size("dp"), lax.axis_size("tensor")
    tokens, width_d = layer_input.shape[1:]
    length = segments.shape[1]
    tokens_all = tokens * parts * halves
    half_heads = w_beta.shape[1]
    heads = half_heads * halves
    half_cols = w_query.shape[1]
    rows = w_query.shape[0]
    inputs_low = layer_input[0]

    valid = jnp.sum(valid_mask)
    counts = jnp.stack([valid // 64, valid % 64]).astype(BF16)
    small_parts = [w_beta, conv_weight, norm_gain, mlp_gain, head_gain, counts]
    small = padded_rows(small_parts, 16)
    first_shard = by_thirds(w_query, w_key, w_value)
    second_shard = jnp.concatenate([by_thirds(w_gate, w_up, w_down.T), w_out.T], 1)
    first_w, small = gather(
        [first_shard, small],
        split_tiles(3 * half_cols, rows)
        + [Tiles(1, "zxy", 0, small.shape[0], 0, WIDTH, WIDTH, 1, 0)],
        2,
    )
    second_w = lax.all_gather(second_shard, ("tensor", "dp"), axis=0, tiled=True).reshape(
        halves, width_d, second_shard.shape[1]
    )

    small = small.reshape(halves, parts, -1)
    marks = [0]
    for part in small_parts:
        marks.append(marks[-1] + part.size)
    beta_w, conv_w, gain_one, gain_two, gain_head, counts = (
        small[:, :, marks[i] : marks[i + 1]] for i in range(len(small_parts))
    )
    beta_w = beta_w.reshape(halves, width_d, half_heads).transpose(1, 0, 2).reshape(width_d, heads)
    beta_w = jnp.pad(beta_w, ((0, 0), (0, WIDTH - heads)))
    taps = conv_w.reshape((halves, parts) + conv_weight.shape).transpose(2, 3, 0, 4, 1, 5)
    taps = taps.reshape(12, heads * WIDTH).astype(F32)
    taps = jnp.concatenate([taps, jnp.zeros((4, heads * WIDTH), F32)], 0)
    gain_one = jnp.broadcast_to(gain_one[0].reshape(1, width_d).astype(F32), (8, width_d))
    gain_two = jnp.broadcast_to(gain_two[0].reshape(1, width_d).astype(F32), (8, width_d))
    gain_head = jnp.broadcast_to(gain_head[0].reshape(1, WIDTH).astype(F32), (8, WIDTH))
    counts = jnp.sum(counts.astype(F32), (0, 1))
    valid_sum = counts[0] * 64.0 + counts[1]

    halo = lax.ppermute(inputs_low[-HALO:], "tensor", [(0, 1), (1, 0)])
    spread = jnp.concatenate([halo, inputs_low], 0).astype(F32)
    rho_one = lax.rsqrt(jnp.mean(spread * spread, -1, keepdims=True) + 1e-05)
    spread = (spread * rho_one * gain_one[0:1]).astype(BF16)
    linear = jnp.einsum("td,jdc->jtc", spread, first_w, preferred_element_type=F32)
    strength = jax.nn.sigmoid(
        jnp.dot(spread[HALO:], beta_w[:, :heads], preferred_element_type=F32)
    )
    aux, seg_row = mixer_tables(segments, length, strength, tokens)
    onb, out, new, inverse, before = mixer_fwd(linear, aux, seg_row, taps, gain_head)
    coef = jnp.broadcast_to((tokens_all / 4.0) / valid_sum, (8, WIDTH))
    mask = valid_mask[0].astype(F32)[:, None]
    outputs, squares, early_g, second_g, donb, d_hidden, grad_gain_two = mlp(
        inputs_low, onb, second_w, gain_two, mask, teacher[0], out_grad[0], coef
    )
    early_g = lax.psum_scatter(
        early_g.reshape(halves * width_d, -1), ("tensor", "dp"), scatter_dimension=0, tiled=True
    ).astype(F32)
    dlin, dbl, dtaps, dgain = mixer_bwd(
        linear, aux, seg_row, taps, gain_head, out, new, inverse, before, donb
    )
    first_g, d_input, grad_gain_one, grad_beta = project_back(
        dlin, first_w, inputs_low, gain_one, dbl, beta_w, d_hidden
    )

    def shares(values):
        return jnp.broadcast_to(values.reshape(1, parts, -1), (halves, parts, values.size // parts))

    tail_parts = [
        grad_beta[:, :heads].reshape(parts, rows, halves, half_heads).transpose(2, 0, 1, 3),
        dtaps[:12]
        .reshape(12, halves, half_heads, parts, WIDTH // parts)
        .transpose(1, 3, 0, 2, 4),
        shares(jnp.sum(grad_gain_one, 0)),
        shares(jnp.sum(grad_gain_two, 0)),
        shares(dgain[0]),
        jnp.broadcast_to(jnp.sum(squares), (halves, parts, 1)),
    ]
    tail = jnp.concatenate([p.reshape(halves, parts, -1) for p in tail_parts], 2)
    tail_rows = -(-tail.shape[2] // (8 * WIDTH)) * 8
    tail = jnp.pad(tail, ((0, 0), (0, 0), (0, tail_rows * WIDTH - tail.shape[2])))
    g_gate, g_up, g_down, g_out, g_query, g_key, g_value, tail = scatter(
        second_g, first_g, tail.reshape(halves, parts * tail_rows, WIDTH), 3
    )
    g_gate, g_up, g_down = (
        jnp.concatenate(pair, 1) for pair in zip(thirds_of(early_g), (g_gate, g_up, g_down))
    )
    tail = tail.reshape(-1)
    sizes = [w_beta.size, conv_weight.size, norm_gain.size, mlp_gain.size, head_gain.size, 1]
    cuts = [sum(sizes[:i]) for i in range(7)]
    g_beta, g_conv, g_one, g_two, g_head, squares = (tail[cuts[i] : cuts[i + 1]] for i in range(6))
    return (
        outputs[None],
        squares[0] / (width_d * valid_sum),
        d_input[None],
        g_one,
        g_query,
        g_key,
        g_value,
        g_beta.reshape(w_beta.shape),
        g_conv.reshape(conv_weight.shape),
        g_head,
        g_out.T,
        g_two,
        g_gate,
        g_up,
        g_down.T,
    )


def solution(mesh):
    in_specs = (
        P("dp", "tensor", None),
        P("dp", None),
        P("dp", "tensor"),
        P("dp", "tensor", None),
        P("dp", "tensor", None),
        P("dp"),
        P("dp", "tensor"),
        P("dp", "tensor"),
        P("dp", "tensor"),
        P("dp", "tensor"),
        P(None, None, "tensor", "dp"),
        P("dp"),
        P("tensor", "dp"),
        P("dp"),
        P("dp", "tensor"),
        P("dp", "tensor"),
        P("tensor", "dp"),
    )
    out_specs = (
        P("dp", "tensor", None),
        P(),
        P("dp", "tensor", None),
        P("dp"),
        P("dp", "tensor"),
        P("dp", "tensor"),
        P("dp", "tensor"),
        P("dp", "tensor"),
        P(None, None, "tensor", "dp"),
        P("dp"),
        P("tensor", "dp"),
        P("dp"),
        P("dp", "tensor"),
        P("dp", "tensor"),
        P("tensor", "dp"),
    )
    return jax.shard_map(local, mesh=mesh, in_specs=in_specs, out_specs=out_specs, check_vma=False)
```

time: 881 us -> 420 us (0.48); the launches traced: 866 us -> 416 us
  waiting for transfers between devices: 441 us -> 6.5 us
  Pallas kernels: 123 us -> 334 us
  matrix products: 116 us -> 5.83 us
  blocking collectives: 84.5 us -> 0 us
  other arithmetic: 43.9 us -> 10.9 us
    pallas_call x0 -> x4, Pallas kernels: none -> 253 us  [the longest x1 108 us: scatter(): pl.pallas_call(functools.partial(scatter_kernel, tiles, groups), in_specs...]
    reduce_scatter x1, waiting for transfers between devices: 204 us -> 0.01 us  [local(): lax.psum_scatter(early_g.reshape(halves * width_d, -1), ('tensor', 'dp'),...]
    unnamed x6 -> x2, waiting for transfers between devices: 115 us -> 0.03 us
    dot_general x39 -> x1, matrix products: 107 us -> 0.42 us  [local(): jnp.dot(spread[HALO:], beta_w[:, :heads], preferred_element_type=F32)]
    psum x1 -> x0, waiting for transfers between devices: 66.3 us -> none  [local(): tail = lax.psum(tail, ('dp', 'tensor'))]
    all_gather x2 -> x1, waiting for transfers between devices: 56.5 us -> 6.46 us  [local(): lax.all_gather(second_shard, ('tensor', 'dp'), axis=0, tiled=True)]
    pallas_call x1, Pallas kernels: 77.5 us -> 31.2 us  [mixer_fwd(): pl.pallas_call(functools.partial(mixer_fwd_kernel, tokens), grid=(heads /...]
    unnamed x1 -> x0, blocking collectives: 42.8 us -> none
  transfers between devices with their start and end apart: 6 -> 3, of which waited for: 5 -> 1; matrix products, arithmetic and copies ran while one was open for 10% -> 9% of each run, Pallas kernels for 9% -> 67%
where the time goes in v2:
time: 420 us; the launch traced here: 416 us
  Pallas kernels  334 us (80%)
  local copies, waits for them, and re-layouts  35.3 us (8%)
  between operations  20.5 us (5%)
  other arithmetic  10.9 us (3%)
  waiting for transfers between devices  6.5 us (2%)
  matrix products  5.83 us (1%)
    pallas_call x1, Pallas kernels, scatter(): pl.pallas_call(functools.partial(scatter_kernel, tiles, groups), in_specs...  108 us
    pallas_call x1, Pallas kernels, gather(): pl.pallas_call(functools.partial(gather_kernel, tiles, arrays), in_specs=...  72.5 us
    pallas_call x1, Pallas kernels, mlp(): pl.pallas_call(functools.partial(mlp_kernel, count), grid=(2 * count + 2,...  56.6 us
    pallas_call x1, Pallas kernels, mixer_bwd(): pl.pallas_call(functools.partial(mixer_bwd_kernel, tokens), grid=(heads /...  50.2 us
    pallas_call x1, Pallas kernels, mixer_fwd(): pl.pallas_call(functools.partial(mixer_fwd_kernel, tokens), grid=(heads /...  31.2 us
    pallas_call x1, Pallas kernels, project_back(): pl.pallas_call(project_back_kernel, grid=(halves * kinds,), in_specs=[pl....  15 us
  transfers between devices with their start and end apart: 3, of which 1 were waited for; matrix products, arithmetic and copies ran while one was open for 9% of the time, Pallas kernels for 67%

profile of v2, /device:TPU:0, one launch (start us, length us, event | category | flops | bytes accessed | tf_op | source)
XLA Modules:
  0.0 416.1 jit_solution(3260103530679451351)
XLA Ops:
  7.2 1.0 stack_reshape.21
  8.3 1.1 stack_reshape.22
  9.3 1.1 stack_reshape.23
  11.7 0.9 pad_maximum_fusion.2
  12.7 3.0 collective-permute-start
  23.6 72.5 %gather.1 = (bf16[2,4,2,2,64,1536]{5,4,3,2,1,0:T(8,128)(2,1)}, bf16[2,4,2,2,16,128]{5,4,3,2,1,0:T(8,128)(2,1)}) custom-call(bf16[64,1536]{1,0:T(8,128)(2,1)} %reshape.487.refs_0_, bf16[16,128]{1,0:T(8,128)(2,1)} %pad_bitcast_fusion.refs_1_), custom_call_target="tpu_custom_call" | custom-call | tf_op jit(solution)/shard_map/gather/pallas_call | solution.py:410
  96.2 1.0 reshape_reshape.6
  99.7 1.4 compare_convert_fusion
  102.7 1.1 reshape.493
  104.6 0.9 copy.150.refs_5_
  108.7 1.0 copy-done
  109.7 5.4 %convolution_bitcast_fusion.lin_ref = f32[2,528,1536]{2,1,0:T(8,128)} fusion(bf16[2,1024,1536]{2,1,0:T(8,128)(2,1)S(1)} %bitcast.116, bf16[528,1024]{1,0:T(8,128)(2,1)S(1)} %fusion.2), kind=kOutput, calls=%fused_computation | convolution fusion | flops 3321888768 | bytes 13860864 | tf_op jit(solution)/shard_map/td,jdc->jtc/dot_general | solution.py:1375
  116.3 31.2 %mixer_fwd.1 = (bf16[2,512,512]{2,1,0:T(8,128)(2,1)}, f32[2,512,512]{2,1,0:T(8,128)}, bf16[8,4,128,128]{3,2,1,0:T(8,128)(2,1)}, bf16[8,4,128,128]{3,2,1,0:T(8,128)(2,1)}, bf16[8,4,128,128]{3,2,1,0:T(8,128)(2,1)}) custom-call(f32[2,528,1536]{2,1,0:T(8,128)} %convolution_bitcast_fusion.lin_ref, f32[512,128]{1,0:T(8,128)} %maximum_maximum_fusion.aux_ref, ...), custom_call_target="tpu_custom_call" | custom-call | tf_op jit(solution)/shard_map/mixer_fwd/pallas_call | solution.py:950
  147.6 6.5 %all-gather.2.cloned.1.call-done = bf16[2048,4736]{1,0:T(8,128)(2,1)} async-done(((bf16[64,4736]{1,0:T(8,128)(2,1)}), bf16[2048,4736]{1,0:T(8,128)(2,1)}) %all-gather.2.cloned.1.call-update) | async-done | bytes 19398672 | tf_op jit(solution)/shard_map/all_gather | solution.py:1349
  155.2 56.6 %mlp.1 = (bf16[512,1024]{1,0:T(8,128)(2,1)}, f32[8,1024]{1,0:T(8,128)}, bf16[2,1024,1536]{2,1,0:T(8,128)(2,1)}, bf16[2,1024,3200]{2,1,0:T(8,128)(2,1)}, f32[2,51...) custom-call(bf16[512,1024]{1,0:T(8,128)(2,1)} %bitcast.117, ...), custom_call_target="tpu_custom_call" | custom-call | tf_op jit(solution)/shard_map/mlp/pallas_call | solution.py:1160
  212.8 50.2 %mixer_bwd.1 = (bf16[2,512,1536]{2,1,0:T(8,128)(2,1)}, f32[512,128]{1,0:T(8,128)}, f32[16,1024]{1,0:T(8,128)}, f32[8,128]{1,0:T(8,128)}) custom-call(f32[2,528,1536]{2,1,0:T(8,128)} %convolution_bitcast_fusion.lin_ref, f32[512,128]{1,0:T(8,128)} %maximum_maximum_fusion.aux_ref, f32[8,512]{1,0:T(8,128)} %broadcast_in_dim.90.seg_ref, ...), custom_call_target="tpu_custom_call" | custom-call | tf_op jit(solution)/shard_map/mixer_bwd/pallas_call | solution.py:997
  263.6 15.0 %project_back.1 = (bf16[2,1024,1536]{2,1,0:T(8,128)(2,1)}, f32[512,1024]{1,0:T(8,128)}, f32[8,1024]{1,0:T(8,128)}, f32[1024,128]{1,0:T(8,128)}) custom-call(bf16[2,512,1536]{2,1,0:T(8,128)(2,1)} %get-tuple-element.55.dlin_ref, bf16[2,1024,1536]{2,1,0:T(8,128)(2,1)} %bitcast.115, bf16[512,1024]{1,0:T(8,128)(2,1)} %bitcast.118, ...), custom_call_target="tpu_custom_call" | custom-call | tf_op jit(solution)/shard_map/project_back/pallas_call | solution.py:1247
  278.7 1.2 copy.152
  284.9 108.3 %scatter.1 = (f32[64,896]{1,0:T(8,128)}, f32[64,896]{1,0:T(8,128)}, f32[64,896]{1,0:T(8,128)}, f32[64,512]{1,0:T(8,128)}, f32[64,512]{1,0:T(8,128)}, /*index=5*/...) custom-call(bf16[2,4,2,2,64,3200]{5,4,3,2,1,0:T(8,128)(2,1)} %bitcast.121, ...), custom_call_target="tpu_custom_call" | custom-call | tf_op jit(solution)/shard_map/scatter/pallas_call | solution.py:485
  394.6 1.3 slice.198
  395.9 1.2 slice.202
  399.2 1.3 fusion.14
  400.5 1.3 reshape.513
  401.9 1.1 slice_reduce_fusion
  (160 shorter events, 30.1 us)
Async XLA Ops:
  7.2 146.8 %all-gather.2.cloned.1.call-start = ((), (), s32[]{:S(2)}) async-start(), calls=%async_computation.1 | async-start | bytes 20004864 | tf_op jit(solution)/shard_map/all_gather | solution.py:1349
  10.6 5.1 %copy-start.18 = (s32[1,512]{1,0:T(1,128)S(1)}, s32[1,512]{1,0:T(1,128)}, u32[]{:S(2)}) copy-start(s32[1,512]{1,0:T(1,128)} %param.19) | copy-start | bytes 6148
  10.6 8.3 %copy-start.5 = (s32[1,1024]{1,0:T(1,128)S(1)}, s32[1,1024]{1,0:T(1,128)}, u32[]{:S(2)}) copy-start(s32[1,1024]{1,0:T(1,128)} %param.18) | copy-start | bytes 12292
  10.6 10.5 %copy-start.19 = (bf16[64,4]{0,1:T(4,128)(2,1)S(1)}, bf16[64,4]{0,1:T(4,128)(2,1)}, u32[]{:S(2)}) copy-start(bf16[64,4]{0,1:T(4,128)(2,1)} %param.26) | copy-start | bytes 1540
  10.6 10.7 %copy-start.17 = (bf16[3,4,4,8]{3,2,1,0:T(4,128)(2,1)S(1)}, bf16[3,4,4,8]{3,2,1,0:T(4,128)(2,1)}, u32[]{:S(2)}) copy-start(bf16[3,4,4,8]{3,2,1,0:T(4,128)(2,1)} %param.27) | copy-start | bytes 2308
  10.6 10.8 %copy-start.11 = (bf16[64,512]{1,0:T(8,128)(2,1)S(1)}, bf16[64,512]{1,0:T(8,128)(2,1)}, u32[]{:S(2)}) copy-start(bf16[64,512]{1,0:T(8,128)(2,1)} %param.23) | copy-start | bytes 196612
  10.7 10.8 %copy-start.12 = (bf16[64,512]{1,0:T(8,128)(2,1)S(1)}, bf16[64,512]{1,0:T(8,128)(2,1)}, u32[]{:S(2)}) copy-start(bf16[64,512]{1,0:T(8,128)(2,1)} %param.24) | copy-start | bytes 196612
  11.2 10.4 %copy-start.13 = (bf16[64,512]{1,0:T(8,128)(2,1)S(1)}, bf16[64,512]{1,0:T(8,128)(2,1)}, u32[]{:S(2)}) copy-start(bf16[64,512]{1,0:T(8,128)(2,1)} %param.25) | copy-start | bytes 196612
  11.6 11.3 %copy-start.20 = (bf16[64]{0:T(256)(128)(2,1)S(1)}, bf16[64]{0:T(256)(128)(2,1)}, u32[]{:S(2)}) copy-start(bf16[64]{0:T(256)(128)(2,1)} %param.22) | copy-start | bytes 388
  11.7 11.3 %copy-start.21 = (bf16[64]{0:T(256)(128)(2,1)S(1)}, bf16[64]{0:T(256)(128)(2,1)}, u32[]{:S(2)}) copy-start(bf16[64]{0:T(256)(128)(2,1)} %param.30) | copy-start | bytes 388
  11.7 11.3 %copy-start.22 = (bf16[8]{0:T(256)(128)(2,1)S(1)}, bf16[8]{0:T(256)(128)(2,1)}, u32[]{:S(2)}) copy-start(bf16[8]{0:T(256)(128)(2,1)} %param.28) | copy-start | bytes 52
  12.6 388.0 %reduce-scatter.2.cloned.1.call-start = ((), (), s32[]{:S(2)}) async-start(), calls=%async_computation.2 | async-start | bytes 6488064 | tf_op jit(solution)/shard_map/reduce_scatter | solution.py:1386
  12.7 94.2 %collective-permute-start = (bf16[16,1024]{1,0:T(8,128)(2,1)S(1)}, bf16[16,1024]{1,0:T(8,128)(2,1)S(1)}, u32[]{:S(2)}, u32[]{:S(2)}) collective-permute-start(bf16[16,1024]{1,0:T(8,128)(2,1)S(1)} %slice_bitcast_fusion), channel_id=1, source_target_pairs={{0,1},{1,0},{2,3},{3,2},{4,5},{5,4},{6,7},{7,6},{8,9},{9,8},{10,11... | collective-permute-start | bytes 98312 | tf_op jit(solution)/shard_map/ppermute | solution.py:1371
  106.8 2.9 copy-start
  263.6 17.5 %copy-start.14 = (f32[16,1024]{1,0:T(8,128)S(1)}, f32[16,1024]{1,0:T(8,128)}, u32[]{:S(2)}) copy-start(f32[16,1024]{1,0:T(8,128)} %get-tuple-element.60) | copy-start | bytes 196612
  278.6 4.1 copy-start.15
  278.6 4.2 %copy-start.16 = (f32[8,1024]{1,0:T(8,128)S(1)}, f32[8,1024]{1,0:T(8,128)}, u32[]{:S(2)}) copy-start(f32[8,1024]{1,0:T(8,128)} %get-tuple-element.64) | copy-start | bytes 98308
  393.2 9.8 %copy-start.4 = (f32[64,896]{1,0:T(8,128)S(1)}, f32[64,896]{1,0:T(8,128)}, u32[]{:S(2)}) copy-start(f32[64,896]{1,0:T(8,128)} %get-tuple-element.74) | copy-start | bytes 688132
  393.2 10.6 %copy-start.3 = (f32[64,896]{1,0:T(8,128)S(1)}, f32[64,896]{1,0:T(8,128)}, u32[]{:S(2)}) copy-start(f32[64,896]{1,0:T(8,128)} %get-tuple-element.73) | copy-start | bytes 688132
  393.2 11.4 %copy-start.2 = (f32[64,896]{1,0:T(8,128)S(1)}, f32[64,896]{1,0:T(8,128)}, u32[]{:S(2)}) copy-start(f32[64,896]{1,0:T(8,128)} %get-tuple-element.72) | copy-start | bytes 688132
  400.5 4.8 %copy-start.9 = (f32[64,512]{1,0:T(8,128)S(1)}, f32[64,512]{1,0:T(8,128)}, u32[]{:S(2)}) copy-start(f32[64,512]{1,0:T(8,128)} %get-tuple-element.201) | copy-start | bytes 393220
  401.9 4.1 copy-start.8
  401.9 4.8 %copy-start.7 = (f32[64,512]{1,0:T(8,128)S(1)}, f32[64,512]{1,0:T(8,128)}, u32[]{:S(2)}) copy-start(f32[64,512]{1,0:T(8,128)} %get-tuple-element.203) | copy-start | bytes 393220
  401.9 5.4 %copy-start.6 = (f32[64,512]{1,0:T(8,128)S(1)}, f32[64,512]{1,0:T(8,128)}, u32[]{:S(2)}) copy-start(f32[64,512]{1,0:T(8,128)} %get-tuple-element.70) | copy-start | bytes 393220
  (2 other events, 3.3 us)
Sparse Core Ops, SparseCore 0:
  12.7 141.2 all-gather.1
  212.0 133.2 reduce-scatter.1

commit v3 on v2

--- a/solution.py
+++ b/solution.py
@@ -1,6 +1,5 @@
 import collections
 import functools
-import itertools
 
 import jax
 import jax.numpy as jnp
@@ -15,14 +14,13 @@
 HALO = 16
 WIDTH = 128
 PAIR = 2
-EARLY = 4
+MOVES = 2
 TAPS = 4
 VMEM_LIMIT = 60 * 1024 * 1024
 
 GRID = (4, 2, 2)
 DEPTH = GRID[0] - 1 + 2
 LAGS = DEPTH + 2
-LINKS = [("z", 1), ("z", -1), ("x", 0), ("y", 0)]
 Tiles = collections.namedtuple(
     "Tiles", ["array", "order", "row", "rows", "col", "stride", "cols", "count", "start"]
 )
@@ -83,50 +81,6 @@
         src_ref=src, dst_ref=dst, send_sem=send_sem, recv_sem=recv_sem,
         device_id=device_of(to), device_id_type=MESH,
     )
-
-
-def offsets(lag):
-    every = itertools.product(range(1 - GRID[0], GRID[0]), (0, 1), (0, 1))
-    return [off for off in every if abs(off[0]) + off[1] + off[2] == lag]
-
-
-def moved(at, off):
-    return dict(
-        at,
-        z=at["z"] + off[0],
-        x=1 - at["x"] if off[1] else at["x"],
-        y=1 - at["y"] if off[2] else at["y"],
-    )
-
-
-def last_axis(order, off):
-    shifts = {"z": off[0], "x": off[1], "y": off[2]}
-    return max([order.index(axis) for axis in order if shifts[axis]], default=-1)
-
-
-def onward(order, off):
-    last = last_axis(order, off)
-    out = []
-    if last >= 0 and order[last] == "z":
-        out.append(("z", 1 if off[0] < 0 else -1))
-    for axis in order[last + 1 :]:
-        out += [("z", 1), ("z", -1)] if axis == "z" else [(axis, 0)]
-    return out
-
-
-def backward_link(order, off):
-    axis = order[last_axis(order, off)]
-    return (axis, (1 if off[0] > 0 else -1) if axis == "z" else 0)
-
-
-def block_id(at):
-    return (at["z"] * GRID[1] + at["x"]) * 2 + at["y"]
-
-
-def inbox_id(order, link, at):
-    if link[0] == "y" or (link[0] == "z" and order[0] != "y"):
-        return at["z"] * 2 + at["x"]
-    return at["z"] * 2 + at["y"]
 
 
 def when(test, action):
@@ -173,6 +127,19 @@
     return [sum(tile.count for tile in tiles[:i]) for i in range(len(tiles))]
 
 
+def order_of(tile):
+    first, last = [axis for axis in tile.order if axis != "z"]
+    return first, last, tile.order[0] == "z"
+
+
+def distances():
+    return range(1 - GRID[0], GRID[0])
+
+
+def ways(distance):
+    return (1, -1) if distance == 0 else ((1,) if distance < 0 else (-1,))
+
+
 class Gather:
     def __init__(self, tiles, shards, fulls, sems):
         self.tiles, self.shards, self.fulls = tiles, shards, fulls
@@ -184,8 +151,8 @@
     def sems(tiles, arrays):
         slots = sum(tile.count for tile in tiles)
         return [
-            pltpu.SemaphoreType.DMA((len(tiles), 2, len(LINKS), 16)),
-            pltpu.SemaphoreType.DMA((slots, 16)),
+            pltpu.SemaphoreType.DMA((len(tiles), 2, 4, GRID[0])),
+            pltpu.SemaphoreType.DMA((slots, 3, GRID[0])),
             pltpu.SemaphoreType.DMA((slots,)),
             pltpu.SemaphoreType.DMA((slots,)),
             pltpu.SemaphoreType.DMA((arrays,)),
@@ -205,36 +172,61 @@
         for copy in copies:
             copy.wait()
 
-    def copy(self, index, group, slot, src, link, own):
-        tile = self.tiles[index]
+    def copy(self, index, group, slot, z, link, own=False):
+        at, tile = self.at, self.tiles[index]
+        first, last, z_first = order_of(tile)
         rows, cols = window(tile, group)
-        full = self.fulls[tile.array].at[src["y"], src["z"], src["x"], src["c"], rows, cols]
+        pair = link == 3 or (link < 2 and not z_first)
+        spot = {"y": at["y"], "x": at["x"]}
+        if pair:
+            spot[first] = slice(None)
+        ref = self.fulls[tile.array].at[spot["y"], z, spot["x"], at["c"], rows, cols]
+        to = ("z", 1 - 2 * link) if link < 2 else (first if link == 2 else last, 0)
         return remote(
-            self.shards[tile.array].at[rows, cols] if own else full,
-            full,
-            self.send_sem.at[index, group % 2, LINKS.index(link), block_id(src)],
-            self.recv_sem.at[slot, block_id(src)],
-            across(self.at, link),
-        )
+            self.shards[tile.array].at[rows, cols] if own else ref,
+            ref,
+            self.send_sem.at[index, group % 2, link, z],
+            self.recv_sem.at[slot, max(link - 1, 0), z],
+            across(at, to),
+        )
+
+    def send(self, index, group, slot, z, link, own=False):
+        def go():
+            one = self.copy(index, group, slot, z, link, own)
+            pl.when(group >= 2)(one.wait_send)
+            one.start()
+
+        when(inside(self.at["z"] + 1 - 2 * link) if link < 2 else None, go)
 
     def visit(self, index, group, slot, lag):
         at, tile = self.at, self.tiles[index]
-        for off in offsets(lag) if lag <= DEPTH else ():
-            src = moved(at, off)
+        _, _, z_first = order_of(tile)
+        offset = 0 if z_first else 1
+        for far in distances():
+            z = at["z"] + far
 
             def handle():
-                if lag:
-                    self.copy(index, group, slot, src, LINKS[-1], False).wait_recv()
-                for link in onward(tile.order, off):
-
-                    def send():
-                        one = self.copy(index, group, slot, src, link, lag == 0)
-                        pl.when(group >= 2)(one.wait_send)
-                        one.start()
-
-                    when(inside(at["z"] + link[1]) if link[0] == "z" else None, send)
-
-            when(inside(src["z"]) if off[0] else None, handle)
+                if z_first and lag == abs(far):
+                    if far:
+                        self.copy(index, group, slot, z, 0).wait_recv()
+                    for way in ways(far):
+                        self.send(index, group, slot, z, (1 - way) // 2, far == 0)
+                    self.send(index, group, slot, z, 2, far == 0)
+                if z_first and lag == abs(far) + 1:
+                    self.copy(index, group, slot, z, 2).wait_recv()
+                    self.send(index, group, slot, z, 3)
+                if not z_first and far == 0 and lag == 0:
+                    self.send(index, group, slot, z, 2, True)
+                if not z_first and lag == abs(far) + 1:
+                    self.copy(index, group, slot, z, 0 if far else 2).wait_recv()
+                    for way in ways(far):
+                        self.send(index, group, slot, z, (1 - way) // 2)
+                    self.send(index, group, slot, z, 3)
+                if lag == abs(far) + 2:
+                    self.copy(index, group, slot, z, 3).wait_recv()
+
+            if any(lag == abs(far) + more for more in range(3)):
+                when(inside(z) if far else None, handle)
         if lag >= DEPTH:
             rows, cols = window(tile, group)
             part = self.fulls[tile.array].at[:, :, :, at["c"], rows, cols]
@@ -253,42 +245,51 @@
 
     def finish(self):
         for index, tile in enumerate(self.tiles):
+            _, _, z_first = order_of(tile)
             for group in range(max(0, tile.count - 2), tile.count):
-                for off in [off for lag in range(DEPTH + 1) for off in offsets(lag)]:
-                    src = moved(self.at, off)
-                    here = inside(src["z"]) if off[0] else None
-                    for link in onward(tile.order, off):
-                        there = inside(self.at["z"] + link[1]) if link[0] == "z" else None
-                        one = self.copy(index, group, 0, src, link, False)
-                        when(both(here, there), one.wait_send)
+                for far in distances():
+                    z = self.at["z"] + far
+                    here = inside(z) if far else None
+                    for way in ways(far):
+                        one = self.copy(index, group, 0, z, (1 - way) // 2)
+                        when(both(here, inside(self.at["z"] + way)), one.wait_send)
+                    if z_first or far == 0:
+                        when(here, self.copy(index, group, 0, z, 2).wait_send)
+                    when(here, self.copy(index, group, 0, z, 3).wait_send)
 
 
 class Scatter:
     def __init__(self, tiles, grads, put, boxes, sems):
         self.tiles, self.grads, self.put = tiles, grads, put
-        count = len(tiles)
-        self.sums, self.pairs, self.inbox = boxes[:count], boxes[count : 2 * count], boxes[2 * count :]
+        self.sums, self.pairs, self.from_z, self.from_first, self.from_last = (
+            boxes[i * len(tiles) : (i + 1) * len(tiles)] for i in range(5)
+        )
         self.send_sem, self.recv_sem, self.core_send, self.core_recv, self.own_sem = sems
         self.at = position()
         self.steps = steps_of(tiles)
 
     @staticmethod
     def boxes(tiles, dtypes):
-        whole, part = [], []
+        whole, from_z, from_first, from_last = [], [], [], []
         for tile in tiles:
-            dtype = dtypes[tile.array]
-            whole.append(
-                pltpu.VMEM((tile.count, 2) + GRID[:2] + (tile.rows, tile.cols), dtype)
+            z_first = order_of(tile)[2]
+            dtype, shape = dtypes[tile.array], (tile.rows, tile.cols)
+            whole.append(pltpu.VMEM((tile.count, 2) + GRID[:2] + shape, dtype))
+            from_z.append(
+                pltpu.VMEM((tile.count, 2, GRID[0]) + (() if z_first else (2,)) + shape, dtype)
             )
-            part.append(pltpu.VMEM((tile.count, len(LINKS), 8, tile.rows, tile.cols), dtype))
-        return whole + whole + part
+            from_first.append(
+                pltpu.VMEM((tile.count,) + ((GRID[0],) if z_first else ()) + shape, dtype)
+            )
+            from_last.append(pltpu.VMEM((tile.count, GRID[0], 2) + shape, dtype))
+        return whole + whole + from_z + from_first + from_last
 
     @staticmethod
     def sems(tiles):
         slots = sum(tile.count for tile in tiles)
         return [
-            pltpu.SemaphoreType.DMA((len(tiles), 2, 16)),
-            pltpu.SemaphoreType.DMA((slots, len(LINKS), 8)),
+            pltpu.SemaphoreType.DMA((len(tiles), 2, 3, GRID[0])),
+            pltpu.SemaphoreType.DMA((slots, 4, GRID[0])),
             pltpu.SemaphoreType.DMA((slots,)),
             pltpu.SemaphoreType.DMA((slots,)),
             pltpu.SemaphoreType.DMA((slots,)),
@@ -297,21 +298,57 @@
     def begin(self):
         greet_all(self.at)
 
-    def copy(self, index, group, slot, dest, link, label):
-        tile = self.tiles[index]
-        box = inbox_id(tile.order, label, dest)
+    def spot(self, index, group, z, kind, other=False):
+        first, last, z_first = order_of(self.tiles[index])
+        spot = {"y": self.at["y"], "x": self.at["x"]}
+        if kind == "last" or (kind == "z" and not z_first):
+            spot[first] = slice(None)
+        if other:
+            axis = first if kind == "first" else last
+            spot[axis] = 1 - self.at[axis]
+        return (group, spot["y"], z, spot["x"])
+
+    def copy(self, index, group, slot, z, kind, way=0):
+        first, last, z_first = order_of(self.tiles[index])
+        if kind == "z":
+            label = (1 + way) // 2
+            to, dst = ("z", way), self.from_z[index].at[group, label, z]
+        elif kind == "first":
+            label, to = 2, (first, 0)
+            dst = self.from_first[index].at[(group, z) if z_first else group]
+        else:
+            label, to, dst = 3, (last, 0), self.from_last[index].at[group, z]
         return remote(
-            self.sums[index].at[group, dest["y"], dest["z"], dest["x"]],
-            self.inbox[index].at[group, LINKS.index(label), box],
-            self.send_sem.at[index, group % 2, block_id(dest)],
-            self.recv_sem.at[slot, LINKS.index(label), box],
-            across(self.at, link),
-        )
+            self.sums[index].at[self.spot(index, group, z, kind, kind != "z")],
+            dst,
+            self.send_sem.at[index, group % 2, max(label - 1, 0), z],
+            self.recv_sem.at[slot, label, z],
+            across(self.at, to),
+        )
+
+    def send(self, index, group, slot, z, kind, way=0):
+        one = self.copy(index, group, slot, z, kind, way)
+        pl.when(group >= 2)(one.wait_send)
+        one.start()
+
+    def add(self, index, group, slot, z, kind, way=0):
+        self.copy(index, group, slot, z, kind, -way).wait_recv()
+        z_first = order_of(self.tiles[index])[2]
+        if kind == "z":
+            came = self.from_z[index][group, (1 - way) // 2, z]
+        elif kind == "first":
+            came = self.from_first[index][(group, z) if z_first else group]
+        else:
+            came = self.from_last[index][group, z]
+        spot = self.spot(index, group, z, kind)
+        total = self.sums[index][spot].astype(F32) + came.astype(F32)
+        self.sums[index][spot] = total.astype(self.sums[index].dtype)
 
     def visit(self, index, group, slot, stage):
         at, tile = self.at, self.tiles[index]
         rows, cols = window(tile, group)
         grad, sums = self.grads[tile.array], self.sums[index]
+        _, _, z_first = order_of(tile)
         if stage <= 1:
             pair = remote(
                 grad.at[:, :, :, 1 - at["c"], rows, cols],
@@ -334,39 +371,38 @@
                 sums[group].astype(F32) + self.pairs[index][group].astype(F32)
             ).astype(sums.dtype)
         lag = DEPTH + 1 - stage
-        for off in offsets(lag):
-            dest = moved(at, off)
+
+        def along_z(z, far):
+            for way in ways(far):
+                pl.when(inside(at["z"] + way))(
+                    functools.partial(self.add, index, group, slot, z, "z", way)
+                )
+            if far:
+                self.send(index, group, slot, z, "z", 1 if far > 0 else -1)
+
+        for far in distances():
+            z = at["z"] + far
 
             def handle():
-                spot = (group, dest["y"], dest["z"], dest["x"])
-
-                def add(links):
-                    total = sums[spot].astype(F32)
-                    for link in links:
-                        self.copy(index, group, slot, dest, link, link).wait_recv()
-                        box = inbox_id(tile.order, link, dest)
-                        total = total + self.inbox[index][group, LINKS.index(link), box].astype(F32)
-                    return total
-
-                fixed = [link for link in onward(tile.order, off) if link[0] != "z"]
-                for link in onward(tile.order, off):
-                    if link[0] == "z":
-
-                        @pl.when(inside(at["z"] + link[1]))
-                        def _():
-                            sums[spot] = add([link]).astype(sums.dtype)
-
-                if lag == 0:
-                    self.put(tile, group, add(fixed))
-                    return
-                if fixed:
-                    sums[spot] = add(fixed).astype(sums.dtype)
-                link = backward_link(tile.order, off)
-                one = self.copy(index, group, slot, dest, link, (link[0], -link[1]))
-                pl.when(group >= 2)(one.wait_send)
-                one.start()
-
-            when(inside(dest["z"]) if off[0] else None, handle)
+                if lag == abs(far) + 2:
+                    self.send(index, group, slot, z, "last")
+                if lag == abs(far) + 1:
+                    self.add(index, group, slot, z, "last")
+                    if z_first:
+                        self.send(index, group, slot, z, "first")
+                    else:
+                        along_z(z, far)
+                        if far == 0:
+                            self.send(index, group, slot, z, "first")
+                if lag == abs(far) and (z_first or far == 0):
+                    self.add(index, group, slot, z, "first")
+                    if z_first:
+                        along_z(z, far)
+                    if far == 0:
+                        self.put(tile, group, sums[group, at["y"], at["z"], at["x"]].astype(F32))
+
+            if any(lag == abs(far) + more for more in range(3)):
+                when(inside(z) if far else None, handle)
 
     def step(self, step):
         for stage in range(LAGS):
@@ -378,12 +414,17 @@
 
     def finish(self):
         for index, tile in enumerate(self.tiles):
+            z_first = order_of(tile)[2]
             for group in range(max(0, tile.count - 2), tile.count):
-                for off in [off for lag in range(1, DEPTH + 1) for off in offsets(lag)]:
-                    dest = moved(self.at, off)
-                    link = backward_link(tile.order, off)
-                    one = self.copy(index, group, 0, dest, link, (link[0], -link[1]))
-                    when(inside(dest["z"]) if off[0] else None, one.wait_send)
+                for far in distances():
+                    z = self.at["z"] + far
+                    here = inside(z) if far else None
+                    if far:
+                        one = self.copy(index, group, 0, z, "z", 1 if far > 0 else -1)
+                        when(here, one.wait_send)
+                    if z_first or far == 0:
+                        when(here, self.copy(index, group, 0, z, "first").wait_send)
+                    when(here, self.copy(index, group, 0, z, "last").wait_send)
 
 
 def run_all(moves):
@@ -421,70 +462,68 @@
     return [full.reshape(halves, -1, full.shape[-1]) for full in fulls]
 
 
-def scatter_kernel(tiles, groups, *refs):
-    boxes = 3 * len(tiles)
-    grads, outs, rest = refs[:3], refs[3:11], refs[11:]
-    gate, upper, down, out, query, key, value, small = outs
-
+def put_turns(turns, rest, columns):
     def put(tile, group, total):
         rows = pl.ds(tile.row, tile.rows)
-        if tile.array == 2:
-            small[...] = total
-            return
-        if tile.count == 1 and tile.array == 0:
-            out[rows, 3 * WIDTH :] = total
-            return
-        thirds = (gate, upper, down) if tile.array == 0 else (query, key, value)
-        offset = tile.col // WIDTH
-        width = tile.cols // WIDTH
-
-        def inner():
-            lanes = pl.ds(pl.multiple_of(group * WIDTH, WIDTH), WIDTH)
-            for i in range(width):
-                thirds[offset + i][rows, lanes] = total[:, i * WIDTH : (i + 1) * WIDTH]
-
+        for i in range(tile.cols // WIDTH):
+            piece = total[:, i * WIDTH : (i + 1) * WIDTH]
+            at = tile.col // WIDTH + i
+            column = at + group * (tile.stride // WIDTH)
+
+            def inner():
+                lanes = pl.multiple_of(lax.div(column, len(turns)) * WIDTH, WIDTH)
+                turns[at % len(turns)][rows, pl.ds(lanes, WIDTH)] = piece
+
+            if rest is None:
+                inner()
+                continue
+            if tile.count > 1 or at < columns:
+                pl.when(column < columns)(inner)
+
+            @pl.when(column >= columns)
+            def _():
+                lanes = pl.multiple_of((column - columns) * WIDTH, WIDTH)
+                rest[rows, pl.ds(lanes, WIDTH)] = piece
+
+    return put
+
+
+def scatter_kernel(tiles, first_ref, small_grad_ref, query, key, value, small_ref, *rest):
+    boxes = 5 * len(tiles)
+    turns = put_turns((query, key, value), None, 0)
+
+    def put(tile, group, total):
         if tile.array == 1:
-            inner()
-            return
-        pl.when(group < groups)(inner)
-
-        @pl.when(group == groups)
-        def _():
-            out[rows, tile.col : tile.col + tile.cols] = total
-
-    run_all(Scatter(tiles, grads, put, rest[:boxes], rest[boxes:]))
-
-
-def scatter(second, first, small, ident):
-    halves = lax.axis_size("tensor")
-    parts = lax.axis_size("dp")
-    rows = second.shape[1] // parts
-    groups = second.shape[2] // (3 * WIDTH) - 1
-    half_cols = second.shape[2] - groups * 3 * WIDTH
+            small_ref[...] = total
+        else:
+            turns(tile, group, total)
+
+    run_all(Scatter(tiles, [first_ref, small_grad_ref], put, rest[:boxes], rest[boxes:]))
+
+
+def blocks_of(grad):
+    return grad.reshape((2,) + GRID + (-1, grad.shape[-1]))
+
+
+def plain_scatter(grad):
+    return lax.psum_scatter(
+        grad.reshape(-1, grad.shape[-1]), ("tensor", "dp"), scatter_dimension=0, tiled=True
+    ).astype(F32)
+
+
+def scatter(first, small, ident):
+    rows = first.shape[1] // lax.axis_size("dp")
     if not on_grid():
-        second, first, small = (
-            lax.psum_scatter(
-                grad.reshape(-1, grad.shape[-1]), ("tensor", "dp"), scatter_dimension=0, tiled=True
-            ).astype(F32)
-            for grad in (second, first, small)
-        )
-        return (
-            thirds_of(second[:, : groups * 3 * WIDTH])
-            + (second[:, groups * 3 * WIDTH :],)
-            + thirds_of(first)
-            + (small,)
-        )
-    grads = [grad.reshape((2,) + GRID + (-1, grad.shape[-1])) for grad in (second, first, small)]
-    tiles = split_tiles(second.shape[2], rows)
-    tiles += split_tiles(first.shape[2], rows, array=1, start=tiles[0].count)
-    small_rows = grads[2].shape[-2]
-    tiles.append(Tiles(2, "zxy", 0, small_rows, 0, WIDTH, WIDTH, 1, 0))
+        return apart(plain_scatter(first), 3) + (plain_scatter(small),)
+    grads = [blocks_of(first), blocks_of(small)]
+    tiles = split_tiles(first.shape[2], rows)
+    small_rows = grads[1].shape[-2]
+    tiles.append(Tiles(1, "zxy", 0, small_rows, 0, WIDTH, WIDTH, 1, 0))
     hbm = pl.BlockSpec(memory_space=pl.ANY)
-    shapes = [(rows, groups * WIDTH)] * 3 + [(rows, half_cols)]
-    shapes += [(rows, first.shape[2] // 3)] * 3 + [(small_rows, WIDTH)]
+    shapes = [(rows, first.shape[2] // 3)] * 3 + [(small_rows, WIDTH)]
     return pl.pallas_call(
-        functools.partial(scatter_kernel, tiles, groups),
-        in_specs=[hbm] * 3,
+        functools.partial(scatter_kernel, tiles),
+        in_specs=[hbm] * 2,
         out_specs=[pl.BlockSpec(memory_space=pltpu.VMEM)] * len(shapes),
         out_shape=[jax.ShapeDtypeStruct(shape, F32) for shape in shapes],
         scratch_shapes=Scatter.boxes(tiles, [grad.dtype for grad in grads]) + Scatter.sems(tiles),
@@ -700,18 +739,32 @@
 
 
 def mixer_bwd_kernel(
-    tokens, lin_ref, aux_ref, seg_ref, taps_ref, gain_ref,
-    o_ref, n_ref, t_ref, s_ref, donb_ref,
-    dlin_ref, dbl_ref, dtaps_ref, dgain_ref,
-    state, extended, outbox, inbox, tailbox, headbox, send_sem, recv_sem, tail_send, tail_recv,
+    tokens, tiles, lin_ref, aux_ref, seg_ref, taps_ref, gain_ref,
+    o_ref, n_ref, t_ref, s_ref, donb_ref, *refs,
 ):
+    moves = None
+    if tiles:
+        grads_ref, refs = refs[0], refs[1:]
+    dlin_ref, dbl_ref, dtaps_ref, dgain_ref, *refs = refs
+    if tiles:
+        sums, refs = refs[:4], refs[4:]
+    state, extended, outbox, inbox, tailbox, headbox = refs[:6]
+    send_sem, recv_sem, tail_send, tail_recv, *refs = refs[6:]
+    if tiles:
+        boxes = 5 * len(tiles)
+        columns = 3 * (sums[0].shape[1] // WIDTH)
+        put = put_turns(sums[:3], sums[3], columns)
+        moves = Scatter(tiles, [grads_ref], put, refs[:boxes], refs[boxes:])
     step = pl.program_id(0)
     mine = lax.axis_index("tensor")
     chunks = tokens // CHUNK
 
     @pl.when(step == 0)
     def _():
-        greet(1 - mine)
+        if moves:
+            moves.begin()
+        else:
+            greet(1 - mine)
         dbl_ref[...] = jnp.zeros_like(dbl_ref)
         dgain_ref[...] = jnp.zeros_like(dgain_ref)
 
@@ -734,6 +787,9 @@
             device_id={"tensor": 1 - mine},
             device_id_type=MESH,
         )
+
+    if moves:
+        moves.step(step * MOVES)
 
     aux = aux_ref[...]
     seg_row = seg_ref[...]
@@ -807,6 +863,10 @@
             spots, grams, pulls, reaches, dqs, dks, gaps
         )
     ]
+
+    if moves:
+        for more in range(1, MOVES):
+            moves.step(step * MOVES + more)
 
     @pl.when(mine == 1)
     def _():
@@ -925,6 +985,14 @@
             dlin_ref[0, :, third(sub, index)] = dlin.astype(BF16)
         dtaps_ref[12:16, lanes] = jnp.zeros((4, WIDTH), F32)
 
+    if moves:
+
+        @pl.when(step == pl.num_programs(0) - 1)
+        def _():
+            done = outbox.shape[0] // PAIR * MOVES
+            lax.fori_loop(done, moves.steps, lambda i, _: (moves.step(i), 0)[1], 0)
+            moves.finish()
+
     @pl.when((step == pl.num_programs(0) - 1) & (mine == 1))
     def _():
         for head in range(outbox.shape[0]):
@@ -979,7 +1047,7 @@
     )(linear, aux, seg_row, taps, gain)
 
 
-def mixer_bwd(linear, aux, seg_row, taps, gain, out, new, inverse, before, donb):
+def mixer_bwd(linear, aux, seg_row, taps, gain, out, new, inverse, before, donb, grads, units):
     halves, rows, cols = linear.shape
     tokens = rows - HALO
     half_heads = cols // 3 // WIDTH
@@ -994,8 +1062,15 @@
     token_spec = pl.BlockSpec((1, tokens, lanes), lambda i: (i // per_half, 0, i % per_half))
     square = pl.BlockSpec((PAIR, chunks, CHUNK, WIDTH), lambda i: (i, 0, 0, 0))
     taps_spec = pl.BlockSpec((16, lanes), lambda i: (0, i))
-    return pl.pallas_call(
-        functools.partial(mixer_bwd_kernel, tokens),
+    tiles, grad_args, grad_specs, sum_shapes, boxes = None, [], [], [], []
+    if on_grid():
+        block_rows = grads.shape[1] // lax.axis_size("dp")
+        tiles = split_tiles(grads.shape[2], block_rows, 2 * WIDTH)
+        grad_args, grad_specs = [blocks_of(grads)], [pl.BlockSpec(memory_space=pl.ANY)]
+        sum_shapes = [(block_rows, units)] * 3 + [(block_rows, grads.shape[2] - 3 * units)]
+        boxes = Scatter.boxes(tiles, [grads.dtype]) + Scatter.sems(tiles)
+    results = pl.pallas_call(
+        functools.partial(mixer_bwd_kernel, tokens, tiles),
         grid=(heads // PAIR,),
         in_specs=[
             pl.BlockSpec((1, rows, 3 * lanes), lambda i: (i // per_half, 0, i % per_half)),
@@ -1008,19 +1083,22 @@
             square,
             square,
             token_spec,
-        ],
+        ]
+        + grad_specs,
         out_specs=[
             pl.BlockSpec((1, tokens, 3 * lanes), lambda i: (i // per_half, 0, i % per_half)),
             whole((tokens, WIDTH)),
             taps_spec,
             whole((8, WIDTH)),
-        ],
+        ]
+        + [whole(shape) for shape in sum_shapes],
         out_shape=[
             jax.ShapeDtypeStruct((halves, tokens, cols), BF16),
             jax.ShapeDtypeStruct((tokens, WIDTH), F32),
             jax.ShapeDtypeStruct((16, heads * WIDTH), F32),
             jax.ShapeDtypeStruct((8, WIDTH), F32),
-        ],
+        ]
+        + [jax.ShapeDtypeStruct(shape, F32) for shape in sum_shapes],
         scratch_shapes=[
             pltpu.VMEM((PAIR, WIDTH, WIDTH), F32),
             pltpu.VMEM((PAIR, 3, tokens + 8, WIDTH), F32),
@@ -1032,12 +1110,17 @@
             pltpu.SemaphoreType.DMA((heads,)),
             pltpu.SemaphoreType.DMA((heads,)),
             pltpu.SemaphoreType.DMA((heads,)),
-        ],
+        ]
+        + boxes,
         compiler_params=pltpu.CompilerParams(
             collective_id=1, has_side_effects=True, vmem_limit_bytes=VMEM_LIMIT
         ),
         name="mixer_bwd",
-    )(linear, aux, seg_row, taps, gain, out, new, inverse, before, donb)
+    )(linear, aux, seg_row, taps, gain, out, new, inverse, before, donb, *grad_args)
+    if tiles:
+        return results
+    second = plain_scatter(grads)
+    return list(results) + list(apart(second[:, : 3 * units], 3)) + [second[:, 3 * units :]]
 
 
 def mlp_kernel(
@@ -1045,8 +1128,8 @@
 ):
     wo_refs, refs = refs[:4], refs[4:]
     gain_ref, mask_ref, teacher_ref, cot_ref, coef_ref = refs[:5]
-    out_ref, square_ref, early_ref, grad_ref, donb_ref, dhidden_ref, dgain_ref = refs[5:12]
-    hidden, normed, normed_t, total, dtotal, dmlp, dmlp_t, gates, uppers, inners = refs[12:]
+    out_ref, square_ref, grad_ref, donb_ref, dhidden_ref, dgain_ref = refs[5:11]
+    hidden, normed, normed_t, total, dtotal, dmlp, dmlp_t, gates, uppers, inners = refs[11:]
     step = pl.program_id(0)
     unit = WIDTH
 
@@ -1068,7 +1151,7 @@
         hidden[...] = rows
         xn = rows * rho_of(rows) * gain_ref[0:1]
         normed[...] = xn.astype(BF16)
-        normed_t[...] = xn.T.astype(BF16)
+        normed_t[...] = xn.astype(BF16).T
         total[...] = jnp.zeros_like(total)
 
     @pl.when(step < count)
@@ -1090,12 +1173,12 @@
         differ = rows - teacher_ref[...].astype(F32)
         masked = mask_ref[...] * differ
         square_ref[...] = jnp.sum(
-            (masked * differ).reshape(-1, 8, rows.shape[1]), 0
+            jnp.sum(masked * differ, 1, keepdims=True), 0, keepdims=True
         )
         dout = cot_ref[...].astype(F32) + masked * coef_ref[0:1, 0:1]
         dhidden_ref[...] = dout
         dmlp[...] = dout.astype(BF16)
-        dmlp_t[...] = dout.T.astype(BF16)
+        dmlp_t[...] = dout.astype(BF16).T
         dtotal[...] = jnp.zeros_like(dtotal)
 
     @pl.when((step >= count) & (step < 2 * count))
@@ -1113,13 +1196,9 @@
         grown = mm(normed_t[...], dgu).astype(BF16)
         down = mm(dmlp_t[...], inners[tile]).astype(BF16)
 
-        def put(ref):
-            for half in range(2):
-                ref[half, :, 0 : 2 * unit] = grown[:, half * 2 * unit : (half + 1) * 2 * unit]
-                ref[half, :, 2 * unit :] = down[:, half * unit : (half + 1) * unit]
-
-        pl.when(tile < EARLY)(functools.partial(put, early_ref))
-        pl.when(tile >= EARLY)(functools.partial(put, grad_ref))
+        for half in range(2):
+            grad_ref[half, :, : 2 * unit] = grown[:, half * 2 * unit : (half + 1) * 2 * unit]
+            grad_ref[half, :, 2 * unit :] = down[:, half * unit : (half + 1) * unit]
 
     @pl.when(step == 2 * count)
     def _():
@@ -1128,27 +1207,27 @@
         unit_rows = rows * rho
         drows = dtotal[...]
         du = drows * gain_ref[0:1]
-        dgain_ref[...] = jnp.sum((drows * unit_rows).reshape(-1, 8, rows.shape[1]), 0)
+        dgain_ref[...] = jnp.sum(drows * unit_rows, 0, keepdims=True)
         dh = dhidden_ref[...] + rho * (du - unit_rows * jnp.mean(du * unit_rows, -1, keepdims=True))
         dhidden_ref[...] = dh
         dattn = dh.astype(BF16)
-        dmlp_t[...] = dh.T.astype(BF16)
+        dmlp_t[...] = dattn.T
         for half in range(2):
             donb_ref[half] = mm(dattn, out_weight(half))
-            grad_ref[half] = mm(dmlp_t[...], onb_ref[half, :, 0 : 3 * unit]).astype(BF16)
+            grad_ref[half] = mm(dmlp_t[...], onb_ref[half, :, : 3 * unit]).astype(BF16)
 
     @pl.when(step == 2 * count + 1)
     def _():
         for half in range(2):
-            grad_ref[half, :, 0:unit] = mm(dmlp_t[...], onb_ref[half, :, 3 * unit :]).astype(BF16)
-
-
-def mlp(inputs, onb, weights, gain, mask, teacher, cotangent, coef):
+            grad_ref[half, :, :unit] = mm(dmlp_t[...], onb_ref[half, :, 3 * unit :]).astype(BF16)
+
+
+def mlp(inputs, onb, mixer_weights, weights, gain, mask, teacher, cotangent, coef):
     tokens, width_d = inputs.shape
     halves, _, cols = weights.shape
     half_cols = onb.shape[2]
-    count = (cols - half_cols) // (3 * WIDTH)
-    first_out = count * 3
+    count = cols // (3 * WIDTH)
+    first_out = (mixer_weights.shape[2] - half_cols) // WIDTH
 
     def whole(shape):
         return pl.BlockSpec(shape, lambda i: (0,) * len(shape))
@@ -1168,21 +1247,19 @@
         + [whole(gain.shape), whole(mask.shape), whole(teacher.shape), whole(cotangent.shape), whole(coef.shape)],
         out_specs=[
             whole((tokens, width_d)),
-            whole((8, width_d)),
-            pl.BlockSpec(wide, lambda i: (0, 0, jnp.clip(i - count, 0, EARLY - 1))),
-            pl.BlockSpec(wide, lambda i: (0, 0, jnp.maximum(i - count - EARLY, 0))),
+            whole((1, 1)),
+            pl.BlockSpec(wide, lambda i: (0, 0, jnp.maximum(i - count, 0))),
             whole((halves, tokens, half_cols)),
             whole((tokens, width_d)),
-            whole((8, width_d)),
+            whole((1, width_d)),
         ],
         out_shape=[
             jax.ShapeDtypeStruct((tokens, width_d), BF16),
-            jax.ShapeDtypeStruct((8, width_d), F32),
-            jax.ShapeDtypeStruct((halves, width_d, EARLY * 3 * WIDTH), BF16),
-            jax.ShapeDtypeStruct((halves, width_d, cols - EARLY * 3 * WIDTH), BF16),
+            jax.ShapeDtypeStruct((1, 1), F32),
+            jax.ShapeDtypeStruct((halves, width_d, cols + half_cols), BF16),
             jax.ShapeDtypeStruct((halves, tokens, half_cols), F32),
             jax.ShapeDtypeStruct((tokens, width_d), F32),
-            jax.ShapeDtypeStruct((8, width_d), F32),
+            jax.ShapeDtypeStruct((1, width_d), F32),
         ],
         scratch_shapes=[
             pltpu.VMEM((tokens, width_d), F32),
@@ -1198,7 +1275,7 @@
         ],
         compiler_params=pltpu.CompilerParams(vmem_limit_bytes=VMEM_LIMIT),
         name="mlp",
-    )(inputs, onb, weights, weights, weights, weights, weights, gain, mask, teacher, cotangent, coef)
+    )(inputs, onb, weights, *[mixer_weights] * 4, gain, mask, teacher, cotangent, coef)
 
 
 def project_back_kernel(
@@ -1215,7 +1292,7 @@
 
     @pl.when(step == 0)
     def _():
-        normed_t[...] = (unit()[0] * gain_ref[0:1]).T.astype(BF16)
+        normed_t[...] = (unit()[0] * gain_ref[0:1]).astype(BF16).T
         dbl = dbl_ref[...].astype(BF16)
         total[...] = mm_t(dbl, beta_ref[...])
         dbeta_ref[...] = mm(normed_t[...], dbl)
@@ -1228,7 +1305,7 @@
         rows, rho = unit()
         drows = total[...]
         du = drows * gain_ref[0:1]
-        dgain_ref[...] = jnp.sum((drows * rows).reshape(-1, 8, rows.shape[1]), 0)
+        dgain_ref[...] = jnp.sum(drows * rows, 0, keepdims=True)
         dinput_ref[...] = dhidden_ref[...] + rho * (
             du - rows * jnp.mean(du * rows, -1, keepdims=True)
         )
@@ -1256,11 +1333,11 @@
             whole(beta_w.shape),
             whole(dhidden.shape),
         ],
-        out_specs=[columns, whole(dhidden.shape), whole((8, width_d)), whole((width_d, WIDTH))],
+        out_specs=[columns, whole(dhidden.shape), whole((1, width_d)), whole((width_d, WIDTH))],
         out_shape=[
             jax.ShapeDtypeStruct((halves, width_d, cols), BF16),
             jax.ShapeDtypeStruct((tokens, width_d), F32),
-            jax.ShapeDtypeStruct((8, width_d), F32),
+            jax.ShapeDtypeStruct((1, width_d), F32),
             jax.ShapeDtypeStruct((width_d, WIDTH), F32),
         ],
         scratch_shapes=[
@@ -1270,6 +1347,19 @@
         compiler_params=pltpu.CompilerParams(vmem_limit_bytes=VMEM_LIMIT),
         name="project_back",
     )(dlin, weights, inputs, gain, dbl, beta_w, dhidden)
+
+
+def finish_kernel(count, *refs):
+    for source, ref in zip(refs[:count], refs[count:]):
+        ref[...] = source[...]
+
+
+def finish(*sums):
+    return pl.pallas_call(
+        functools.partial(finish_kernel, len(sums)),
+        out_shape=[jax.ShapeDtypeStruct(a.shape, F32) for a in sums],
+        name="finish",
+    )(*sums)
 
 
 def mixer_tables(segments, length, beta, tokens):
@@ -1299,7 +1389,7 @@
         1,
     )
     row = lax.dynamic_slice_in_dim(seg.astype(F32), mine * tokens, tokens, 0)
-    return aux, jnp.broadcast_to(row[None], (8, tokens))
+    return aux, row[None]
 
 
 def by_thirds(first, second, third_one):
@@ -1308,10 +1398,10 @@
     return tiles.reshape(rows, -1)
 
 
-def thirds_of(values):
+def apart(values, count):
     rows = values.shape[0]
-    tiles = values.reshape(rows, -1, 3, WIDTH)
-    return tuple(tiles[:, :, i].reshape(rows, -1) for i in range(3))
+    tiles = values.reshape(rows, -1, count, WIDTH)
+    return tuple(tiles[:, :, i].reshape(rows, -1) for i in range(count))
 
 
 def padded_rows(parts, multiple):
@@ -1338,11 +1428,11 @@
     counts = jnp.stack([valid // 64, valid % 64]).astype(BF16)
     small_parts = [w_beta, conv_weight, norm_gain, mlp_gain, head_gain, counts]
     small = padded_rows(small_parts, 16)
-    first_shard = by_thirds(w_query, w_key, w_value)
-    second_shard = jnp.concatenate([by_thirds(w_gate, w_up, w_down.T), w_out.T], 1)
+    first_shard = jnp.concatenate([by_thirds(w_query, w_key, w_value), w_out.T], 1)
+    second_shard = by_thirds(w_gate, w_up, w_down.T)
     first_w, small = gather(
         [first_shard, small],
-        split_tiles(3 * half_cols, rows)
+        split_tiles(first_shard.shape[1], rows)
         + [Tiles(1, "zxy", 0, small.shape[0], 0, WIDTH, WIDTH, 1, 0)],
         2,
     )
@@ -1362,9 +1452,9 @@
     taps = conv_w.reshape((halves, parts) + conv_weight.shape).transpose(2, 3, 0, 4, 1, 5)
     taps = taps.reshape(12, heads * WIDTH).astype(F32)
     taps = jnp.concatenate([taps, jnp.zeros((4, heads * WIDTH), F32)], 0)
-    gain_one = jnp.broadcast_to(gain_one[0].reshape(1, width_d).astype(F32), (8, width_d))
-    gain_two = jnp.broadcast_to(gain_two[0].reshape(1, width_d).astype(F32), (8, width_d))
-    gain_head = jnp.broadcast_to(gain_head[0].reshape(1, WIDTH).astype(F32), (8, WIDTH))
+    gain_one = gain_one[0].reshape(1, width_d).astype(F32)
+    gain_two = gain_two[0].reshape(1, width_d).astype(F32)
+    gain_head = gain_head[0].reshape(1, WIDTH).astype(F32)
     counts = jnp.sum(counts.astype(F32), (0, 1))
     valid_sum = counts[0] * 64.0 + counts[1]
 
@@ -1372,22 +1462,22 @@
     spread = jnp.concatenate([halo, inputs_low], 0).astype(F32)
     rho_one = lax.rsqrt(jnp.mean(spread * spread, -1, keepdims=True) + 1e-05)
     spread = (spread * rho_one * gain_one[0:1]).astype(BF16)
-    linear = jnp.einsum("td,jdc->jtc", spread, first_w, preferred_element_type=F32)
+    linear = jnp.einsum(
+        "td,jdc->jtc", spread, first_w[:, :, : 3 * half_cols], preferred_element_type=F32
+    )
     strength = jax.nn.sigmoid(
         jnp.dot(spread[HALO:], beta_w[:, :heads], preferred_element_type=F32)
     )
     aux, seg_row = mixer_tables(segments, length, strength, tokens)
     onb, out, new, inverse, before = mixer_fwd(linear, aux, seg_row, taps, gain_head)
-    coef = jnp.broadcast_to((tokens_all / 4.0) / valid_sum, (8, WIDTH))
+    coef = ((tokens_all / 4.0) / valid_sum).reshape(1, 1)
     mask = valid_mask[0].astype(F32)[:, None]
-    outputs, squares, early_g, second_g, donb, d_hidden, grad_gain_two = mlp(
-        inputs_low, onb, second_w, gain_two, mask, teacher[0], out_grad[0], coef
-    )
-    early_g = lax.psum_scatter(
-        early_g.reshape(halves * width_d, -1), ("tensor", "dp"), scatter_dimension=0, tiled=True
-    ).astype(F32)
-    dlin, dbl, dtaps, dgain = mixer_bwd(
-        linear, aux, seg_row, taps, gain_head, out, new, inverse, before, donb
+    outputs, squares, second_g, donb, d_hidden, grad_gain_two = mlp(
+        inputs_low, onb, first_w, second_w, gain_two, mask, teacher[0], out_grad[0], coef
+    )
+    dlin, dbl, dtaps, dgain, g_gate, g_up, g_down, g_out = mixer_bwd(
+        linear, aux, seg_row, taps, gain_head, out, new, inverse, before, donb,
+        second_g, w_gate.shape[1],
     )
     first_g, d_input, grad_gain_one, grad_beta = project_back(
         dlin, first_w, inputs_low, gain_one, dbl, beta_w, d_hidden
@@ -1401,19 +1491,19 @@
         dtaps[:12]
         .reshape(12, halves, half_heads, parts, WIDTH // parts)
         .transpose(1, 3, 0, 2, 4),
-        shares(jnp.sum(grad_gain_one, 0)),
-        shares(jnp.sum(grad_gain_two, 0)),
+        shares(grad_gain_one),
+        shares(grad_gain_two),
         shares(dgain[0]),
-        jnp.broadcast_to(jnp.sum(squares), (halves, parts, 1)),
+        jnp.broadcast_to(squares.reshape(1, 1, 1), (halves, parts, 1)),
     ]
     tail = jnp.concatenate([p.reshape(halves, parts, -1) for p in tail_parts], 2)
     tail_rows = -(-tail.shape[2] // (8 * WIDTH)) * 8
     tail = jnp.pad(tail, ((0, 0), (0, 0), (0, tail_rows * WIDTH - tail.shape[2])))
-    g_gate, g_up, g_down, g_out, g_query, g_key, g_value, tail = scatter(
-        second_g, first_g, tail.reshape(halves, parts * tail_rows, WIDTH), 3
-    )
-    g_gate, g_up, g_down = (
-        jnp.concatenate(pair, 1) for pair in zip(thirds_of(early_g), (g_gate, g_up, g_down))
+    g_query, g_key, g_value, tail = scatter(
+        first_g, tail.reshape(halves, parts * tail_rows, WIDTH), 3
+    )
+    g_gate, g_up, g_down, g_out, g_query, g_key, g_value = finish(
+        g_gate, g_up, g_down, g_out, g_query, g_key, g_value
     )
     tail = tail.reshape(-1)
     sizes = [w_beta.size, conv_weight.size, norm_gain.size, mlp_gain.size, head_gain.size, 1]

time: 420 us -> 401 us (0.955)
  Pallas kernels: 334 us -> 327 us
  waiting for transfers between devices: 6.5 us -> 0.04 us
  local copies, waits for them, and re-layouts: 35.3 us -> 29.1 us
    pallas_call x2 -> x3, Pallas kernels: 158 us -> 151 us  [the longest x1 112 us: mixer_bwd(): pl.pallas_call(functools.partial(mixer_bwd_kernel, tokens, tiles), grid=(...]
    all_gather x1, waiting for transfers between devices: 6.46 us -> 0.02 us  [local(): lax.all_gather(second_shard, ('tensor', 'dp'), axis=0, tiled=True)]
  transfers between devices with their start and end apart: 3 -> 2, of which waited for: 1 -> 0; matrix products, arithmetic and copies ran while one was open for 9% -> 7% of each run, Pallas kernels for 67% -> 27%
where the time goes in v3:
time: 401 us; the launch traced here: 397 us
  Pallas kernels  327 us (82%)
  local copies, waits for them, and re-layouts  29.1 us (7%)
  between operations  20.5 us (5%)
  other arithmetic  9.13 us (2%)
  matrix products  8.62 us (2%)
    pallas_call x1, Pallas kernels, mixer_bwd(): pl.pallas_call(functools.partial(mixer_bwd_kernel, tokens, tiles), grid=(...  112 us
    pallas_call x1, Pallas kernels, gather(): pl.pallas_call(functools.partial(gather_kernel, tiles, arrays), in_specs=...  75.8 us
    pallas_call x1, Pallas kernels, mlp(): pl.pallas_call(functools.partial(mlp_kernel, count), grid=(2 * count + 2,...  53.5 us
    pallas_call x1, Pallas kernels, scatter(): pl.pallas_call(functools.partial(scatter_kernel, tiles), in_specs=[hbm] *...  36.8 us
    pallas_call x1, Pallas kernels, mixer_fwd(): pl.pallas_call(functools.partial(mixer_fwd_kernel, tokens), grid=(heads /...  31.8 us
    pallas_call x1, Pallas kernels, project_back(): pl.pallas_call(project_back_kernel, grid=(halves * kinds,), in_specs=[pl....  14.7 us
    dot_general x1, matrix products, local(): jnp.einsum('td,jdc->jtc', spread, first_w[:, :, :3 * half_cols], preferre...  8.2 us
  transfers between devices with their start and end apart: 2, of which 0 were waited for; matrix products, arithmetic and copies ran while one was open for 7% of the time, Pallas kernels for 27%

profile of v3, /device:TPU:0, one launch (start us, length us, event | category | flops | bytes accessed | tf_op | source)
XLA Modules:
  0.0 397.0 jit_solution(10173146835045107807)
XLA Ops:
  7.2 1.0 stack_reshape.21
  8.3 1.1 stack_reshape.22
  9.3 1.1 stack_reshape.23
  11.2 1.3 reshape.509
  12.5 3.0 collective-permute-start
  23.6 75.8 %gather.1 = (bf16[2,4,2,2,64,2048]{5,4,3,2,1,0:T(8,128)(2,1)}, bf16[2,4,2,2,16,128]{5,4,3,2,1,0:T(8,128)(2,1)}) custom-call(bf16[64,2048]{1,0:T(8,128)(2,1)} %pad_maximum_fusion.3.refs_0_, bf16[16,128]{1,0:T(8,128)(2,1)} %pad_bitcast_fusion.refs_1_), custom_call_target="tpu_custom_call" | custom-call | tf_op jit(solution)/shard_map/gather/pallas_call | solution.py:451
  99.3 1.0 reshape_reshape.6
  102.9 1.4 compare_convert_fusion
  106.5 1.1 reshape.507
  110.1 0.9 copy.115.refs_5_
  112.5 0.8 pad.16.beta_ref
  114.3 0.8 maximum_maximum_fusion.aux_ref
  115.1 8.2 %fusion.2.lin_ref = f32[2,528,1536]{2,1,0:T(8,128)} fusion(bf16[2,1024,2048]{2,1,0:T(8,128)(2,1)} %bitcast.97, bf16[528,1024]{1,0:T(8,128)(2,1)S(1)} %fusion.7), kind=kOutput, calls=%fused_computation.2 | convolution fusion | flops 3321888768 | bytes 13860864 | tf_op jit(solution)/shard_map/td,jdc->jtc/dot_general | solution.py:1465
  123.3 31.8 %mixer_fwd.1 = (bf16[2,512,512]{2,1,0:T(8,128)(2,1)}, f32[2,512,512]{2,1,0:T(8,128)}, bf16[8,4,128,128]{3,2,1,0:T(8,128)(2,1)}, bf16[8,4,128,128]{3,2,1,0:T(8,128)(2,1)}, bf16[8,4,128,128]{3,2,1,0:T(8,128)(2,1)}) custom-call(f32[2,528,1536]{2,1,0:T(8,128)} %fusion.2.lin_ref, f32[512,128]{1,0:T(8,128)} %maximum_maximum_fusion.aux_ref, f32[1,512]{1,0:T(1,128)} %bitcast.127, ...), custom_call_target="tpu_custom_call" | custom-call | tf_op jit(solution)/shard_map/mixer_fwd/pallas_call | solution.py:1018
  155.1 53.5 %mlp.1 = (bf16[512,1024]{1,0:T(8,128)(2,1)}, f32[1,1]{1,0:T(1,128)}, bf16[2,1024,4736]{2,1,0:T(8,128)(2,1)}, f32[2,512,512]{2,1,0:T(8,128)}, f32[512,1024]{1,0:T(8,128)}, /*index=5*/f32[1,1024]{1,0:T(1,128)}) custom-call(bf16[512,1024]{1,0:T(8,128)(2,1)} %bitcast.105, bf16[2,512,512]{2,1,0:T(8,128)(2,1)} %get-tuple-element.53.onb_ref, ...), custom_call_target="tpu_custom_call" | custom-call | tf_op jit(solution)/shard_map/mlp/pallas_call | solution.py:1239
  208.6 111.5 %mixer_bwd.1 = (bf16[2,512,1536]{2,1,0:T(8,128)(2,1)}, f32[512,128]{1,0:T(8,128)}, f32[16,1024]{1,0:T(8,128)}, f32[8,128]{1,0:T(8,128)}, f32[64,1408]{1,0:T(8,12...) custom-call(f32[2,528,1536]{2,1,0:T(8,128)} %fusion.2.lin_ref, ...), custom_call_target="tpu_custom_call" | custom-call | tf_op jit(solution)/shard_map/mixer_bwd/pallas_call | solution.py:1072
  320.2 14.7 %project_back.1 = (bf16[2,1024,1536]{2,1,0:T(8,128)(2,1)}, f32[512,1024]{1,0:T(8,128)}, f32[1,1024]{1,0:T(1,128)}, f32[1024,128]{1,0:T(8,128)}) custom-call(bf16[2,512,1536]{2,1,0:T(8,128)(2,1)} %get-tuple-element.61.dlin_ref, bf16[2,1024,2048]{2,1,0:T(8,128)(2,1)} %bitcast.102, bf16[512,1024]{1,0:T(8,128)(2,1)} %bitcast.106, f32[1,1024]{1,0:T(1,128)} %reshape.524.gain_ref, ...), custom_call_target="tpu_custom_call" | custom-call | tf_op jit(solution)/shard_map/project_back/pallas_call | solution.py:1324
  334.9 1.2 copy.117
  337.0 1.3 reduce.10
  342.2 36.8 %scatter.1 = (f32[64,512]{1,0:T(8,128)}, f32[64,512]{1,0:T(8,128)}, f32[64,512]{1,0:T(8,128)}, f32[8,128]{1,0:T(8,128)}) custom-call(bf16[2,4,2,2,64,1536]{5,4,3,2,1,0:T(8,128)(2,1)} %bitcast.109, f32[2,4,2,2,8,128]{5,4,3,2,1,0:T(8,128)} %bitcast.117), custom_call_target="tpu_custom_call" | custom-call | tf_op jit(solution)/shard_map/scatter/pallas_call | solution.py:524
  380.4 1.3 slice.192
  381.6 1.3 fusion.19
  382.9 1.2 slice.196
  386.3 2.6 finish.1
  (124 shorter events, 22.1 us)
Async XLA Ops:
  7.2 147.9 %all-gather.2.cloned.1.call-start = ((), (), s32[]{:S(2)}) async-start(), calls=%async_computation | async-start | bytes 17842176 | tf_op jit(solution)/shard_map/all_gather | solution.py:1439
  10.4 2.1 copy-start
  10.4 5.2 %copy-start.9 = (s32[1,512]{1,0:T(1,128)S(1)}, s32[1,512]{1,0:T(1,128)}, u32[]{:S(2)}) copy-start(s32[1,512]{1,0:T(1,128)} %param.19) | copy-start | bytes 6148
  10.4 8.4 %copy-start.1 = (s32[1,1024]{1,0:T(1,128)S(1)}, s32[1,1024]{1,0:T(1,128)}, u32[]{:S(2)}) copy-start(s32[1,1024]{1,0:T(1,128)} %param.18) | copy-start | bytes 12292
  10.4 10.5 %copy-start.10 = (bf16[64,4]{0,1:T(4,128)(2,1)S(1)}, bf16[64,4]{0,1:T(4,128)(2,1)}, u32[]{:S(2)}) copy-start(bf16[64,4]{0,1:T(4,128)(2,1)} %param.26) | copy-start | bytes 1540
  10.6 10.6 %copy-start.7 = (bf16[3,4,4,8]{3,2,1,0:T(4,128)(2,1)S(1)}, bf16[3,4,4,8]{3,2,1,0:T(4,128)(2,1)}, u32[]{:S(2)}) copy-start(bf16[3,4,4,8]{3,2,1,0:T(4,128)(2,1)} %param.27) | copy-start | bytes 2308
  10.6 10.7 %copy-start.2 = (bf16[64,512]{1,0:T(8,128)(2,1)S(1)}, bf16[64,512]{1,0:T(8,128)(2,1)}, u32[]{:S(2)}) copy-start(bf16[64,512]{1,0:T(8,128)(2,1)} %param.23) | copy-start | bytes 196612
  10.6 10.7 %copy-start.3 = (bf16[64,512]{1,0:T(8,128)(2,1)S(1)}, bf16[64,512]{1,0:T(8,128)(2,1)}, u32[]{:S(2)}) copy-start(bf16[64,512]{1,0:T(8,128)(2,1)} %param.24) | copy-start | bytes 196612
  10.7 10.8 %copy-start.4 = (bf16[64,512]{1,0:T(8,128)(2,1)S(1)}, bf16[64,512]{1,0:T(8,128)(2,1)}, u32[]{:S(2)}) copy-start(bf16[64,512]{1,0:T(8,128)(2,1)} %param.25) | copy-start | bytes 196612
  11.2 10.9 %copy-start.11 = (bf16[64]{0:T(256)(128)(2,1)S(1)}, bf16[64]{0:T(256)(128)(2,1)}, u32[]{:S(2)}) copy-start(bf16[64]{0:T(256)(128)(2,1)} %param.22) | copy-start | bytes 388
  11.2 10.9 %copy-start.12 = (bf16[64]{0:T(256)(128)(2,1)S(1)}, bf16[64]{0:T(256)(128)(2,1)}, u32[]{:S(2)}) copy-start(bf16[64]{0:T(256)(128)(2,1)} %param.30) | copy-start | bytes 388
  11.2 10.9 %copy-start.13 = (bf16[8]{0:T(256)(128)(2,1)S(1)}, bf16[8]{0:T(256)(128)(2,1)}, u32[]{:S(2)}) copy-start(bf16[8]{0:T(256)(128)(2,1)} %param.28) | copy-start | bytes 52
  11.2 11.6 %copy-start.5 = (bf16[512,64]{0,1:T(8,128)(2,1)S(1)}, bf16[512,64]{0,1:T(8,128)(2,1)}, u32[]{:S(2)}) copy-start(bf16[512,64]{0,1:T(8,128)(2,1)} %param.29) | copy-start | bytes 196612
  12.5 100.7 %collective-permute-start = (bf16[16,1024]{1,0:T(8,128)(2,1)S(1)}, bf16[16,1024]{1,0:T(8,128)(2,1)S(1)}, u32[]{:S(2)}, u32[]{:S(2)}) collective-permute-start(bf16[16,1024]{1,0:T(8,128)(2,1)S(1)} %slice_bitcast_fusion), channel_id=1, source_target_pairs={{0,1},{1,0},{2,3},{3,2},{4,5},{5,4},{6,7},{7,6},{8,9},{9,8},{10,11... | collective-permute-start | bytes 98312 | tf_op jit(solution)/shard_map/ppermute | solution.py:1461
  320.2 18.2 %copy-start.6 = (f32[16,1024]{1,0:T(8,128)S(1)}, f32[16,1024]{1,0:T(8,128)}, u32[]{:S(2)}) copy-start(f32[16,1024]{1,0:T(8,128)} %get-tuple-element.66) | copy-start | bytes 196612
  334.9 5.1 %copy-start.8 = (f32[1,1024]{1,0:T(1,128)S(1)}, f32[1,1024]{1,0:T(1,128)}, u32[]{:S(2)}) copy-start(f32[1,1024]{1,0:T(1,128)} %get-tuple-element.68) | copy-start | bytes 12292
Sparse Core Ops, SparseCore 0:
  12.6 138.5 all-gather.1

commit v4 on v3

--- a/solution.py
+++ b/solution.py
@@ -1222,12 +1222,11 @@
             grad_ref[half, :, :unit] = mm(dmlp_t[...], onb_ref[half, :, 3 * unit :]).astype(BF16)
 
 
-def mlp(inputs, onb, mixer_weights, weights, gain, mask, teacher, cotangent, coef):
+def mlp(inputs, onb, out_weights, weights, gain, mask, teacher, cotangent, coef):
     tokens, width_d = inputs.shape
     halves, _, cols = weights.shape
     half_cols = onb.shape[2]
     count = cols // (3 * WIDTH)
-    first_out = (mixer_weights.shape[2] - half_cols) // WIDTH
 
     def whole(shape):
         return pl.BlockSpec(shape, lambda i: (0,) * len(shape))
@@ -1241,7 +1240,7 @@
         grid=(2 * count + 2,),
         in_specs=[whole(inputs.shape), whole(onb.shape), pl.BlockSpec(wide, tile)]
         + [
-            pl.BlockSpec((halves, width_d, WIDTH), functools.partial(lambda n, i: (0, 0, n), first_out + n))
+            pl.BlockSpec((halves, width_d, WIDTH), functools.partial(lambda n, i: (0, 0, n), n))
             for n in range(4)
         ]
         + [whole(gain.shape), whole(mask.shape), whole(teacher.shape), whole(cotangent.shape), whole(coef.shape)],
@@ -1275,7 +1274,7 @@
         ],
         compiler_params=pltpu.CompilerParams(vmem_limit_bytes=VMEM_LIMIT),
         name="mlp",
-    )(inputs, onb, weights, *[mixer_weights] * 4, gain, mask, teacher, cotangent, coef)
+    )(inputs, onb, weights, *[out_weights] * 4, gain, mask, teacher, cotangent, coef)
 
 
 def project_back_kernel(
@@ -1349,17 +1348,23 @@
     )(dlin, weights, inputs, gain, dbl, beta_w, dhidden)
 
 
-def finish_kernel(count, *refs):
-    for source, ref in zip(refs[:count], refs[count:]):
+def finish_kernel(spans, count, small_ref, scale_ref, *refs):
+    outs = refs[count:]
+    for source, ref in zip(refs[:count], outs):
         ref[...] = source[...]
-
-
-def finish(*sums):
+    for (start, size), ref in zip(spans, outs[count:]):
+        row, lane = start // WIDTH, start % WIDTH
+        ref[...] = small_ref[row : row + 1, lane : lane + size]
+    outs[-1][...] = outs[-1][...] * scale_ref[...]
+
+
+def finish(sums, small, spans, scale):
+    shapes = [a.shape for a in sums] + [(1, size) for _, size in spans]
     return pl.pallas_call(
-        functools.partial(finish_kernel, len(sums)),
-        out_shape=[jax.ShapeDtypeStruct(a.shape, F32) for a in sums],
+        functools.partial(finish_kernel, spans, len(sums)),
+        out_shape=[jax.ShapeDtypeStruct(shape, F32) for shape in shapes],
         name="finish",
-    )(*sums)
+    )(small, scale, *sums)
 
 
 def mixer_tables(segments, length, beta, tokens):
@@ -1428,14 +1433,12 @@
     counts = jnp.stack([valid // 64, valid % 64]).astype(BF16)
     small_parts = [w_beta, conv_weight, norm_gain, mlp_gain, head_gain, counts]
     small = padded_rows(small_parts, 16)
-    first_shard = jnp.concatenate([by_thirds(w_query, w_key, w_value), w_out.T], 1)
+    first_shard = by_thirds(w_query, w_key, w_value)
     second_shard = by_thirds(w_gate, w_up, w_down.T)
-    first_w, small = gather(
-        [first_shard, small],
-        split_tiles(first_shard.shape[1], rows)
-        + [Tiles(1, "zxy", 0, small.shape[0], 0, WIDTH, WIDTH, 1, 0)],
-        2,
-    )
+    tiles = split_tiles(first_shard.shape[1], rows)
+    tiles += split_tiles(half_cols, rows, array=1, start=tiles[0].count)
+    tiles.append(Tiles(2, "zxy", 0, small.shape[0], 0, WIDTH, WIDTH, 1, 0))
+    first_w, out_w, small = gather([first_shard, w_out.T, small], tiles, 2)
     second_w = lax.all_gather(second_shard, ("tensor", "dp"), axis=0, tiled=True).reshape(
         halves, width_d, second_shard.shape[1]
     )
@@ -1462,9 +1465,7 @@
     spread = jnp.concatenate([halo, inputs_low], 0).astype(F32)
     rho_one = lax.rsqrt(jnp.mean(spread * spread, -1, keepdims=True) + 1e-05)
     spread = (spread * rho_one * gain_one[0:1]).astype(BF16)
-    linear = jnp.einsum(
-        "td,jdc->jtc", spread, first_w[:, :, : 3 * half_cols], preferred_element_type=F32
-    )
+    linear = jnp.einsum("td,jdc->jtc", spread, first_w, preferred_element_type=F32)
     strength = jax.nn.sigmoid(
         jnp.dot(spread[HALO:], beta_w[:, :heads], preferred_element_type=F32)
     )
@@ -1473,7 +1474,7 @@
     coef = ((tokens_all / 4.0) / valid_sum).reshape(1, 1)
     mask = valid_mask[0].astype(F32)[:, None]
     outputs, squares, second_g, donb, d_hidden, grad_gain_two = mlp(
-        inputs_low, onb, first_w, second_w, gain_two, mask, teacher[0], out_grad[0], coef
+        inputs_low, onb, out_w, second_w, gain_two, mask, teacher[0], out_grad[0], coef
     )
     dlin, dbl, dtaps, dgain, g_gate, g_up, g_down, g_out = mixer_bwd(
         linear, aux, seg_row, taps, gain_head, out, new, inverse, before, donb,
@@ -1487,7 +1488,7 @@
         return jnp.broadcast_to(values.reshape(1, parts, -1), (halves, parts, values.size // parts))
 
     tail_parts = [
-        grad_beta[:, :heads].reshape(parts, rows, halves, half_heads).transpose(2, 0, 1, 3),
+        grad_beta[:, :heads].reshape(parts, rows, halves, half_heads).transpose(2, 0, 3, 1),
         dtaps[:12]
         .reshape(12, halves, half_heads, parts, WIDTH // parts)
         .transpose(1, 3, 0, 2, 4),
@@ -1502,26 +1503,29 @@
     g_query, g_key, g_value, tail = scatter(
         first_g, tail.reshape(halves, parts * tail_rows, WIDTH), 3
     )
-    g_gate, g_up, g_down, g_out, g_query, g_key, g_value = finish(
-        g_gate, g_up, g_down, g_out, g_query, g_key, g_value
+    sizes = [w_beta.size, conv_weight.size, norm_gain.size, mlp_gain.size, head_gain.size, 1]
+    cuts = [sum(sizes[:i]) for i in range(7)]
+    g_gate, g_up, g_down, g_out, g_query, g_key, g_value, g_one, g_two, g_head, loss = finish(
+        [g_gate, g_up, g_down, g_out, g_query, g_key, g_value],
+        tail,
+        list(zip(cuts, sizes))[2:],
+        (1.0 / (width_d * valid_sum)).reshape(1, 1),
     )
     tail = tail.reshape(-1)
-    sizes = [w_beta.size, conv_weight.size, norm_gain.size, mlp_gain.size, head_gain.size, 1]
-    cuts = [sum(sizes[:i]) for i in range(7)]
-    g_beta, g_conv, g_one, g_two, g_head, squares = (tail[cuts[i] : cuts[i + 1]] for i in range(6))
+    g_beta, g_conv = tail[: cuts[1]], tail[cuts[1] : cuts[2]]
     return (
         outputs[None],
-        squares[0] / (width_d * valid_sum),
+        loss.reshape(()),
         d_input[None],
-        g_one,
+        g_one.reshape(-1),
         g_query,
         g_key,
         g_value,
-        g_beta.reshape(w_beta.shape),
+        g_beta.reshape(half_heads, rows).T,
         g_conv.reshape(conv_weight.shape),
-        g_head,
+        g_head.reshape(-1),
         g_out.T,
-        g_two,
+        g_two.reshape(-1),
         g_gate,
         g_up,
         g_down.T,

time: 401 us -> 393 us (0.980)
  transfers between devices with their start and end apart: 2 -> 2, of which waited for: 0 -> 0; matrix products, arithmetic and copies ran while one was open for 7% -> 6% of each run, Pallas kernels for 27% -> 28%
where the time goes in v4:
time: 393 us; the launch traced here: 389 us
  Pallas kernels  326 us (83%)
  local copies, waits for them, and re-layouts  26.9 us (7%)
  between operations  18.7 us (5%)
  other arithmetic  8.4 us (2%)
  matrix products  5.95 us (2%)
    pallas_call x1, Pallas kernels, mixer_bwd(): pl.pallas_call(functools.partial(mixer_bwd_kernel, tokens, tiles), grid=(...  112 us
    pallas_call x1, Pallas kernels, gather(): pl.pallas_call(functools.partial(gather_kernel, tiles, arrays), in_specs=...  76.6 us
    pallas_call x1, Pallas kernels, mlp(): pl.pallas_call(functools.partial(mlp_kernel, count), grid=(2 * count + 2,...  53.5 us
    pallas_call x1, Pallas kernels, scatter(): pl.pallas_call(functools.partial(scatter_kernel, tiles), in_specs=[hbm] *...  36.1 us
    pallas_call x1, Pallas kernels, mixer_fwd(): pl.pallas_call(functools.partial(mixer_fwd_kernel, tokens), grid=(heads /...  30.8 us
    pallas_call x1, Pallas kernels, project_back(): pl.pallas_call(project_back_kernel, grid=(halves * kinds,), in_specs=[pl....  14.6 us
  transfers between devices with their start and end apart: 2, of which 0 were waited for; matrix products, arithmetic and copies ran while one was open for 6% of the time, Pallas kernels for 28%

profile of v4, /device:TPU:0, one launch (start us, length us, event | category | flops | bytes accessed | tf_op | source)
XLA Modules:
  0.0 388.9 jit_solution(9066899794690240897)
XLA Ops:
  7.2 1.0 stack_reshape.21
  8.3 1.1 stack_reshape.22
  9.3 1.1 stack_reshape.23
  11.2 1.3 reshape.527
  12.5 3.0 collective-permute-start
  19.5 0.7 fusion.13
  21.9 0.8 reshape.519.refs_0_
  23.5 76.6 %gather.1 = (bf16[2,4,2,2,64,1536]{5,4,3,2,1,0:T(8,128)(2,1)}, bf16[2,4,2,2,64,512]{5,4,3,2,1,0:T(8,128)(2,1)}, bf16[2,4,2,2,16,128]{5,4,3,2,1,0:T(8,128)(2,1)}) custom-call(bf16[64,1536]{1,0:T(8,128)(2,1)} %reshape.519.refs_0_, bf16[64,512]{1,0:T(8,128)(2,1)} %bitcast.129, bf16[16,128]{1,0:T(8,128)(2,1)} %pad_bitcast_fusion.refs_2_), custom_call_target="tpu_custom_call" | custom-call | tf_op jit(solution)/shard_map/gather/pallas_call | solution.py:451
  100.1 1.0 reshape_reshape.6
  103.7 1.4 compare_convert_fusion
  107.3 1.1 reshape.525
  110.9 0.9 copy.147.refs_5_
  113.3 0.8 pad.16.beta_ref
  115.1 0.8 maximum_maximum_fusion.aux_ref
  116.0 1.1 copy-done
  117.1 5.5 %convolution_bitcast_fusion.lin_ref = f32[2,528,1536]{2,1,0:T(8,128)} fusion(bf16[2,1024,1536]{2,1,0:T(8,128)(2,1)S(1)} %bitcast.107, bf16[528,1024]{1,0:T(8,128)(2,1)S(1)} %fusion.2), kind=kOutput, calls=%fused_computation | convolution fusion | flops 3321888768 | bytes 13860864 | tf_op jit(solution)/shard_map/td,jdc->jtc/dot_general | solution.py:1468
  122.6 30.8 %mixer_fwd.1 = (bf16[2,512,512]{2,1,0:T(8,128)(2,1)}, f32[2,512,512]{2,1,0:T(8,128)}, bf16[8,4,128,128]{3,2,1,0:T(8,128)(2,1)}, bf16[8,4,128,128]{3,2,1,0:T(8,128)(2,1)}, bf16[8,4,128,128]{3,2,1,0:T(8,128)(2,1)}) custom-call(f32[2,528,1536]{2,1,0:T(8,128)} %convolution_bitcast_fusion.lin_ref, f32[512,128]{1,0:T(8,128)} %maximum_maximum_fusion.aux_ref, ...), custom_call_target="tpu_custom_call" | custom-call | tf_op jit(solution)/shard_map/mixer_fwd/pallas_call | solution.py:1018
  153.5 53.5 %mlp.1 = (bf16[512,1024]{1,0:T(8,128)(2,1)}, f32[1,1]{1,0:T(1,128)}, bf16[2,1024,4736]{2,1,0:T(8,128)(2,1)}, f32[2,512,512]{2,1,0:T(8,128)}, f32[512,1024]{1,0:T(8,128)}, /*index=5*/f32[1,1024]{1,0:T(1,128)}) custom-call(bf16[512,1024]{1,0:T(8,128)(2,1)} %bitcast.110, bf16[2,512,512]{2,1,0:T(8,128)(2,1)} %get-tuple-element.58.onb_ref, ...), custom_call_target="tpu_custom_call" | custom-call | tf_op jit(solution)/shard_map/mlp/pallas_call | solution.py:1238
  207.0 111.6 %mixer_bwd.1 = (bf16[2,512,1536]{2,1,0:T(8,128)(2,1)}, f32[512,128]{1,0:T(8,128)}, f32[16,1024]{1,0:T(8,128)}, f32[8,128]{1,0:T(8,128)}, f32[64,1408]{1,0:T(8,12...) custom-call(f32[2,528,1536]{2,1,0:T(8,128)} %convolution_bitcast_fusion.lin_ref, ...), custom_call_target="tpu_custom_call" | custom-call | tf_op jit(solution)/shard_map/mixer_bwd/pallas_call | solution.py:1072
  318.6 14.6 %project_back.1 = (bf16[2,1024,1536]{2,1,0:T(8,128)(2,1)}, f32[512,1024]{1,0:T(8,128)}, f32[1,1024]{1,0:T(1,128)}, f32[1024,128]{1,0:T(8,128)}) custom-call(bf16[2,512,1536]{2,1,0:T(8,128)(2,1)} %get-tuple-element.67.dlin_ref, bf16[2,1024,1536]{2,1,0:T(8,128)(2,1)} %bitcast.106, bf16[512,1024]{1,0:T(8,128)(2,1)} %bitcast.111, f32[1,1024]{1,0:T(1,128)} %reshape.547.gain_ref, ...), custom_call_target="tpu_custom_call" | custom-call | tf_op jit(solution)/shard_map/project_back/pallas_call | solution.py:1323
  333.2 1.2 copy.149
  335.2 1.3 reduce.10
  340.4 36.1 %scatter.1 = (f32[64,512]{1,0:T(8,128)}, f32[64,512]{1,0:T(8,128)}, f32[64,512]{1,0:T(8,128)}, f32[8,128]{1,0:T(8,128)}) custom-call(bf16[2,4,2,2,64,1536]{5,4,3,2,1,0:T(8,128)(2,1)} %bitcast.114, f32[2,4,2,2,8,128]{5,4,3,2,1,0:T(8,128)} %bitcast.121), custom_call_target="tpu_custom_call" | custom-call | tf_op jit(solution)/shard_map/scatter/pallas_call | solution.py:524
  379.3 2.5 finish.1
  (119 shorter events, 20.2 us)
Async XLA Ops:
  7.2 146.3 %all-gather.2.cloned.1.call-start = ((), (), s32[]{:S(2)}) async-start(), calls=%async_computation | async-start | bytes 17842176 | tf_op jit(solution)/shard_map/all_gather | solution.py:1442
  10.4 2.1 copy-start.1
  10.4 5.1 %copy-start.9 = (s32[1,512]{1,0:T(1,128)S(1)}, s32[1,512]{1,0:T(1,128)}, u32[]{:S(2)}) copy-start(s32[1,512]{1,0:T(1,128)} %param.19) | copy-start | bytes 6148
  10.4 8.4 %copy-start.2 = (s32[1,1024]{1,0:T(1,128)S(1)}, s32[1,1024]{1,0:T(1,128)}, u32[]{:S(2)}) copy-start(s32[1,1024]{1,0:T(1,128)} %param.18) | copy-start | bytes 12292
  10.4 10.5 %copy-start.10 = (bf16[64,4]{0,1:T(4,128)(2,1)S(1)}, bf16[64,4]{0,1:T(4,128)(2,1)}, u32[]{:S(2)}) copy-start(bf16[64,4]{0,1:T(4,128)(2,1)} %param.26) | copy-start | bytes 1540
  10.6 10.6 %copy-start.7 = (bf16[3,4,4,8]{3,2,1,0:T(4,128)(2,1)S(1)}, bf16[3,4,4,8]{3,2,1,0:T(4,128)(2,1)}, u32[]{:S(2)}) copy-start(bf16[3,4,4,8]{3,2,1,0:T(4,128)(2,1)} %param.27) | copy-start | bytes 2308
  10.6 10.7 %copy-start.3 = (bf16[64,512]{1,0:T(8,128)(2,1)S(1)}, bf16[64,512]{1,0:T(8,128)(2,1)}, u32[]{:S(2)}) copy-start(bf16[64,512]{1,0:T(8,128)(2,1)} %param.23) | copy-start | bytes 196612
  10.6 10.7 %copy-start.4 = (bf16[64,512]{1,0:T(8,128)(2,1)S(1)}, bf16[64,512]{1,0:T(8,128)(2,1)}, u32[]{:S(2)}) copy-start(bf16[64,512]{1,0:T(8,128)(2,1)} %param.24) | copy-start | bytes 196612
  10.7 10.7 %copy-start.5 = (bf16[64,512]{1,0:T(8,128)(2,1)S(1)}, bf16[64,512]{1,0:T(8,128)(2,1)}, u32[]{:S(2)}) copy-start(bf16[64,512]{1,0:T(8,128)(2,1)} %param.25) | copy-start | bytes 196612
  11.2 11.6 %copy-start.11 = (bf16[64]{0:T(256)(128)(2,1)S(1)}, bf16[64]{0:T(256)(128)(2,1)}, u32[]{:S(2)}) copy-start(bf16[64]{0:T(256)(128)(2,1)} %param.22) | copy-start | bytes 388
  11.2 11.6 %copy-start.12 = (bf16[64]{0:T(256)(128)(2,1)S(1)}, bf16[64]{0:T(256)(128)(2,1)}, u32[]{:S(2)}) copy-start(bf16[64]{0:T(256)(128)(2,1)} %param.30) | copy-start | bytes 388
  11.2 11.6 %copy-start.13 = (bf16[8]{0:T(256)(128)(2,1)S(1)}, bf16[8]{0:T(256)(128)(2,1)}, u32[]{:S(2)}) copy-start(bf16[8]{0:T(256)(128)(2,1)} %param.28) | copy-start | bytes 52
  12.5 101.6 %collective-permute-start = (bf16[16,1024]{1,0:T(8,128)(2,1)S(1)}, bf16[16,1024]{1,0:T(8,128)(2,1)S(1)}, u32[]{:S(2)}, u32[]{:S(2)}) collective-permute-start(bf16[16,1024]{1,0:T(8,128)(2,1)S(1)} %slice_bitcast_fusion), channel_id=1, source_target_pairs={{0,1},{1,0},{2,3},{3,2},{4,5},{5,4},{6,7},{7,6},{8,9},{9,8},{10,11... | collective-permute-start | bytes 98312 | tf_op jit(solution)/shard_map/ppermute | solution.py:1464
  114.1 3.0 copy-start
  318.6 18.0 %copy-start.6 = (f32[16,1024]{1,0:T(8,128)S(1)}, f32[16,1024]{1,0:T(8,128)}, u32[]{:S(2)}) copy-start(f32[16,1024]{1,0:T(8,128)} %get-tuple-element.72) | copy-start | bytes 196612
  333.2 5.0 %copy-start.8 = (f32[1,1024]{1,0:T(1,128)S(1)}, f32[1,1024]{1,0:T(1,128)}, u32[]{:S(2)}) copy-start(f32[1,1024]{1,0:T(1,128)} %get-tuple-element.74) | copy-start | bytes 12292
Sparse Core Ops, SparseCore 0:
  12.6 138.5 all-gather.1

commit v5 on v4

--- a/solution.py
+++ b/solution.py
@@ -433,33 +433,49 @@
     moves.finish()
 
 
-def gather_kernel(tiles, arrays, *refs):
-    run_all(Gather(tiles, refs[:arrays], refs[arrays : 2 * arrays], refs[2 * arrays :]))
-
-
-def gather(shards, tiles, ident):
+def gather_kernel(tiles, arrays, inputs_ref, *refs):
+    shards, fulls, edge_ref = refs[:arrays], refs[arrays : 2 * arrays], refs[2 * arrays]
+    *sems, edge_sem = refs[2 * arrays + 1 :]
+    moves = Gather(tiles, shards, fulls, sems)
+    moves.begin()
+    edge = remote(
+        inputs_ref.at[pl.ds(inputs_ref.shape[0] - HALO, HALO)],
+        edge_ref,
+        edge_sem.at[0],
+        edge_sem.at[1],
+        across(moves.at, ("y", 0)),
+    )
+    edge.start()
+    lax.fori_loop(0, moves.steps, lambda step, _: (moves.step(step), 0)[1], 0)
+    moves.finish()
+    edge.wait()
+
+
+def gather(shards, inputs, tiles, ident):
     halves = lax.axis_size("tensor")
     if not on_grid():
-        return [
+        fulls = [
             lax.all_gather(shard, ("tensor", "dp"), axis=0, tiled=False).reshape(
                 (halves, -1) + shard.shape[1:]
             )
             for shard in shards
         ]
+        return fulls + [lax.ppermute(inputs[-HALO:], "tensor", [(0, 1), (1, 0)])]
     hbm = pl.BlockSpec(memory_space=pl.ANY)
     arrays = len(shards)
-    fulls = pl.pallas_call(
+    *fulls, edge = pl.pallas_call(
         functools.partial(gather_kernel, tiles, arrays),
-        in_specs=[hbm] * arrays,
-        out_specs=[hbm] * arrays,
+        in_specs=[hbm] * (arrays + 1),
+        out_specs=[hbm] * (arrays + 1),
         out_shape=[
             jax.ShapeDtypeStruct((halves,) + GRID + shard.shape, shard.dtype) for shard in shards
-        ],
-        scratch_shapes=Gather.sems(tiles, arrays),
+        ]
+        + [jax.ShapeDtypeStruct((HALO, inputs.shape[1]), inputs.dtype)],
+        scratch_shapes=Gather.sems(tiles, arrays) + [pltpu.SemaphoreType.DMA((2,))],
         compiler_params=pltpu.CompilerParams(collective_id=ident, has_side_effects=True),
         name="gather",
-    )(*shards)
-    return [full.reshape(halves, -1, full.shape[-1]) for full in fulls]
+    )(inputs, *shards)
+    return [full.reshape(halves, -1, full.shape[-1]) for full in fulls] + [edge]
 
 
 def put_turns(turns, rest, columns):
@@ -1438,7 +1454,7 @@
     tiles = split_tiles(first_shard.shape[1], rows)
     tiles += split_tiles(half_cols, rows, array=1, start=tiles[0].count)
     tiles.append(Tiles(2, "zxy", 0, small.shape[0], 0, WIDTH, WIDTH, 1, 0))
-    first_w, out_w, small = gather([first_shard, w_out.T, small], tiles, 2)
+    first_w, out_w, small, halo = gather([first_shard, w_out.T, small], inputs_low, tiles, 2)
     second_w = lax.all_gather(second_shard, ("tensor", "dp"), axis=0, tiled=True).reshape(
         halves, width_d, second_shard.shape[1]
     )
@@ -1461,7 +1477,6 @@
     counts = jnp.sum(counts.astype(F32), (0, 1))
     valid_sum = counts[0] * 64.0 + counts[1]
 
-    halo = lax.ppermute(inputs_low[-HALO:], "tensor", [(0, 1), (1, 0)])
     spread = jnp.concatenate([halo, inputs_low], 0).astype(F32)
     rho_one = lax.rsqrt(jnp.mean(spread * spread, -1, keepdims=True) + 1e-05)
     spread = (spread * rho_one * gain_one[0:1]).astype(BF16)

time: 393 us -> 391 us (level)
  transfers between devices with their start and end apart: 2 -> 1, of which waited for: 0 -> 1; matrix products, arithmetic and copies ran while one was open for 6% -> 6% of each run, Pallas kernels for 28% -> 28%
where the time goes in v5:
time: 391 us; the launch traced here: 388 us
  Pallas kernels  328 us (84%)
  local copies, waits for them, and re-layouts  26.1 us (7%)
  between operations  18.7 us (5%)
  other arithmetic  8.39 us (2%)
  matrix products  5.95 us (2%)
    pallas_call x1, Pallas kernels, mixer_bwd(): pl.pallas_call(functools.partial(mixer_bwd_kernel, tokens, tiles), grid=(...  111 us
    pallas_call x1, Pallas kernels, gather(): pl.pallas_call(functools.partial(gather_kernel, tiles, arrays), in_specs=...  76.4 us
    pallas_call x1, Pallas kernels, mlp(): pl.pallas_call(functools.partial(mlp_kernel, count), grid=(2 * count + 2,...  53.4 us
    pallas_call x1, Pallas kernels, scatter(): pl.pallas_call(functools.partial(scatter_kernel, tiles), in_specs=[hbm] *...  37.4 us
    pallas_call x1, Pallas kernels, mixer_fwd(): pl.pallas_call(functools.partial(mixer_fwd_kernel, tokens), grid=(heads /...  31.7 us
    pallas_call x1, Pallas kernels, project_back(): pl.pallas_call(project_back_kernel, grid=(halves * kinds,), in_specs=[pl....  14.6 us
  transfers between devices with their start and end apart: 1, of which 1 were waited for; matrix products, arithmetic and copies ran while one was open for 6% of the time, Pallas kernels for 28%

profile of v5, /device:TPU:0, one launch (start us, length us, event | category | flops | bytes accessed | tf_op | source)
XLA Modules:
  0.0 387.7 jit_solution(3643790402595364650)
XLA Ops:
  7.2 1.0 stack_reshape.21
  8.3 1.1 stack_reshape.22
  9.3 1.1 stack_reshape.23
  11.2 1.3 reshape.526
  16.5 0.7 fusion.13
  18.9 0.8 reshape.518.refs_0_
  20.4 76.4 %gather.1 = (bf16[2,4,2,2,64,1536]{5,4,3,2,1,0:T(8,128)(2,1)}, bf16[2,4,2,2,64,512]{5,4,3,2,1,0:T(8,128)(2,1)}, bf16[2,4,2,2,16,128]{5,4,3,2,1,0:T(8,128)(2,1)}, bf16[16,1024]{1,0:T(8,128)(2,1)}) custom-call(bf16[512,1024]{1,0:T(8,128)(2,1)} %bitcast.106, bf16[64,1536]{1,0:T(8,128)(2,1)} %reshape.518.refs_0_, bf16[64,512]{1,0:T(8,128)(2,1)} %bitcast.128, ...), custom_call_target="tpu_custom_call" | custom-call | tf_op jit(solution)/shard_map/gather/pallas_call | solution.py:466
  96.9 1.0 reshape_reshape.6
  98.8 1.1 reshape.524
  101.0 0.7 fusion.8
  101.8 1.4 compare_convert_fusion
  106.4 0.9 copy.147.refs_5_
  109.5 0.8 pad.16.beta_ref
  112.0 0.8 maximum_maximum_fusion.aux_ref
  113.1 5.5 %convolution_bitcast_fusion.lin_ref = f32[2,528,1536]{2,1,0:T(8,128)} fusion(bf16[2,1024,1536]{2,1,0:T(8,128)(2,1)S(1)} %bitcast.105, bf16[528,1024]{1,0:T(8,128)(2,1)S(1)} %fusion.2), kind=kOutput, calls=%fused_computation | convolution fusion | flops 3321888768 | bytes 13860864 | tf_op jit(solution)/shard_map/td,jdc->jtc/dot_general | solution.py:1483
  118.7 31.7 %mixer_fwd.1 = (bf16[2,512,512]{2,1,0:T(8,128)(2,1)}, f32[2,512,512]{2,1,0:T(8,128)}, bf16[8,4,128,128]{3,2,1,0:T(8,128)(2,1)}, bf16[8,4,128,128]{3,2,1,0:T(8,128)(2,1)}, bf16[8,4,128,128]{3,2,1,0:T(8,128)(2,1)}) custom-call(f32[2,528,1536]{2,1,0:T(8,128)} %convolution_bitcast_fusion.lin_ref, f32[512,128]{1,0:T(8,128)} %maximum_maximum_fusion.aux_ref, ...), custom_call_target="tpu_custom_call" | custom-call | tf_op jit(solution)/shard_map/mixer_fwd/pallas_call | solution.py:1034
  150.4 0.8 all-gather.2.cloned.1.call-done
  151.2 53.4 %mlp.1 = (bf16[512,1024]{1,0:T(8,128)(2,1)}, f32[1,1]{1,0:T(1,128)}, bf16[2,1024,4736]{2,1,0:T(8,128)(2,1)}, f32[2,512,512]{2,1,0:T(8,128)}, f32[512,1024]{1,0:T(8,128)}, /*index=5*/f32[1,1024]{1,0:T(1,128)}) custom-call(bf16[512,1024]{1,0:T(8,128)(2,1)} %bitcast.107, bf16[2,512,512]{2,1,0:T(8,128)(2,1)} %get-tuple-element.60.onb_ref, ...), custom_call_target="tpu_custom_call" | custom-call | tf_op jit(solution)/shard_map/mlp/pallas_call | solution.py:1254
  204.7 111.5 %mixer_bwd.1 = (bf16[2,512,1536]{2,1,0:T(8,128)(2,1)}, f32[512,128]{1,0:T(8,128)}, f32[16,1024]{1,0:T(8,128)}, f32[8,128]{1,0:T(8,128)}, f32[64,1408]{1,0:T(8,12...) custom-call(f32[2,528,1536]{2,1,0:T(8,128)} %convolution_bitcast_fusion.lin_ref, ...), custom_call_target="tpu_custom_call" | custom-call | tf_op jit(solution)/shard_map/mixer_bwd/pallas_call | solution.py:1088
  316.2 14.6 %project_back.1 = (bf16[2,1024,1536]{2,1,0:T(8,128)(2,1)}, f32[512,1024]{1,0:T(8,128)}, f32[1,1024]{1,0:T(1,128)}, f32[1024,128]{1,0:T(8,128)}) custom-call(bf16[2,512,1536]{2,1,0:T(8,128)(2,1)} %get-tuple-element.69.dlin_ref, bf16[2,1024,1536]{2,1,0:T(8,128)(2,1)} %bitcast.104, bf16[512,1024]{1,0:T(8,128)(2,1)} %bitcast.108, f32[1,1024]{1,0:T(1,128)} %reshape.546.gain_ref, ...), custom_call_target="tpu_custom_call" | custom-call | tf_op jit(solution)/shard_map/project_back/pallas_call | solution.py:1339
  330.8 1.2 copy.149
  332.8 1.3 reduce.10
  338.0 37.4 %scatter.1 = (f32[64,512]{1,0:T(8,128)}, f32[64,512]{1,0:T(8,128)}, f32[64,512]{1,0:T(8,128)}, f32[8,128]{1,0:T(8,128)}) custom-call(bf16[2,4,2,2,64,1536]{5,4,3,2,1,0:T(8,128)(2,1)} %bitcast.113, f32[2,4,2,2,8,128]{5,4,3,2,1,0:T(8,128)} %bitcast.120), custom_call_target="tpu_custom_call" | custom-call | tf_op jit(solution)/shard_map/scatter/pallas_call | solution.py:540
  378.1 2.5 finish.1
  (118 shorter events, 19.8 us)
Async XLA Ops:
  7.2 144.0 %all-gather.2.cloned.1.call-start = ((), (), s32[]{:S(2)}) async-start(), calls=%async_computation | async-start | bytes 17842176 | tf_op jit(solution)/shard_map/all_gather | solution.py:1458
  10.4 2.1 copy-start.10
  10.4 5.3 %copy-start.2 = (s32[1,1024]{1,0:T(1,128)S(1)}, s32[1,1024]{1,0:T(1,128)}, u32[]{:S(2)}) copy-start(s32[1,1024]{1,0:T(1,128)} %param.18) | copy-start | bytes 12292
  10.4 7.5 %copy-start.11 = (bf16[64,4]{0,1:T(4,128)(2,1)S(1)}, bf16[64,4]{0,1:T(4,128)(2,1)}, u32[]{:S(2)}) copy-start(bf16[64,4]{0,1:T(4,128)(2,1)} %param.26) | copy-start | bytes 1540
  10.4 7.7 %copy-start.8 = (bf16[3,4,4,8]{3,2,1,0:T(4,128)(2,1)S(1)}, bf16[3,4,4,8]{3,2,1,0:T(4,128)(2,1)}, u32[]{:S(2)}) copy-start(bf16[3,4,4,8]{3,2,1,0:T(4,128)(2,1)} %param.27) | copy-start | bytes 2308
  10.4 7.8 %copy-start.4 = (bf16[64,512]{1,0:T(8,128)(2,1)S(1)}, bf16[64,512]{1,0:T(8,128)(2,1)}, u32[]{:S(2)}) copy-start(bf16[64,512]{1,0:T(8,128)(2,1)} %param.23) | copy-start | bytes 196612
  10.6 7.7 %copy-start.5 = (bf16[64,512]{1,0:T(8,128)(2,1)S(1)}, bf16[64,512]{1,0:T(8,128)(2,1)}, u32[]{:S(2)}) copy-start(bf16[64,512]{1,0:T(8,128)(2,1)} %param.24) | copy-start | bytes 196612
  10.6 7.7 %copy-start.6 = (bf16[64,512]{1,0:T(8,128)(2,1)S(1)}, bf16[64,512]{1,0:T(8,128)(2,1)}, u32[]{:S(2)}) copy-start(bf16[64,512]{1,0:T(8,128)(2,1)} %param.25) | copy-start | bytes 196612
  11.2 8.6 %copy-start.12 = (bf16[64]{0:T(256)(128)(2,1)S(1)}, bf16[64]{0:T(256)(128)(2,1)}, u32[]{:S(2)}) copy-start(bf16[64]{0:T(256)(128)(2,1)} %param.22) | copy-start | bytes 388
  11.2 8.6 %copy-start.13 = (bf16[64]{0:T(256)(128)(2,1)S(1)}, bf16[64]{0:T(256)(128)(2,1)}, u32[]{:S(2)}) copy-start(bf16[64]{0:T(256)(128)(2,1)} %param.30) | copy-start | bytes 388
  11.2 8.5 %copy-start.14 = (bf16[8]{0:T(256)(128)(2,1)S(1)}, bf16[8]{0:T(256)(128)(2,1)}, u32[]{:S(2)}) copy-start(bf16[8]{0:T(256)(128)(2,1)} %param.28) | copy-start | bytes 52
  97.9 12.4 %copy-start.1 = (bf16[1,512,1024]{2,1,0:T(8,128)(2,1)S(1)}, bf16[1,512,1024]{2,1,0:T(8,128)(2,1)}, u32[]{:S(2)}) copy-start(bf16[1,512,1024]{2,1,0:T(8,128)(2,1)} %param.17) | copy-start | bytes 3145732
  97.9 12.4 %copy-start.3 = (bf16[16,1024]{1,0:T(8,128)(2,1)S(1)}, bf16[16,1024]{1,0:T(8,128)(2,1)}, u32[]{:S(2)}) copy-start(bf16[16,1024]{1,0:T(8,128)(2,1)} %get-tuple-element.58) | copy-start | bytes 98308
  110.3 2.8 copy-start
  316.2 18.0 %copy-start.7 = (f32[16,1024]{1,0:T(8,128)S(1)}, f32[16,1024]{1,0:T(8,128)}, u32[]{:S(2)}) copy-start(f32[16,1024]{1,0:T(8,128)} %get-tuple-element.74) | copy-start | bytes 196612
  330.8 5.0 %copy-start.9 = (f32[1,1024]{1,0:T(1,128)S(1)}, f32[1,1024]{1,0:T(1,128)}, u32[]{:S(2)}) copy-start(f32[1,1024]{1,0:T(1,128)} %get-tuple-element.76) | copy-start | bytes 12292
Sparse Core Ops, SparseCore 0:
  12.6 138.5 all-gather.1
